TPU v7x, 256 devices: a whole 4x4x8 slice. The times are simulated.
256 devices in a mesh: gx: 16 (over y, x_hi, core), gy: 16 (over x_lo, z).
Axes of the slice: x: 4 (x_hi: 2, x_lo: 2; x = x_hi * 2 + x_lo), y: 4, z: 8, core: 2. Of those that a mesh axis runs over, the one named last changes fastest.
Arguments:
- tokens: bfloat16 [128, 128, 1536], P('gx', 'gy'), may hold values from -6 to 6
- cotangent: bfloat16 [128, 128, 1536], P('gx', 'gy'), may hold values from -6 to 6
- qkv_weight: bfloat16 [192, 576], replicated, may hold values from -4 to 4
- qkv_bias: float32 [576], replicated, may hold values from -4 to 4
- proj_weight: bfloat16 [192, 192], replicated, may hold values from -0.4375 to 0.4375
- proj_bias: float32 [192], replicated, may hold values from -4 to 4
- fc1_weight: bfloat16 [192, 768], replicated, may hold values from -0.4375 to 0.4375
- fc1_bias: float32 [768], replicated, may hold values from -4 to 4
- fc2_weight: bfloat16 [768, 192], replicated, may hold values from -0.21875 to 0.21875
- norm1_gain: float32 [192], replicated, may hold values from 0.1 to 1.9
- norm1_bias: float32 [192], replicated, may hold values from -4 to 4
- norm2_gain: float32 [192], replicated, may hold values from 0.1 to 1.9
- norm2_bias: float32 [192], replicated, may hold values from -4 to 4
Outputs:
- grad_tokens: bfloat16 [128, 128, 1536], P('gx', 'gy')
- grad_qkv: float32 [192, 576], replicated
- grad_proj: float32 [192, 192], replicated
- grad_fc1: float32 [192, 768], replicated
- grad_fc2: float32 [768, 192], replicated
- grad_vectors: float32 [2304], replicated
All inputs are finite; a program needn't handle non-finite values.
Results may differ from a plain program's by a relative error of at most 0.017.
The roundings to bfloat16 on the way count: a program that leaves them out, or rounds other values in their place, can miss the bound.
Values may be sent and summed in bfloat16 or wider, within the bound.
No kernel may reach another device: no remote copies, remote signals or barrier semaphores. Data moves between devices by JAX's collectives and lax.ppermute only.
A program may use at most 64 MiB of HBM per device.

v0:
```python
from functools import partial

import jax
import jax.numpy as jnp
from jax import lax
from jax.sharding import PartitionSpec as P

HEADS = 6
WIN = 8


eps = 1e-05


def shifted(value, axis, steps):
    count = lax.axis_size(axis)
    pairs = [(source, (source + steps) % count) for source in range(count)]
    return lax.ppermute(value, axis, pairs)


def matmul(left_side, right_side):
    return jnp.dot(left_side, right_side, preferred_element_type=jnp.float32)


def contract_rows(left_side, right_side):
    return lax.dot_general(
        left_side, right_side, (((0,), (0,)), ((), ())), preferred_element_type=jnp.float32
    )


def times_transposed(left_side, right_side):
    return lax.dot_general(
        left_side, right_side, (((1,), (1,)), ((), ())), preferred_element_type=jnp.float32
    )


def norm_forward(inputs, gain_vector, bias_vector):
    centred = inputs - jnp.mean(inputs, axis=-1, keepdims=True)
    inverse = lax.rsqrt(jnp.mean(centred * centred, axis=-1, keepdims=True) + eps)
    normed = centred * inverse
    return ((normed * gain_vector + bias_vector).astype(jnp.bfloat16), normed, inverse)


def norm_backward(incoming, normed, inverse, gain_vector):
    scaled = incoming * gain_vector
    centre = jnp.mean(scaled, axis=-1, keepdims=True)
    projection = jnp.mean(scaled * normed, axis=-1, keepdims=True)
    result = inverse * (scaled - centre - normed * projection)
    return (result, jnp.sum(incoming * normed, axis=0), jnp.sum(incoming, axis=0))


def gelu_parts(hidden_pre):
    normal_cdf = 0.5 * (1.0 + lax.erf(hidden_pre * 0.7071067811865476))
    normal_pdf = jnp.exp(-0.5 * hidden_pre * hidden_pre) * 0.3989422804014327
    return (hidden_pre * normal_cdf, normal_cdf + hidden_pre * normal_pdf)


def split_heads(projected, features, query_scale):
    row_count = projected.shape[0]
    head_size = features // HEADS
    queries = (
        (projected[:, :features] * query_scale)
        .astype(jnp.bfloat16)
        .reshape(row_count, HEADS, head_size)
    )
    key_heads = (
        projected[:, features : 2 * features]
        .astype(jnp.bfloat16)
        .reshape(row_count, HEADS, head_size)
    )
    values = projected[:, 2 * features :].astype(jnp.bfloat16).reshape(row_count, HEADS, head_size)
    return (queries, key_heads, values)


def attend_forward(attn_in, weights):
    qkv_weight, qkv_bias, proj_weight, proj_bias = (weights[0], weights[1], weights[2], weights[3])
    row_count, features = attn_in.shape
    query_scale = (features // HEADS) ** (-0.5)
    projected = matmul(attn_in, qkv_weight) + qkv_bias
    queries, key_heads, values = split_heads(projected, features, query_scale)
    scores = jnp.einsum("qhd,khd->hqk", queries, key_heads, preferred_element_type=jnp.float32)
    attention_b = jax.nn.softmax(scores, axis=-1).astype(jnp.bfloat16)
    blended = jnp.einsum("hqk,khd->qhd", attention_b, values, preferred_element_type=jnp.float32)
    blended = blended.reshape(row_count, features).astype(jnp.bfloat16)
    branch = (matmul(blended, proj_weight) + proj_bias).astype(jnp.bfloat16)
    return (branch, (queries, key_heads, values, blended))


def attend_backward(grad_branch, attn_in, stored, weights):
    qkv_weight, proj_weight = (weights[0], weights[2])
    queries, key_heads, values, blended = stored
    row_count, features = attn_in.shape
    query_scale = (features // HEADS) ** (-0.5)
    grad_proj = contract_rows(blended, grad_branch)
    grad_proj_bias = jnp.sum(grad_branch.astype(jnp.float32), axis=0)
    grad_blend = times_transposed(grad_branch, proj_weight).astype(jnp.bfloat16)
    grad_blend = grad_blend.reshape(row_count, HEADS, features // HEADS)
    scores = jnp.einsum("qhd,khd->hqk", queries, key_heads, preferred_element_type=jnp.float32)
    attention = jax.nn.softmax(scores, axis=-1)
    attention_b = attention.astype(jnp.bfloat16)
    grad_values = jnp.einsum(
        "hqk,qhd->khd", attention_b, grad_blend, preferred_element_type=jnp.float32
    )
    grad_attention = jnp.einsum(
        "qhd,khd->hqk", grad_blend, values, preferred_element_type=jnp.float32
    )
    grad_scores = attention * (
        grad_attention - jnp.sum(grad_attention * attention, axis=-1, keepdims=True)
    )
    grad_scores = grad_scores.astype(jnp.bfloat16)
    grad_queries = (
        jnp.einsum("hqk,khd->qhd", grad_scores, key_heads, preferred_element_type=jnp.float32)
        * query_scale
    )
    grad_keys = jnp.einsum("hqk,qhd->khd", grad_scores, queries, preferred_element_type=jnp.float32)
    grad_proj_in = jnp.concatenate(
        [
            grad_queries.reshape(row_count, features),
            grad_keys.reshape(row_count, features),
            grad_values.reshape(row_count, features),
        ],
        axis=-1,
    )
    grad_proj_b = grad_proj_in.astype(jnp.bfloat16)
    grad_qkv = contract_rows(attn_in, grad_proj_b)
    grad_attn_in = times_transposed(grad_proj_b, qkv_weight).astype(jnp.bfloat16)
    return (grad_attn_in, (grad_qkv, jnp.sum(grad_proj_in, axis=0), grad_proj, grad_proj_bias))


def mlp_pass(tokens32, branch, cot_rows, weights):
    fc1_weight, fc1_bias, fc2_weight = (weights[4], weights[5], weights[6])
    norm2_gain, norm2_bias = (weights[9], weights[10])
    residual = tokens32 + branch.astype(jnp.float32)
    mlp_in, hat_two, inv_two = norm_forward(residual, norm2_gain, norm2_bias)
    hidden_pre = matmul(mlp_in, fc1_weight) + fc1_bias
    active, derivative = gelu_parts(hidden_pre)
    active_b = active.astype(jnp.bfloat16)
    grad_fc2 = contract_rows(active_b, cot_rows)
    grad_pre = times_transposed(cot_rows, fc2_weight) * derivative
    grad_pre_b = grad_pre.astype(jnp.bfloat16)
    grad_fc1 = contract_rows(mlp_in, grad_pre_b)
    grad_mlp_in = times_transposed(grad_pre_b, fc1_weight)
    grad_norm2, gain_two, bias_two = norm_backward(grad_mlp_in, hat_two, inv_two, norm2_gain)
    grad_resid = cot_rows.astype(jnp.float32) + grad_norm2
    grad_branch = grad_resid.astype(jnp.bfloat16)
    return (
        grad_resid,
        grad_branch,
        (grad_fc1, jnp.sum(grad_pre, axis=0), grad_fc2, gain_two, bias_two),
    )


def ordered(attn_grads, mlp_grads, first_grads):
    return (
        attn_grads[0],
        attn_grads[2],
        mlp_grads[0],
        mlp_grads[2],
        attn_grads[1],
        attn_grads[3],
        mlp_grads[1],
        first_grads[0],
        first_grads[1],
        mlp_grads[3],
        mlp_grads[4],
    )


def attend_step(weights, running, inputs):
    grad_branch, attn_in, stored = inputs
    grad_attn_in, attn_grads = attend_backward(grad_branch, attn_in, stored, weights)
    return (
        tuple((first_term + second_term for first_term, second_term in zip(running, attn_grads))),
        grad_attn_in,
    )


def lead_tile(field):
    margin = WIN // 2
    border = shifted(field[:margin], "gx", -1)
    field = jnp.concatenate([field[margin:], border], axis=0)
    border = shifted(field[:, :margin], "gy", -1)
    return jnp.concatenate([field[:, margin:], border], axis=1)


def trail_tile(field):
    margin = WIN // 2
    border = shifted(field[-margin:], "gx", 1)
    field = jnp.concatenate([border, field[:-margin]], axis=0)
    border = shifted(field[:, -margin:], "gy", 1)
    return jnp.concatenate([border, field[:, :-margin]], axis=1)


def to_windows(field, features):
    rows_x, rows_y, packed = field.shape
    depth_count = packed // features
    shaped = field.reshape(rows_x // WIN, WIN, rows_y // WIN, WIN, depth_count, features)
    return shaped.transpose(0, 2, 1, 3, 4, 5).reshape(-1, WIN * WIN * depth_count, features)


def from_windows(windows, rows_x, rows_y, features):
    depth_count = windows.shape[1] // (WIN * WIN)
    shaped = windows.reshape(rows_x // WIN, rows_y // WIN, WIN, WIN, depth_count, features)
    return shaped.transpose(0, 2, 1, 3, 4, 5).reshape(rows_x, rows_y, depth_count * features)


def on_device(
    tokens,
    cotangent,
    qkv_weight,
    qkv_bias,
    proj_weight,
    proj_bias,
    fc1_weight,
    fc1_bias,
    fc2_weight,
    norm1_gain,
    norm1_bias,
    norm2_gain,
    norm2_bias,
):
    weights = (
        qkv_weight,
        qkv_bias,
        proj_weight,
        proj_bias,
        fc1_weight,
        fc1_bias,
        fc2_weight,
        norm1_gain,
        norm1_bias,
        norm2_gain,
        norm2_bias,
    )
    rows_x, rows_y, packed = tokens.shape
    features = norm1_gain.shape[0]
    token_count = rows_x * rows_y * (packed // features) * lax.axis_size("gx") * lax.axis_size("gy")
    factor = float(token_count) ** (-0.5)
    tokens32 = tokens.reshape(-1, features).astype(jnp.float32)
    attn_in, hat_one, inv_one = norm_forward(tokens32, norm1_gain, norm1_bias)
    attn_win = to_windows(lead_tile(attn_in.reshape(rows_x, rows_y, packed)), features)
    branch_win, stored = lax.map(lambda window: attend_forward(window, weights), attn_win)
    branch = trail_tile(from_windows(branch_win, rows_x, rows_y, features)).reshape(-1, features)
    grad_resid, grad_branch, mlp_grads = mlp_pass(
        tokens32, branch, cotangent.reshape(-1, features), weights
    )
    grad_win = to_windows(lead_tile(grad_branch.reshape(rows_x, rows_y, packed)), features)
    attn_zeros = tuple(
        (
            jnp.zeros(entry.shape, jnp.float32)
            for entry in (qkv_weight, qkv_bias, proj_weight, proj_bias)
        )
    )
    attn_grads, grad_in_win = lax.scan(
        partial(attend_step, weights), attn_zeros, (grad_win, attn_win, stored)
    )
    grad_in = trail_tile(from_windows(grad_in_win, rows_x, rows_y, features)).reshape(-1, features)
    grad_norm1, gain_one, bias_one = norm_backward(
        grad_in.astype(jnp.float32), hat_one, inv_one, norm1_gain
    )
    grad_tokens = (grad_resid + grad_norm1).astype(jnp.bfloat16).reshape(rows_x, rows_y, packed)
    gradients = ordered(attn_grads, mlp_grads, (gain_one, bias_one))
    scaled = tuple((entry * factor for entry in gradients))
    summed = lax.psum(
        (
            scaled[0],
            scaled[1],
            scaled[2],
            scaled[3],
            scaled[4],
            scaled[5],
            scaled[6],
            scaled[7],
            scaled[8],
            scaled[9],
            scaled[10],
        ),
        ("gx", "gy"),
    )
    grad_vectors = jnp.concatenate(summed[4:])
    return (grad_tokens, summed[0], summed[1], summed[2], summed[3], grad_vectors)


def solution(mesh):
    in_specs = (
        P("gx", "gy", None),
        P("gx", "gy", None),
        P(),
        P(),
        P(),
        P(),
        P(),
        P(),
        P(),
        P(),
        P(),
        P(),
        P(),
    )
    out_specs = (P("gx", "gy", None), P(), P(), P(), P(), P())
    return jax.shard_map(
        on_device, mesh=mesh, in_specs=in_specs, out_specs=out_specs, check_vma=False
    )
```

profile of v0, /device:TPU:1, one launch (start us, length us, event | category | flops | bytes accessed | tf_op | source)
XLA Modules:
  0.0 355.2 jit_solution(13242442823513031815)
XLA Ops:
  7.2 1.2 reshape.142
  9.3 3.3 collective-permute-start
  12.9 2.9 collective-permute-done
  15.9 6.5 %collective-permute-start.1 = (bf16[8,4,1536]{2,1,0:T(4,128)(2,1)S(1)}, bf16[8,4,1536]{2,1,0:T(4,128)(2,1)S(1)}, u32[]{:S(2)}, u32[]{:S(2)}) collective-permute-start(bf16[8,4,1536]{2,1,0:T(4,128)(2,1)S(1)} %get-tuple-element.116), channel_id=1, source_target_pairs={{0,15},{1,0},{2,1},{3,2},{4,3},{5,4},{6,5},{7,6},{8,7},{9,8},{10,9... | collective-permute-start | bytes 294920 | tf_op jit(solution)/shard_map/ppermute | solution.py:18
  22.4 1.6 collective-permute-done.1
  24.2 0.2 squeeze.20
  24.4 0.4 fusion.43
  24.9 4.5 %fusion.44 = (f32[6,512]{1,0:T(8,128)S(1)}, f32[6,512,512]{1,2,0:T(8,128)}) fusion(bf16[512,6,32]{0,2,1:T(8,128)(2,1)S(1)} %bitcast.53, bf16[512,6,32]{0,2,1:T(8,128)(2,1)S(1)} %bitcast.49), kind=kOutput, calls=%fused_computation.92 | convolution fusion | flops 103809536 | bytes 6696960 | tf_op jit(solution)/shard_map/while/body/eval_jaxpr/sub | solution.py:82
  29.5 2.5 fusion.11
  32.0 0.3 fusion.10
  32.6 1.4 collective-permute-start.2
  34.3 1.4 collective-permute-done.2
  35.7 0.3 collective-permute-start.3
  36.0 0.2 reshape.133
  36.4 5.8 %collective-permute-done.3 = bf16[8,4,1536]{2,1,0:T(4,128)(2,1)S(1)} collective-permute-done((bf16[8,4,1536]{2,1,0:T(4,128)(2,1)S(1)}, bf16[8,4,1536]{2,1,0:T(4,128)(2,1)S(1)}, u32[]{:S(2)}, u32[]{:S(2)}) %collective-permute-start.3) | collective-permute-done | bytes 98336 | tf_op jit(solution)/shard_map/ppermute | solution.py:18
  42.5 0.2 copy.31
  43.0 0.5 convolution_add_fusion
  43.6 1.3 convolution_multiply_fusion
  44.9 0.8 fusion.45
  45.7 0.6 multiply_reduce_fusion.1
  46.3 1.2 convolution_multiply_fusion.1
  48.0 7.8 %collective-permute-start.4 = (bf16[4,8,1536]{2,1,0:T(8,128)(2,1)S(1)}, bf16[4,8,1536]{2,1,0:T(8,128)(2,1)S(1)}, u32[]{:S(2)}, u32[]{:S(2)}) collective-permute-start(bf16[4,8,1536]{2,1,0:T(8,128)(2,1)S(1)} %slice.104), channel_id=1, source_target_pairs={{0,240},{16,0},{32,16},{48,32},{64,48},{80,64},{96,80},{112,96},{1... | collective-permute-start | bytes 294920 | tf_op jit(solution)/shard_map/ppermute | solution.py:18
  56.0 0.7 collective-permute-done.4
  56.8 1.8 collective-permute-start.5
  58.6 1.7 collective-permute-done.5
  60.4 0.2 squeeze.21
  60.7 0.9 convolution_multiply_fusion.4
  61.6 0.2 convolution_convert_fusion.1
  61.8 2.7 fusion.6
  64.5 4.1 %multiply_reduce_fusion = (f32[6,512]{1,0:T(8,128)S(1)}, f32[6,512,512]{1,2,0:T(8,128)S(1)}) fusion(f32[6,512,512]{1,2,0:T(8,128)} %get-tuple-element.122, f32[6,512]{1,0:T(8,128)S(1)} %get-tuple-element.121, bf16[512,6,32]{0,2,1:T(8,128)(2,1)S(1)} %bitcast.69, bf16[512,6,32]{0,2,1:T(8,128)(2,1)} %bitcast.71), kind=kOutput, calls=%fused_computation.2 | convolution fusion | flops 105378816 | bytes 13000704 | tf_op jit(solution)/shard_map/while/body/eval_jaxpr/qhd,khd->hqk/dot_general | solution.py:104
  68.6 0.7 slice-done.1
  69.3 1.8 multiply_convert_fusion
  71.1 1.0 fusion.46
  72.1 0.6 convolution_multiply_fusion.3
  72.7 0.2 fusion.14
  72.9 1.0 convolution_convert_fusion
  73.9 1.2 convolution_multiply_fusion.2
  75.8 3.3 collective-permute-done.6
  79.3 5.9 %collective-permute-done.7 = bf16[8,4,1536]{2,1,0:T(4,128)(2,1)S(1)} collective-permute-done((bf16[8,4,1536]{2,1,0:T(4,128)(2,1)S(1)}, bf16[8,4,1536]{2,1,0:T(4,128)(2,1)S(1)}, u32[]{:S(2)}, u32[]{:S(2)}) %collective-permute-start.7) | collective-permute-done | bytes 98336 | tf_op jit(solution)/shard_map/ppermute | solution.py:18
  86.0 0.3 add_convert_fusion
  86.4 0.9 reshape.141
  87.4 80.3 %all-reduce = (f32[576]{0:T(1024)S(1)}, f32[192]{0:T(256)S(1)}, f32[768]{0:T(1024)S(1)}, f32[192]{0:T(256)S(1)}, f32[192]{0:T(256)S(1)}, /*index=5*/f32[192]{0:T(256)S(1)}, f32[192]{0:T(256)S(1)}) all-reduce(f32[576]{0:T(1024)S(1)} %broadcast_multiply_fusion.1, ...), channel_id=1, replica_groups=mesh['gx'=16,'gy'=16] {'gx','gy'}, use_global_device_ids=true, to_apply=%region_16.17 | all-reduce | flops 2304 | bytes 18432 | tf_op jit(solution)/shard_map/psum | solution.py:264
  167.6 0.7 concatenate.40
  168.3 174.9 %all-reduce.4.cloned.1.call-done = (f32[192,576]{1,0:T(8,128)}, f32[192,192]{1,0:T(8,128)}, f32[192,768]{1,0:T(8,128)}, f32[768,192]{0,1:T(8,128)}) async-done(((f32[192,576]{1,0:T(8,128)}, f32[192,192]{1,0:T(8,128)}, f32[192,768]{1,0:T(8,128)}, f32[768,192]{0,1:T(8,128)}), (f32[192,576]{1,0:T(8,128)}, f32[192,192]{1,0:T(8,128)}, f32[192,768]{1,0:T(8,128)}, ...) | async-done | bytes 1769488 | tf_op jit(solution)/shard_map/psum | solution.py:264
  343.2 1.9 copy.54
  345.1 1.6 copy.55
  346.8 0.8 copy.56
  347.6 0.8 copy.57
  (106 shorter events, 5.3 us)
Async XLA Ops:
  7.2 35.7 %copy-start = (bf16[192,768]{1,0:T(8,128)(2,1)S(1)}, bf16[192,768]{1,0:T(8,128)(2,1)}, u32[]{:S(2)}) copy-start(bf16[192,768]{1,0:T(8,128)(2,1)} %param.19) | copy-start | bytes 884740
  7.2 1.7 copy-start.9
  7.2 1.7 copy-start.13
  7.2 336.0 %all-reduce.4.cloned.1.call-start = ((), (), s32[]{:S(2)}) async-start(), calls=%async_computation | async-start | bytes 3735552 | tf_op jit(solution)/shard_map/psum | solution.py:264
  9.0 15.4 %copy-start.4 = (bf16[192,576]{1,0:T(8,128)(2,1)S(1)}, bf16[192,576]{1,0:T(8,128)(2,1)}, u32[]{:S(2)}) copy-start(bf16[192,576]{1,0:T(8,128)(2,1)} %param.15) | copy-start | bytes 663556
  9.0 15.4 %copy-start.10 = (f32[576]{0:T(1024)S(1)}, f32[576]{0:T(1024)}, u32[]{:S(2)}) copy-start(f32[576]{0:T(1024)} %param.16) | copy-start | bytes 6916
  9.3 6.5 %collective-permute-start = (bf16[4,8,1536]{2,1,0:T(8,128)(2,1)S(1)}, bf16[4,8,1536]{2,1,0:T(8,128)(2,1)S(1)}, u32[]{:S(2)}, u32[]{:S(2)}) collective-permute-start(bf16[4,8,1536]{2,1,0:T(8,128)(2,1)S(1)} %slice.89), channel_id=1, source_target_pairs={{0,240},{16,0},{32,16},{48,32},{64,48},{80,64},{96,80},{112,96},{1... | collective-permute-start | bytes 294920 | tf_op jit(solution)/shard_map/ppermute | solution.py:18
  15.9 8.2 %collective-permute-start.1 = (bf16[8,4,1536]{2,1,0:T(4,128)(2,1)S(1)}, bf16[8,4,1536]{2,1,0:T(4,128)(2,1)S(1)}, u32[]{:S(2)}, u32[]{:S(2)}) collective-permute-start(bf16[8,4,1536]{2,1,0:T(4,128)(2,1)S(1)} %get-tuple-element.116), channel_id=1, source_target_pairs={{0,15},{1,0},{2,1},{3,2},{4,3},{5,4},{6,5},{7,6},{8,7},{9,8},{10,9... | collective-permute-start | bytes 294920 | tf_op jit(solution)/shard_map/ppermute | solution.py:18
  24.9 7.1 %copy-start.7 = (bf16[512,192]{0,1:T(8,128)(2,1)}, bf16[512,192]{0,1:T(8,128)(2,1)S(1)}, u32[]{:S(2)}) copy-start(bf16[512,192]{0,1:T(8,128)(2,1)S(1)} %get-tuple-element.102) | copy-start | bytes 589828
  29.5 2.5 copy-start.3
  29.5 2.6 copy-start.14
  32.0 4.0 %copy-start.5 = (bf16[8,8,1536]{2,1,0:T(8,128)(2,1)S(1)}, bf16[8,8,1536]{2,1,0:T(8,128)(2,1)}, u32[]{:S(2)}) copy-start(bf16[8,8,1536]{2,1,0:T(8,128)(2,1)} %param.14) | copy-start | bytes 589828
  32.6 3.1 collective-permute-start.2
  35.7 6.5 %collective-permute-start.3 = (bf16[8,4,1536]{2,1,0:T(4,128)(2,1)S(1)}, bf16[8,4,1536]{2,1,0:T(4,128)(2,1)S(1)}, u32[]{:S(2)}, u32[]{:S(2)}) collective-permute-start(bf16[8,4,1536]{2,1,0:T(4,128)(2,1)S(1)} %get-tuple-element.111), channel_id=1, source_target_pairs={{0,1},{1,2},{2,3},{3,4},{4,5},{5,6},{6,7},{7,8},{8,9},{9,10},{10,1... | collective-permute-start | bytes 294920 | tf_op jit(solution)/shard_map/ppermute | solution.py:18
  42.3 0.7 copy-start.8
  42.3 0.7 copy-start.11
  42.3 0.7 copy-start.12
  43.5 1.4 copy-start.15
  48.0 8.8 %collective-permute-start.4 = (bf16[4,8,1536]{2,1,0:T(8,128)(2,1)S(1)}, bf16[4,8,1536]{2,1,0:T(8,128)(2,1)S(1)}, u32[]{:S(2)}, u32[]{:S(2)}) collective-permute-start(bf16[4,8,1536]{2,1,0:T(8,128)(2,1)S(1)} %slice.104), channel_id=1, source_target_pairs={{0,240},{16,0},{32,16},{48,32},{64,48},{80,64},{96,80},{112,96},{1... | collective-permute-start | bytes 294920 | tf_op jit(solution)/shard_map/ppermute | solution.py:18
  56.8 3.5 collective-permute-start.5
  64.5 4.1 %slice-start = ((s8[6291456]{0:T(1024)(128)(4,1)}), s8[4194304]{0:T(1024)(128)(4,1)S(1)}, s32[]{:S(2)}) async-start(s8[6291456]{0:T(1024)(128)(4,1)} %bitcast.47), calls=%async_computation.1 | async-start | bytes 8388608
  64.5 4.8 %slice-start.1 = ((s8[6291456]{0:T(1024)(128)(4,1)}), s8[2097152]{0:T(1024)(128)(4,1)S(1)}, s32[]{:S(2)}) async-start(s8[6291456]{0:T(1024)(128)(4,1)} %bitcast.47), calls=%async_computation.2 | async-start | bytes 4194304
  73.9 1.2 copy-start.6
  75.7 3.5 collective-permute-start.6
  79.2 6.1 %collective-permute-start.7 = (bf16[8,4,1536]{2,1,0:T(4,128)(2,1)S(1)}, bf16[8,4,1536]{2,1,0:T(4,128)(2,1)S(1)}, u32[]{:S(2)}, u32[]{:S(2)}) collective-permute-start(bf16[8,4,1536]{2,1,0:T(4,128)(2,1)S(1)} %get-tuple-element.103), channel_id=1, source_target_pairs={{0,1},{1,2},{2,3},{3,4},{4,5},{5,6},{6,7},{7,8},{8,9},{9,10},{10,1... | collective-permute-start | bytes 294920 | tf_op jit(solution)/shard_map/ppermute | solution.py:18
  343.2 3.6 %copy-start.2 = (f32[192,768]{1,0:T(8,128)S(1)}, f32[192,768]{1,0:T(8,128)}, u32[]{:S(2)}) copy-start(f32[192,768]{1,0:T(8,128)} %get-tuple-element.137) | copy-start | bytes 1769476
  343.2 4.4 %copy-start.1 = (f32[768,192]{0,1:T(8,128)S(1)}, f32[768,192]{0,1:T(8,128)}, u32[]{:S(2)}) copy-start(f32[768,192]{0,1:T(8,128)} %get-tuple-element.138) | copy-start | bytes 1769476
Sparse Core Ops, SparseCore 0:
  79.5 263.6 all-reduce.3
where the time goes:
time: 357 us; the launch traced here: 355 us
  waiting for transfers between devices  198 us (55%)
  blocking collectives  80.3 us (22%)
  matrix products  23.8 us (7%)
  starting transfers between devices  21.4 us (6%)
  between operations  14.7 us (4%)
  local copies, waits for them, and re-layouts  13.1 us (4%)
  other arithmetic  3.79 us (1%)
    psum x1, waiting for transfers between devices, on_device(): lax.psum((scaled[0], scaled[1], scaled[2], scaled[3], scaled[4], scaled[5...  175 us
    psum x1, blocking collectives, on_device(): lax.psum((scaled[0], scaled[1], scaled[2], scaled[3], scaled[4], scaled[5...  80.3 us
    ppermute x8, waiting for transfers between devices, shifted(): return lax.ppermute(value, axis, pairs)  23.4 us
    ppermute x8, starting transfers between devices, shifted(): return lax.ppermute(value, axis, pairs)  21.3 us
  transfers between devices with their start and end apart: 9, of which 9 were waited for; matrix products, arithmetic and copies ran while one was open for 1% of the time, Pallas kernels for 0%

commit v1 on v0

v1 whole, which is shorter than its diff:
```python
from functools import partial

import jax
import jax.numpy as jnp
from jax import lax
from jax.experimental import pallas as pl
from jax.experimental.pallas import tpu as pltpu
from jax.sharding import PartitionSpec as P

HEADS = 6
WIN = 8
LANES = 128
eps = 1e-05
BF16 = jnp.bfloat16
F32 = jnp.float32
BOTH = ("gx", "gy")


def dot_nn(left, right):
    return lax.dot_general(left, right, (((1,), (0,)), ((), ())), preferred_element_type=F32)


def dot_nt(left, right):
    return lax.dot_general(left, right, (((1,), (1,)), ((), ())), preferred_element_type=F32)


def dot_tn(left, right):
    return lax.dot_general(left, right, (((0,), (0,)), ((), ())), preferred_element_type=F32)


def norm_forward(value):
    centred = value - jnp.mean(value, axis=0, keepdims=True)
    inverse = lax.rsqrt(jnp.mean(centred * centred, axis=0, keepdims=True) + eps)
    return centred * inverse, inverse


def norm_backward(incoming, normed, inverse, gain):
    scaled = incoming * gain
    centre = jnp.mean(scaled, axis=0, keepdims=True)
    projection = jnp.mean(scaled * normed, axis=0, keepdims=True)
    return inverse * (scaled - centre - normed * projection)


def token_partial(value):
    total = value[:, :LANES]
    for at in range(LANES, value.shape[1], LANES):
        total = total + value[:, at : at + LANES]
    return total


def gather_window(refs, depth, features):
    field = jnp.concatenate([ref[...] for ref in refs], axis=0)
    return jnp.concatenate(
        [field[:, t * features : (t + 1) * features] for t in range(depth)], axis=0
    )


def window_kernel(
    core, tok0, tok1, tok2, tok3, cot0, cot1, cot2, cot3,
    qkv_wt, qkv_w, proj_wt, proj_w, fc1_wt, fc1_w, fc2_w, columns,
    out0, out1, out2, out3, keep, send,
    attn_ref, gp_ref, grads,
):
    features = proj_w.shape[0]
    hidden_width = fc2_w.shape[0]
    head = features // HEADS
    depth = tok0.shape[1] // features
    scale = head ** (-0.5)
    at = 0
    params = []
    for size in (3 * features, features, hidden_width) + (features,) * 4:
        params.append(columns[at : at + size, 0:1])
        at += size
    qkv_b, proj_b, fc1_b, g1, b1, g2, b2 = params

    tok_t = gather_window((tok0, tok1, tok2, tok3), depth, features).astype(F32).T
    hat1, inv1 = norm_forward(tok_t)
    attn_in = (hat1 * g1 + b1).astype(BF16)
    projected = dot_nn(qkv_wt[...], attn_in) + qkv_b
    queries = (projected[:features] * scale).astype(BF16)
    keys = projected[features : 2 * features].astype(BF16)
    values = projected[2 * features :].astype(BF16)
    blended = []
    for h in range(HEADS):
        rows = slice(h * head, (h + 1) * head)
        scores = dot_tn(keys[rows], queries[rows])
        top = jnp.max(scores, axis=0, keepdims=True)
        raised = jnp.exp(scores - top)
        attention = raised * (1.0 / jnp.sum(raised, axis=0, keepdims=True))
        attn_ref[h] = attention
        blended.append(dot_nn(values[rows], attention.astype(BF16)))
    blended = jnp.concatenate(blended, axis=0).astype(BF16)
    branch = (dot_nn(proj_wt[...], blended) + proj_b).astype(BF16)
    residual = tok_t + branch.astype(F32)
    hat2, inv2 = norm_forward(residual)
    mlp_in = (hat2 * g2 + b2).astype(BF16)

    cot = gather_window((cot0, cot1, cot2, cot3), depth, features)
    cot_t = cot.astype(F32).T
    hidden = dot_nn(fc1_wt[...], mlp_in) + fc1_b
    cdf = 0.5 * (1.0 + lax.erf(hidden * 0.7071067811865476))
    pdf = jnp.exp(-0.5 * hidden * hidden) * 0.3989422804014327
    active = (hidden * cdf).astype(BF16)
    fc2_sum = dot_nn(active, cot).astype(BF16)
    grad_pre = dot_nn(fc2_w[...], cot_t.astype(BF16)) * (cdf + hidden * pdf)
    grad_pre_b = grad_pre.astype(BF16)
    fc1_sum = dot_nt(mlp_in, grad_pre_b).astype(BF16)
    at = 0
    for col in range(0, hidden_width, LANES):
        grads[at : at + features, :] = fc1_sum[:, col : col + LANES]
        at += features
    grads[at : at + hidden_width, :] = fc2_sum[:, :LANES]
    at += hidden_width
    half = hidden_width // 2
    grads[at : at + half, :] = jnp.concatenate(
        [fc2_sum[:half, LANES:], fc2_sum[half:, LANES:]], axis=1
    )
    at += half
    grad_mlp_in = dot_nn(fc1_w[...], grad_pre_b)
    grad_resid = cot_t + norm_backward(grad_mlp_in, hat2, inv2, g2)
    grad_branch = grad_resid.astype(BF16)
    proj_sum = dot_nt(blended, grad_branch).astype(BF16)
    grad_blend = dot_nn(proj_w[...], grad_branch).astype(BF16)

    for h in range(HEADS):
        rows = slice(h * head, (h + 1) * head)
        grad_out = grad_blend[rows]
        attention = attn_ref[h]
        grad_attention = dot_tn(values[rows], grad_out)
        total = jnp.sum(grad_attention * attention, axis=0, keepdims=True)
        grad_scores = (attention * (grad_attention - total)).astype(BF16)
        low = h * head
        gp_ref[low : low + head, :] = dot_nn(keys[rows], grad_scores) * scale
        low += features
        gp_ref[low : low + head, :] = dot_nt(queries[rows], grad_scores)
        low += features
        gp_ref[low : low + head, :] = dot_nt(grad_out, attention.astype(BF16))
    grad_proj_in = gp_ref[...]
    grad_proj_b = grad_proj_in.astype(BF16)
    qkv_sum = dot_nt(attn_in, grad_proj_b).astype(BF16)
    both_sums = jnp.concatenate([qkv_sum, proj_sum], axis=1)
    for col in range(0, 4 * features, LANES):
        grads[at : at + features, :] = both_sums[:, col : col + LANES]
        at += features
    grad_attn_in = dot_nn(qkv_w[...], grad_proj_b).astype(BF16).astype(F32)
    grad_tok = grad_resid + norm_backward(grad_attn_in, hat1, inv1, g1)

    partials = jnp.concatenate(
        [
            token_partial(value)
            for value in (
                grad_proj_in,
                grad_branch.astype(F32),
                grad_pre,
                grad_attn_in * hat1,
                grad_attn_in,
                grad_mlp_in * hat2,
                grad_mlp_in,
            )
        ],
        axis=0,
    )
    high = partials.astype(BF16)
    low = (partials - high.astype(F32)).astype(BF16)
    split = jnp.concatenate([high, low], axis=1)
    sums = dot_nt(jnp.ones((16, 2 * LANES), BF16), split)
    rows = [sums[0:1, i : i + LANES] for i in range(0, sums.shape[1], LANES)]
    rows.append(jnp.zeros((grads.shape[0] - at - len(rows), LANES), F32))
    grads[at:, :] = jnp.concatenate(rows, axis=0).astype(BF16)
    size = keep.shape[0]

    @pl.when(core[0] == 0)
    def _():
        keep[...] = grads[:size, :]
        send[...] = grads[size:, :]

    @pl.when(core[0] != 0)
    def _():
        keep[...] = grads[size:, :]
        send[...] = grads[:size, :]

    rows_t = grad_tok.T.astype(BF16)
    places = rows_t.shape[0] // depth
    quarter = places // 4
    for k, out in enumerate((out0, out1, out2, out3)):
        out[...] = jnp.concatenate(
            [
                rows_t[t * places + k * quarter : t * places + (k + 1) * quarter]
                for t in range(depth)
            ],
            axis=1,
        )


VMEM = pl.BlockSpec(memory_space=pltpu.VMEM)
SMEM = pl.BlockSpec(memory_space=pltpu.SMEM)
PARAMS = pltpu.CompilerParams(vmem_limit_bytes=48 * 1024 * 1024)


def grad_rows(features, hidden_width):
    vector_rows = (8 * features + hidden_width) // LANES
    used = features * (2 * hidden_width + 4 * features) // LANES + vector_rows
    return -(-used // 512) * 512


def window_call(core, toks, cots, prepared, weights):
    qkv_w, proj_w, fc1_w, fc2_w = weights
    features, hidden_width = fc1_w.shape
    tokens = 4 * toks[0].size // features
    rows = grad_rows(features, hidden_width)
    quad = jax.ShapeDtypeStruct(toks[0].shape, BF16)
    half = jax.ShapeDtypeStruct((rows // 2, LANES), BF16)
    qkv_wt, proj_wt, fc1_wt, columns = prepared
    return pl.pallas_call(
        window_kernel,
        out_shape=[quad] * 4 + [half] * 2,
        in_specs=[SMEM] + [VMEM] * 16,
        out_specs=[VMEM] * 6,
        scratch_shapes=[
            pltpu.VMEM((HEADS, tokens, tokens), F32),
            pltpu.VMEM((qkv_w.shape[1], tokens), F32),
            pltpu.VMEM((rows, LANES), BF16),
        ],
        compiler_params=PARAMS,
        name="window",
    )(core, *toks, *cots, qkv_wt, qkv_w, proj_wt, proj_w, fc1_wt, fc1_w, fc2_w, columns)


def prepare_kernel(qkv_w, proj_w, fc1_w, *refs):
    vectors, (qkv_wt, proj_wt, fc1_wt, columns) = refs[:-4], refs[-4:]
    qkv_wt[...] = qkv_w[...].astype(F32).T.astype(BF16)
    proj_wt[...] = proj_w[...].astype(F32).T.astype(BF16)
    fc1_wt[...] = fc1_w[...].astype(F32).T.astype(BF16)
    row = jnp.concatenate([ref[...] for ref in vectors], axis=1)
    columns[...] = jnp.broadcast_to(row, (8, row.shape[1])).T


def prepare(qkv_w, proj_w, fc1_w, vectors):
    vectors = [v[None, :] for v in vectors]
    count = sum(v.size for v in vectors)
    return pl.pallas_call(
        prepare_kernel,
        out_shape=[jax.ShapeDtypeStruct(w.shape[::-1], BF16) for w in (qkv_w, proj_w, fc1_w)]
        + [jax.ShapeDtypeStruct((count, 8), F32)],
        in_specs=[VMEM] * (3 + len(vectors)),
        out_specs=[VMEM] * 4,
        compiler_params=PARAMS,
        name="prepare",
    )(qkv_w, proj_w, fc1_w, *vectors)


def split_kernel(field_ref, *outs):
    margin = WIN // 2
    field = field_ref[...].astype(F32)
    for out, (low_x, low_y) in zip(outs, ((margin, margin), (0, margin), (margin, 0), (0, 0))):
        out[...] = jnp.concatenate(
            [field[low_x + i, low_y : low_y + margin] for i in range(margin)], axis=0
        ).astype(BF16)


def split_quarters(field):
    quad = jax.ShapeDtypeStruct((WIN * WIN // 4, field.shape[2]), BF16)
    return pl.pallas_call(
        split_kernel,
        out_shape=[quad] * 4,
        in_specs=[VMEM],
        out_specs=[VMEM] * 4,
        compiler_params=PARAMS,
        name="split",
    )(field)


def join_kernel(*refs):
    margin = WIN // 2
    own, part_x, part_y, part_xy = [ref[...].astype(F32) for ref in refs[:4]]
    out = refs[4]
    for i in range(margin):
        rows = slice(i * margin, (i + 1) * margin)
        out[i] = jnp.concatenate([part_xy[rows], part_x[rows]], axis=0).astype(BF16)
        out[margin + i] = jnp.concatenate([part_y[rows], own[rows]], axis=0).astype(BF16)


def join_quarters(parts):
    return pl.pallas_call(
        join_kernel,
        out_shape=jax.ShapeDtypeStruct((WIN, WIN, parts[0].shape[1]), BF16),
        in_specs=[VMEM] * 4,
        out_specs=VMEM,
        compiler_params=PARAMS,
        name="join",
    )(*parts)


def exchange(parts, steps):
    own, part_x, part_y, part_xy = parts
    nx, ny = lax.axis_size("gx"), lax.axis_size("gy")
    ring_x = [(i, (i + steps) % nx) for i in range(nx)]
    ring_y = [(i, (i + steps) % ny) for i in range(ny)]
    both = [
        (i * ny + j, ((i + steps) % nx) * ny + (j + steps) % ny)
        for i in range(nx)
        for j in range(ny)
    ]
    return [
        own,
        lax.ppermute(part_x, "gx", ring_x),
        lax.ppermute(part_y, "gy", ring_y),
        lax.ppermute(part_xy, BOTH, both),
    ]


def swap(value, bit):
    return lax.ppermute(value, BOTH, [(i, i ^ bit) for i in range(256)])


CORE = 16
PLANE = [
    [16 * (4 * y + 2 * xh + core) + 8 * xl + z for y in range(4) for xh in (0, 1) for xl in (0, 1)]
    for core in (0, 1)
    for z in range(8)
]


def sum_everywhere(keep, send):
    mine = keep + swap(send, CORE)
    chunk = mine.shape[0] // 16
    pieces = lax.all_to_all(
        mine.reshape(16, chunk, LANES), BOTH, 0, 0, axis_index_groups=PLANE, tiled=True
    )
    total = jnp.sum(pieces.astype(F32), axis=0).astype(BF16)
    for bit in (1, 2, 4):
        total = total + swap(total, bit)
    spread = jnp.broadcast_to(total[None], (16, chunk, LANES))
    whole = lax.all_to_all(spread, BOTH, 0, 0, axis_index_groups=PLANE, tiled=True)
    whole = whole.reshape(-1, LANES)
    return whole, swap(whole, CORE)


def finish_kernel(core, mine, other, o_qkv, o_proj, o_fc1, o_fc2, o_vec, grads, *, factor):
    size = mine.shape[0]

    @pl.when(core[0] == 0)
    def _():
        grads[:size, :] = mine[...]
        grads[size:, :] = other[...]

    @pl.when(core[0] != 0)
    def _():
        grads[:size, :] = other[...]
        grads[size:, :] = mine[...]

    features, hidden_width = o_fc1.shape
    at = 0

    def take(rows):
        nonlocal at
        at += rows
        return grads[at - rows : at, :].astype(F32) * factor

    for col in range(0, hidden_width, LANES):
        o_fc1[:, col : col + LANES] = take(features)
    o_fc2[:, :LANES] = take(hidden_width)
    half = hidden_width // 2
    rest = take(half)
    o_fc2[:half, LANES:] = rest[:, : features - LANES]
    o_fc2[half:, LANES:] = rest[:, features - LANES :]
    both = jnp.concatenate([take(features) for _ in range(4 * features // LANES)], axis=1)
    o_qkv[...] = both[:, : 3 * features]
    o_proj[...] = both[:, 3 * features :]
    o_vec[...] = take(LANES)[: o_vec.shape[0]]


def finish(core, mine, other, shapes, factor):
    rows = shapes[4] // LANES
    outs = [jax.ShapeDtypeStruct(shape, F32) for shape in (*shapes[:4], (rows, LANES))]
    return pl.pallas_call(
        partial(finish_kernel, factor=factor),
        out_shape=outs,
        in_specs=[SMEM, VMEM, VMEM],
        out_specs=[VMEM] * 5,
        scratch_shapes=[pltpu.VMEM((2 * mine.shape[0], LANES), BF16)],
        compiler_params=PARAMS,
        name="finish",
    )(core, mine, other)


def on_device(
    tokens, cotangent, qkv_w, qkv_b, proj_w, proj_b, fc1_w, fc1_b, fc2_w, g1, b1, g2, b2
):
    features = g1.shape[0]
    token_count = tokens.size // features * lax.axis_size("gx") * lax.axis_size("gy")
    factor = float(token_count) ** (-0.5)
    core = (lax.axis_index("gx") % 2).astype(jnp.int32).reshape(1)
    vectors = (qkv_b, proj_b, fc1_b, g1, b1, g2, b2)
    toks = exchange(split_quarters(tokens), -1)
    cots = exchange(split_quarters(cotangent), -1)
    prepared = prepare(qkv_w, proj_w, fc1_w, vectors)
    *quads, keep, send = window_call(core, toks, cots, prepared, (qkv_w, proj_w, fc1_w, fc2_w))
    grad_tokens = join_quarters(exchange(quads, 1))
    mine, other = sum_everywhere(keep, send)
    shapes = [w.shape for w in (qkv_w, proj_w, fc1_w, fc2_w)] + [sum(v.size for v in vectors)]
    grads = finish(core, mine, other, shapes, factor)
    return (grad_tokens, *grads[:4], grads[4].reshape(-1))


def solution(mesh):
    spec = P("gx", "gy", None)
    return jax.shard_map(
        on_device,
        mesh=mesh,
        in_specs=(spec, spec) + (P(),) * 11,
        out_specs=(spec,) + (P(),) * 5,
        check_vma=False,
    )
```

time: 357 us -> 95.3 us (0.27)
  waiting for transfers between devices: 198 us -> 15.7 us
  blocking collectives: 80.3 us -> 24.7 us
  matrix products: 23.8 us -> 0 us
  Pallas kernels: 0 us -> 14 us
  between operations: 14.7 us -> 0.82 us
  starting transfers between devices: 21.4 us -> 30.1 us
  local copies, waits for them, and re-layouts: 13.1 us -> 8.94 us
    psum x1 -> x0, waiting for transfers between devices: 175 us -> none  [on_device(): lax.psum((scaled[0], scaled[1], scaled[2], scaled[3], scaled[4], scaled[5...]
    psum x1 -> x0, blocking collectives: 80.3 us -> none  [on_device(): lax.psum((scaled[0], scaled[1], scaled[2], scaled[3], scaled[4], scaled[5...]
    all_to_all x0 -> x2, blocking collectives: none -> 24.7 us  [the longest x1 13 us: sum_everywhere(): lax.all_to_all(mine.reshape(16, chunk, LANES), BOTH, 0, 0, axis_index_gro...]
    dot_general x16 -> x0, matrix products: 19.3 us -> none  [the longest x4 4.63 us: contract_rows(): lax.dot_general(left_side, right_side, (((0,), (0,)), ((), ())), preferre...]
    pallas_call x0 -> x6, Pallas kernels: none -> 14 us  [the longest x1 11.3 us: window_call(): pl.pallas_call(window_kernel, out_shape=[quad] * 4 + [half] * 2, in_specs...]
    ppermute x8 -> x14, starting transfers between devices: 21.3 us -> 30.1 us  [the longest x5 11.5 us: swap(): return lax.ppermute(value, BOTH, [(i, i ^ bit) for i in range(256)])]
    ppermute x8 -> x14, waiting for transfers between devices: 23.4 us -> 15.7 us  [the longest x5 10.8 us: swap(): return lax.ppermute(value, BOTH, [(i, i ^ bit) for i in range(256)])]
    sub x1 -> x0, matrix products: 4.54 us -> none  [attend_forward(): attention_b = jax.nn.softmax(scores, axis=-1).astype(jnp.bfloat16)]
  transfers between devices with their start and end apart: 9 -> 14, of which waited for: 9 -> 6; matrix products, arithmetic and copies ran while one was open for 1% -> 3% of each run, Pallas kernels for 0% -> 2%
where the time goes in v1:
time: 95.3 us; the launch traced here: 94.5 us
  starting transfers between devices  30.1 us (32%)
  blocking collectives  24.7 us (26%)
  waiting for transfers between devices  15.7 us (16%)
  Pallas kernels  14 us (15%)
  local copies, waits for them, and re-layouts  8.94 us (9%)
    all_to_all x1, blocking collectives, sum_everywhere(): lax.all_to_all(mine.reshape(16, chunk, LANES), BOTH, 0, 0, axis_index_gro...  13 us
    all_to_all x1, blocking collectives, sum_everywhere(): lax.all_to_all(spread, BOTH, 0, 0, axis_index_groups=PLANE, tiled=True)  11.7 us
    ppermute x5, starting transfers between devices, swap(): return lax.ppermute(value, BOTH, [(i, i ^ bit) for i in range(256)])  11.5 us
    pallas_call x1, Pallas kernels, window_call(): pl.pallas_call(window_kernel, out_shape=[quad] * 4 + [half] * 2, in_specs...  11.3 us
    ppermute x5, waiting for transfers between devices, swap(): return lax.ppermute(value, BOTH, [(i, i ^ bit) for i in range(256)])  10.8 us
    ppermute x3, starting transfers between devices, exchange(): lax.ppermute(part_xy, BOTH, both)  8.32 us
    unnamed x22, local copies, waits for them, and re-layouts  7.5 us
    ppermute x3, starting transfers between devices, exchange(): lax.ppermute(part_y, 'gy', ring_y)  6.44 us
  transfers between devices with their start and end apart: 14, of which 6 were waited for; matrix products, arithmetic and copies ran while one was open for 3% of the time, Pallas kernels for 2%

profile of v1, /device:TPU:1, one launch (start us, length us, event | category | flops | bytes accessed | tf_op | source)
XLA Modules:
  0.0 94.5 jit_solution(7138966286200231073)
XLA Ops:
  0.7 1.0 %copy-done.3 = bf16[8,8,1536]{2,1,0:T(8,128)(2,1)S(1)} copy-done((bf16[8,8,1536]{2,1,0:T(8,128)(2,1)S(1)}, bf16[8,8,1536]{2,1,0:T(8,128)(2,1)}, u32[]{:S(2)}) %copy-start.3) | copy-done | bytes 196632
  1.7 0.1 split.2
  1.7 3.3 %collective-permute-start = (bf16[16,1536]{1,0:T(8,128)(2,1)S(1)}, bf16[16,1536]{1,0:T(8,128)(2,1)S(1)}, u32[]{:S(2)}, u32[]{:S(2)}) collective-permute-start(bf16[16,1536]{1,0:T(8,128)(2,1)S(1)} %get-tuple-element.30), channel_id=1, source_target_pairs={{0,240},{16,0},{32,16},{48,32},{64,48},{80,64},{96,80},{112,96},{1... | collective-permute-start | bytes 147464 | tf_op jit(solution)/shard_map/ppermute | solution.py:306
  5.0 4.8 %collective-permute-start.1 = (bf16[16,1536]{1,0:T(8,128)(2,1)S(1)}, bf16[16,1536]{1,0:T(8,128)(2,1)S(1)}, u32[]{:S(2)}, u32[]{:S(2)}) collective-permute-start(bf16[16,1536]{1,0:T(8,128)(2,1)S(1)} %get-tuple-element.31), channel_id=1, source_target_pairs={{0,15},{1,0},{2,1},{3,2},{4,3},{5,4},{6,5},{7,6},{8,7},{9,8},{10,9... | collective-permute-start | bytes 147464 | tf_op jit(solution)/shard_map/ppermute | solution.py:307
  9.8 4.9 %collective-permute-start.2 = (bf16[16,1536]{1,0:T(8,128)(2,1)S(1)}, bf16[16,1536]{1,0:T(8,128)(2,1)S(1)}, u32[]{:S(2)}, u32[]{:S(2)}) collective-permute-start(bf16[16,1536]{1,0:T(8,128)(2,1)S(1)} %get-tuple-element.32), channel_id=1, source_target_pairs={{0,255},{1,240},{2,241},{3,242},{4,243},{5,244},{6,245},{7,246},{8... | collective-permute-start | bytes 147464 | tf_op jit(solution)/shard_map/ppermute | solution.py:308
  14.7 0.9 copy-done.4
  15.6 0.1 split.3
  15.7 0.1 collective-permute-start.3
  15.8 0.9 collective-permute-start.4
  16.7 2.2 %collective-permute-start.5 = (bf16[16,1536]{1,0:T(8,128)(2,1)S(1)}, bf16[16,1536]{1,0:T(8,128)(2,1)S(1)}, u32[]{:S(2)}, u32[]{:S(2)}) collective-permute-start(bf16[16,1536]{1,0:T(8,128)(2,1)S(1)} %get-tuple-element.36), channel_id=1, source_target_pairs={{0,255},{1,240},{2,241},{3,242},{4,243},{5,244},{6,245},{7,246},{8... | collective-permute-start | bytes 147464 | tf_op jit(solution)/shard_map/ppermute | solution.py:308
  18.9 0.7 broadcast_in_dim.27.refs_0_
  19.6 0.7 broadcast_in_dim.29.refs_2_
  20.3 1.1 %copy.19.fc2_w = bf16[768,192]{1,0:T(8,128)(2,1)S(1)} copy(bf16[768,192]{0,1:T(8,128)(2,1)} %param.21) | data formatting | bytes 589824 | tf_op args[8]
  21.5 0.0 copy-start.5
  21.5 0.7 copy-done.5
  22.2 0.7 copy-done.6
  22.8 0.7 copy-done.7
  23.5 0.7 copy-done.8
  24.2 0.7 copy-done.9
  24.9 0.6 prepare.1
  25.5 0.0 collective-permute-done.1.tok2
  25.5 0.0 collective-permute-done.2.tok3
  25.5 0.0 collective-permute-done.4.cot2
  25.5 0.0 collective-permute-done.5.cot3
  25.6 11.3 %window.1 = (bf16[16,1536]{1,0:T(8,128)(2,1)S(1)}, bf16[16,1536]{1,0:T(8,128)(2,1)S(1)}, bf16[16,1536]{1,0:T(8,128)(2,1)S(1)}, bf16[16,1536]{1,0:T(8,128)(2,1)S(...) custom-call(s32[1]{0:T(128)} %bitcast.core, bf16[16,1536]{1,0:T(8,128)(2,1)S(1)} %get-tuple-element.29.tok0, ...), custom_call_target="tpu_custom_call" | custom-call | tf_op jit(solution)/shard_map/window/pallas_call | solution.py:214
  36.9 1.5 %collective-permute-start.9 = (bf16[1792,128]{1,0:T(8,128)(2,1)S(1)}, bf16[1792,128]{1,0:T(8,128)(2,1)S(1)}, u32[]{:S(2)}, u32[]{:S(2)}) collective-permute-start(bf16[1792,128]{1,0:T(8,128)(2,1)S(1)} %get-tuple-element.46), channel_id=1, source_target_pairs={{0,16},{1,17},{2,18},{3,19},{4,20},{5,21},{6,22},{7,23},{8,24},{9,... | collective-permute-start | bytes 1376264 | tf_op jit(solution)/shard_map/ppermute | solution.py:313
  38.3 1.4 %collective-permute-done.9 = bf16[1792,128]{1,0:T(8,128)(2,1)S(1)} collective-permute-done((bf16[1792,128]{1,0:T(8,128)(2,1)S(1)}, bf16[1792,128]{1,0:T(8,128)(2,1)S(1)}, u32[]{:S(2)}, u32[]{:S(2)}) %collective-permute-start.9) | collective-permute-done | bytes 458784 | tf_op jit(solution)/shard_map/ppermute | solution.py:313
  39.8 0.1 add.17
  39.9 13.0 %all_to_all.10 = bf16[16,112,128]{2,1,0:T(8,128)(2,1)S(1)} all-to-all(bf16[16,112,128]{2,1,0:T(8,128)(2,1)S(1)} %bitcast.16), channel_id=1, replica_groups={{0,8,32,40,64,72,96,104,128,136,160,168,192,200,224,232},{1,9,33,41,65,..., dimensions={0} | all-to-all | bytes 917504 | tf_op jit(solution)/shard_map/all_to_all | solution.py:327
  52.9 0.1 reduce_sum.12
  53.0 0.8 collective-permute-start.10
  53.8 2.0 %collective-permute-done.10 = bf16[112,128]{1,0:T(8,128)(2,1)S(1)} collective-permute-done((bf16[112,128]{1,0:T(8,128)(2,1)S(1)}, bf16[112,128]{1,0:T(8,128)(2,1)S(1)}, u32[]{:S(2)}, u32[]{:S(2)}) %collective-permute-start.10) | collective-permute-done | bytes 28704 | tf_op jit(solution)/shard_map/ppermute | solution.py:313
  55.8 1.5 %collective-permute-start.11 = (bf16[112,128]{1,0:T(8,128)(2,1)S(1)}, bf16[112,128]{1,0:T(8,128)(2,1)S(1)}, u32[]{:S(2)}, u32[]{:S(2)}) collective-permute-start(bf16[112,128]{1,0:T(8,128)(2,1)S(1)} %add.18), channel_id=1, source_target_pairs={{0,2},{1,3},{2,0},{3,1},{4,6},{5,7},{6,4},{7,5},{8,10},{9,11},{10,... | collective-permute-start | bytes 86024 | tf_op jit(solution)/shard_map/ppermute | solution.py:313
  57.3 2.5 %collective-permute-done.11 = bf16[112,128]{1,0:T(8,128)(2,1)S(1)} collective-permute-done((bf16[112,128]{1,0:T(8,128)(2,1)S(1)}, bf16[112,128]{1,0:T(8,128)(2,1)S(1)}, u32[]{:S(2)}, u32[]{:S(2)}) %collective-permute-start.11) | collective-permute-done | bytes 28704 | tf_op jit(solution)/shard_map/ppermute | solution.py:313
  59.8 1.8 %collective-permute-start.12 = (bf16[112,128]{1,0:T(8,128)(2,1)S(1)}, bf16[112,128]{1,0:T(8,128)(2,1)S(1)}, u32[]{:S(2)}, u32[]{:S(2)}) collective-permute-start(bf16[112,128]{1,0:T(8,128)(2,1)S(1)} %add.19), channel_id=1, source_target_pairs={{0,4},{1,5},{2,6},{3,7},{4,0},{5,1},{6,2},{7,3},{8,12},{9,13},{10,... | collective-permute-start | bytes 86024 | tf_op jit(solution)/shard_map/ppermute | solution.py:313
  61.5 4.9 %collective-permute-done.12 = bf16[112,128]{1,0:T(8,128)(2,1)S(1)} collective-permute-done((bf16[112,128]{1,0:T(8,128)(2,1)S(1)}, bf16[112,128]{1,0:T(8,128)(2,1)S(1)}, u32[]{:S(2)}, u32[]{:S(2)}) %collective-permute-start.12) | collective-permute-done | bytes 28704 | tf_op jit(solution)/shard_map/ppermute | solution.py:313
  66.5 0.1 broadcast_in_dim.34
  66.6 11.7 %all_to_all.11 = bf16[16,112,128]{2,1,0:T(8,128)(2,1)S(1)} all-to-all(bf16[16,112,128]{2,1,0:T(8,128)(2,1)S(1)} %broadcast_in_dim.34), channel_id=1, replica_groups={{0,8,32,40,64,72,96,104,128,136,160,168,192,200,224,232},{1,9,33,41,65,..., dimensions={0} | all-to-all | bytes 917504 | tf_op jit(solution)/shard_map/all_to_all | solution.py:334
  78.3 5.9 %collective-permute-start.13 = (bf16[1792,128]{1,0:T(8,128)(2,1)S(1)}, bf16[1792,128]{1,0:T(8,128)(2,1)S(1)}, u32[]{:S(2)}, u32[]{:S(2)}) collective-permute-start(bf16[1792,128]{1,0:T(8,128)(2,1)S(1)} %bitcast.9), channel_id=1, source_target_pairs={{0,16},{1,17},{2,18},{3,19},{4,20},{5,21},{6,22},{7,23},{8,24},{9,... | collective-permute-start | bytes 1376264 | tf_op jit(solution)/shard_map/ppermute | solution.py:313
  84.2 0.5 collective-permute-start.6
  84.7 0.7 collective-permute-start.7
  85.4 1.2 %collective-permute-start.8 = (bf16[16,1536]{1,0:T(8,128)(2,1)S(1)}, bf16[16,1536]{1,0:T(8,128)(2,1)S(1)}, u32[]{:S(2)}, u32[]{:S(2)}) collective-permute-start(bf16[16,1536]{1,0:T(8,128)(2,1)S(1)} %get-tuple-element.44), channel_id=1, source_target_pairs={{0,17},{1,18},{2,19},{3,20},{4,21},{5,22},{6,23},{7,24},{8,25},{9,... | collective-permute-start | bytes 147464 | tf_op jit(solution)/shard_map/ppermute | solution.py:308
  86.6 0.0 collective-permute-done.6.refs_1_
  86.6 3.5 %collective-permute-done.7.refs_2_ = bf16[16,1536]{1,0:T(8,128)(2,1)S(1)} collective-permute-done((bf16[16,1536]{1,0:T(8,128)(2,1)S(1)}, bf16[16,1536]{1,0:T(8,128)(2,1)S(1)}, u32[]{:S(2)}, u32[]{:S(2)}) %collective-permute-start.7) | collective-permute-done | bytes 49184 | tf_op jit(solution)/shard_map/ppermute | solution.py:307
  90.1 1.4 %collective-permute-done.8.refs_3_ = bf16[16,1536]{1,0:T(8,128)(2,1)S(1)} collective-permute-done((bf16[16,1536]{1,0:T(8,128)(2,1)S(1)}, bf16[16,1536]{1,0:T(8,128)(2,1)S(1)}, u32[]{:S(2)}, u32[]{:S(2)}) %collective-permute-start.8) | collective-permute-done | bytes 49184 | tf_op jit(solution)/shard_map/ppermute | solution.py:308
  91.5 0.7 join.1
  92.2 1.3 %finish.1 = (f32[192,576]{1,0:T(8,128)}, f32[192,192]{1,0:T(8,128)}, f32[192,768]{1,0:T(8,128)}, f32[768,192]{1,0:T(8,128)S(1)}, f32[18,128]{1,0:T(8,128)}) custom-call(s32[1]{0:T(128)} %bitcast.core, bf16[1792,128]{1,0:T(8,128)(2,1)S(1)} %bitcast.10, bf16[1792,128]{1,0:T(8,128)(2,1)S(1)} %collective-permute-done.13.other), custom_call_target="tpu_custom_call" | custom-call | tf_op jit(solution)/shard_map/finish/pallas_call | solution.py:376
  93.5 1.1 %copy.20 = f32[768,192]{0,1:T(8,128)} copy(f32[768,192]{1,0:T(8,128)S(1)} %get-tuple-element.56) | data formatting | bytes 1179648
  (18 shorter events, 0.1 us)
Async XLA Ops:
  0.6 20.8 %copy-start = (bf16[192,768]{1,0:T(8,128)(2,1)S(1)}, bf16[192,768]{1,0:T(8,128)(2,1)}, u32[]{:S(2)}) copy-start(bf16[192,768]{1,0:T(8,128)(2,1)} %fc1_w.3) | copy-start | bytes 884740
  0.6 20.8 %copy-start.2 = (bf16[192,192]{1,0:T(8,128)(2,1)S(1)}, bf16[192,192]{1,0:T(8,128)(2,1)}, u32[]{:S(2)}) copy-start(bf16[192,192]{1,0:T(8,128)(2,1)} %proj_w.3) | copy-start | bytes 221188
  0.7 20.8 %copy-start.1 = (bf16[192,576]{1,0:T(8,128)(2,1)S(1)}, bf16[192,576]{1,0:T(8,128)(2,1)}, u32[]{:S(2)}) copy-start(bf16[192,576]{1,0:T(8,128)(2,1)} %qkv_w.3) | copy-start | bytes 663556
  0.7 1.0 %copy-start.3 = (bf16[8,8,1536]{2,1,0:T(8,128)(2,1)S(1)}, bf16[8,8,1536]{2,1,0:T(8,128)(2,1)}, u32[]{:S(2)}) copy-start(bf16[8,8,1536]{2,1,0:T(8,128)(2,1)} %field_ref.2) | copy-start | bytes 589828
  1.7 15.0 %collective-permute-start = (bf16[16,1536]{1,0:T(8,128)(2,1)S(1)}, bf16[16,1536]{1,0:T(8,128)(2,1)S(1)}, u32[]{:S(2)}, u32[]{:S(2)}) collective-permute-start(bf16[16,1536]{1,0:T(8,128)(2,1)S(1)} %get-tuple-element.30), channel_id=1, source_target_pairs={{0,240},{16,0},{32,16},{48,32},{64,48},{80,64},{96,80},{112,96},{1... | collective-permute-start | bytes 147464 | tf_op jit(solution)/shard_map/ppermute | solution.py:306
  5.0 20.5 %collective-permute-start.1 = (bf16[16,1536]{1,0:T(8,128)(2,1)S(1)}, bf16[16,1536]{1,0:T(8,128)(2,1)S(1)}, u32[]{:S(2)}, u32[]{:S(2)}) collective-permute-start(bf16[16,1536]{1,0:T(8,128)(2,1)S(1)} %get-tuple-element.31), channel_id=1, source_target_pairs={{0,15},{1,0},{2,1},{3,2},{4,3},{5,4},{6,5},{7,6},{8,7},{9,8},{10,9... | collective-permute-start | bytes 147464 | tf_op jit(solution)/shard_map/ppermute | solution.py:307
  9.8 15.7 %collective-permute-start.2 = (bf16[16,1536]{1,0:T(8,128)(2,1)S(1)}, bf16[16,1536]{1,0:T(8,128)(2,1)S(1)}, u32[]{:S(2)}, u32[]{:S(2)}) collective-permute-start(bf16[16,1536]{1,0:T(8,128)(2,1)S(1)} %get-tuple-element.32), channel_id=1, source_target_pairs={{0,255},{1,240},{2,241},{3,242},{4,243},{5,244},{6,245},{7,246},{8... | collective-permute-start | bytes 147464 | tf_op jit(solution)/shard_map/ppermute | solution.py:308
  14.7 0.9 copy-start.4
  15.7 9.8 %collective-permute-start.3 = (bf16[16,1536]{1,0:T(8,128)(2,1)S(1)}, bf16[16,1536]{1,0:T(8,128)(2,1)S(1)}, u32[]{:S(2)}, u32[]{:S(2)}) collective-permute-start(bf16[16,1536]{1,0:T(8,128)(2,1)S(1)} %get-tuple-element.34), channel_id=1, source_target_pairs={{0,240},{16,0},{32,16},{48,32},{64,48},{80,64},{96,80},{112,96},{1... | collective-permute-start | bytes 147464 | tf_op jit(solution)/shard_map/ppermute | solution.py:306
  15.8 9.7 %collective-permute-start.4 = (bf16[16,1536]{1,0:T(8,128)(2,1)S(1)}, bf16[16,1536]{1,0:T(8,128)(2,1)S(1)}, u32[]{:S(2)}, u32[]{:S(2)}) collective-permute-start(bf16[16,1536]{1,0:T(8,128)(2,1)S(1)} %get-tuple-element.35), channel_id=1, source_target_pairs={{0,15},{1,0},{2,1},{3,2},{4,3},{5,4},{6,5},{7,6},{8,7},{9,8},{10,9... | collective-permute-start | bytes 147464 | tf_op jit(solution)/shard_map/ppermute | solution.py:307
  16.7 8.8 %collective-permute-start.5 = (bf16[16,1536]{1,0:T(8,128)(2,1)S(1)}, bf16[16,1536]{1,0:T(8,128)(2,1)S(1)}, u32[]{:S(2)}, u32[]{:S(2)}) collective-permute-start(bf16[16,1536]{1,0:T(8,128)(2,1)S(1)} %get-tuple-element.36), channel_id=1, source_target_pairs={{0,255},{1,240},{2,241},{3,242},{4,243},{5,244},{6,245},{7,246},{8... | collective-permute-start | bytes 147464 | tf_op jit(solution)/shard_map/ppermute | solution.py:308
  21.5 0.7 copy-start.5
  22.2 0.7 copy-start.6
  22.8 0.7 copy-start.7
  23.5 0.7 copy-start.8
  24.2 0.7 copy-start.9
  36.9 2.9 %collective-permute-start.9 = (bf16[1792,128]{1,0:T(8,128)(2,1)S(1)}, bf16[1792,128]{1,0:T(8,128)(2,1)S(1)}, u32[]{:S(2)}, u32[]{:S(2)}) collective-permute-start(bf16[1792,128]{1,0:T(8,128)(2,1)S(1)} %get-tuple-element.46), channel_id=1, source_target_pairs={{0,16},{1,17},{2,18},{3,19},{4,20},{5,21},{6,22},{7,23},{8,24},{9,... | collective-permute-start | bytes 1376264 | tf_op jit(solution)/shard_map/ppermute | solution.py:313
  53.0 2.8 %collective-permute-start.10 = (bf16[112,128]{1,0:T(8,128)(2,1)S(1)}, bf16[112,128]{1,0:T(8,128)(2,1)S(1)}, u32[]{:S(2)}, u32[]{:S(2)}) collective-permute-start(bf16[112,128]{1,0:T(8,128)(2,1)S(1)} %reduce_sum.12), channel_id=1, source_target_pairs={{0,1},{1,0},{2,3},{3,2},{4,5},{5,4},{6,7},{7,6},{8,9},{9,8},{10,11... | collective-permute-start | bytes 86024 | tf_op jit(solution)/shard_map/ppermute | solution.py:313
  55.8 3.9 %collective-permute-start.11 = (bf16[112,128]{1,0:T(8,128)(2,1)S(1)}, bf16[112,128]{1,0:T(8,128)(2,1)S(1)}, u32[]{:S(2)}, u32[]{:S(2)}) collective-permute-start(bf16[112,128]{1,0:T(8,128)(2,1)S(1)} %add.18), channel_id=1, source_target_pairs={{0,2},{1,3},{2,0},{3,1},{4,6},{5,7},{6,4},{7,5},{8,10},{9,11},{10,... | collective-permute-start | bytes 86024 | tf_op jit(solution)/shard_map/ppermute | solution.py:313
  59.8 6.7 %collective-permute-start.12 = (bf16[112,128]{1,0:T(8,128)(2,1)S(1)}, bf16[112,128]{1,0:T(8,128)(2,1)S(1)}, u32[]{:S(2)}, u32[]{:S(2)}) collective-permute-start(bf16[112,128]{1,0:T(8,128)(2,1)S(1)} %add.19), channel_id=1, source_target_pairs={{0,4},{1,5},{2,6},{3,7},{4,0},{5,1},{6,2},{7,3},{8,12},{9,13},{10,... | collective-permute-start | bytes 86024 | tf_op jit(solution)/shard_map/ppermute | solution.py:313
  78.3 13.9 %collective-permute-start.13 = (bf16[1792,128]{1,0:T(8,128)(2,1)S(1)}, bf16[1792,128]{1,0:T(8,128)(2,1)S(1)}, u32[]{:S(2)}, u32[]{:S(2)}) collective-permute-start(bf16[1792,128]{1,0:T(8,128)(2,1)S(1)} %bitcast.9), channel_id=1, source_target_pairs={{0,16},{1,17},{2,18},{3,19},{4,20},{5,21},{6,22},{7,23},{8,24},{9,... | collective-permute-start | bytes 1376264 | tf_op jit(solution)/shard_map/ppermute | solution.py:313
  84.2 2.4 %collective-permute-start.6 = (bf16[16,1536]{1,0:T(8,128)(2,1)S(1)}, bf16[16,1536]{1,0:T(8,128)(2,1)S(1)}, u32[]{:S(2)}, u32[]{:S(2)}) collective-permute-start(bf16[16,1536]{1,0:T(8,128)(2,1)S(1)} %get-tuple-element.42), channel_id=1, source_target_pairs={{0,16},{16,32},{32,48},{48,64},{64,80},{80,96},{96,112},{112,128},... | collective-permute-start | bytes 147464 | tf_op jit(solution)/shard_map/ppermute | solution.py:306
  84.7 5.4 %collective-permute-start.7 = (bf16[16,1536]{1,0:T(8,128)(2,1)S(1)}, bf16[16,1536]{1,0:T(8,128)(2,1)S(1)}, u32[]{:S(2)}, u32[]{:S(2)}) collective-permute-start(bf16[16,1536]{1,0:T(8,128)(2,1)S(1)} %get-tuple-element.43), channel_id=1, source_target_pairs={{0,1},{1,2},{2,3},{3,4},{4,5},{5,6},{6,7},{7,8},{8,9},{9,10},{10,1... | collective-permute-start | bytes 147464 | tf_op jit(solution)/shard_map/ppermute | solution.py:307
  85.4 6.1 %collective-permute-start.8 = (bf16[16,1536]{1,0:T(8,128)(2,1)S(1)}, bf16[16,1536]{1,0:T(8,128)(2,1)S(1)}, u32[]{:S(2)}, u32[]{:S(2)}) collective-permute-start(bf16[16,1536]{1,0:T(8,128)(2,1)S(1)} %get-tuple-element.44), channel_id=1, source_target_pairs={{0,17},{1,18},{2,19},{3,20},{4,21},{5,22},{6,23},{7,24},{8,25},{9,... | collective-permute-start | bytes 147464 | tf_op jit(solution)/shard_map/ppermute | solution.py:308

commit v2 on v1

--- a/solution.py
+++ b/solution.py
@@ -48,35 +48,41 @@
     return total
 
 
-def gather_window(refs, depth, features):
-    field = jnp.concatenate([ref[...] for ref in refs], axis=0)
+def gather_window(refs, which, depth, features):
+    rows = refs[0].shape[0] // 2
+    field = jnp.concatenate([ref[which * rows : (which + 1) * rows, :] for ref in refs], axis=0)
     return jnp.concatenate(
         [field[:, t * features : (t + 1) * features] for t in range(depth)], axis=0
     )
 
 
 def window_kernel(
-    core, tok0, tok1, tok2, tok3, cot0, cot1, cot2, cot3,
-    qkv_wt, qkv_w, proj_wt, proj_w, fc1_wt, fc1_w, fc2_w, columns,
+    core, quad0, quad1, quad2, quad3, weights, vectors,
     out0, out1, out2, out3, keep, send,
     attn_ref, gp_ref, grads,
 ):
-    features = proj_w.shape[0]
-    hidden_width = fc2_w.shape[0]
+    features = weights.shape[0]
+    hidden_width = vectors.shape[0] * LANES - 8 * features
     head = features // HEADS
-    depth = tok0.shape[1] // features
+    depth = quad0.shape[1] // features
+    quads = (quad0, quad1, quad2, quad3)
     scale = head ** (-0.5)
     at = 0
+    fc1_w, fc2_wt, qkv_w, proj_w = [
+        weights[:, low : low + size] for low, size in weight_places(features, hidden_width)
+    ]
+    row = jnp.concatenate([vectors[i : i + 1, :] for i in range(vectors.shape[0])], axis=1)
+    columns = jnp.broadcast_to(row, (8, row.shape[1])).T
     params = []
     for size in (3 * features, features, hidden_width) + (features,) * 4:
         params.append(columns[at : at + size, 0:1])
         at += size
     qkv_b, proj_b, fc1_b, g1, b1, g2, b2 = params
 
-    tok_t = gather_window((tok0, tok1, tok2, tok3), depth, features).astype(F32).T
+    tok_t = gather_window(quads, 0, depth, features).astype(F32).T
     hat1, inv1 = norm_forward(tok_t)
     attn_in = (hat1 * g1 + b1).astype(BF16)
-    projected = dot_nn(qkv_wt[...], attn_in) + qkv_b
+    projected = dot_tn(qkv_w, attn_in) + qkv_b
     queries = (projected[:features] * scale).astype(BF16)
     keys = projected[features : 2 * features].astype(BF16)
     values = projected[2 * features :].astype(BF16)
@@ -90,37 +96,31 @@
         attn_ref[h] = attention
         blended.append(dot_nn(values[rows], attention.astype(BF16)))
     blended = jnp.concatenate(blended, axis=0).astype(BF16)
-    branch = (dot_nn(proj_wt[...], blended) + proj_b).astype(BF16)
+    branch = (dot_tn(proj_w, blended) + proj_b).astype(BF16)
     residual = tok_t + branch.astype(F32)
     hat2, inv2 = norm_forward(residual)
     mlp_in = (hat2 * g2 + b2).astype(BF16)
 
-    cot = gather_window((cot0, cot1, cot2, cot3), depth, features)
-    cot_t = cot.astype(F32).T
-    hidden = dot_nn(fc1_wt[...], mlp_in) + fc1_b
+    cot_t = gather_window(quads, 1, depth, features).astype(F32).T
+    cot_b = cot_t.astype(BF16)
+    hidden = dot_tn(fc1_w, mlp_in) + fc1_b
     cdf = 0.5 * (1.0 + lax.erf(hidden * 0.7071067811865476))
     pdf = jnp.exp(-0.5 * hidden * hidden) * 0.3989422804014327
     active = (hidden * cdf).astype(BF16)
-    fc2_sum = dot_nn(active, cot).astype(BF16)
-    grad_pre = dot_nn(fc2_w[...], cot_t.astype(BF16)) * (cdf + hidden * pdf)
+    fc2_sum = dot_nt(cot_b, active).astype(BF16)
+    grad_pre = dot_tn(fc2_wt, cot_b) * (cdf + hidden * pdf)
     grad_pre_b = grad_pre.astype(BF16)
     fc1_sum = dot_nt(mlp_in, grad_pre_b).astype(BF16)
     at = 0
-    for col in range(0, hidden_width, LANES):
-        grads[at : at + features, :] = fc1_sum[:, col : col + LANES]
-        at += features
-    grads[at : at + hidden_width, :] = fc2_sum[:, :LANES]
-    at += hidden_width
-    half = hidden_width // 2
-    grads[at : at + half, :] = jnp.concatenate(
-        [fc2_sum[:half, LANES:], fc2_sum[half:, LANES:]], axis=1
-    )
-    at += half
-    grad_mlp_in = dot_nn(fc1_w[...], grad_pre_b)
+    for value in (fc1_sum, fc2_sum):
+        for col in range(0, hidden_width, LANES):
+            grads[at : at + features, :] = value[:, col : col + LANES]
+            at += features
+    grad_mlp_in = dot_nn(fc1_w, grad_pre_b)
     grad_resid = cot_t + norm_backward(grad_mlp_in, hat2, inv2, g2)
     grad_branch = grad_resid.astype(BF16)
     proj_sum = dot_nt(blended, grad_branch).astype(BF16)
-    grad_blend = dot_nn(proj_w[...], grad_branch).astype(BF16)
+    grad_blend = dot_nn(proj_w, grad_branch).astype(BF16)
 
     for h in range(HEADS):
         rows = slice(h * head, (h + 1) * head)
@@ -142,7 +142,7 @@
     for col in range(0, 4 * features, LANES):
         grads[at : at + features, :] = both_sums[:, col : col + LANES]
         at += features
-    grad_attn_in = dot_nn(qkv_w[...], grad_proj_b).astype(BF16).astype(F32)
+    grad_attn_in = dot_nn(qkv_w, grad_proj_b).astype(BF16).astype(F32)
     grad_tok = grad_resid + norm_backward(grad_attn_in, hat1, inv1, g1)
 
     partials = jnp.concatenate(
@@ -203,63 +203,53 @@
     return -(-used // 512) * 512
 
 
-def window_call(core, toks, cots, prepared, weights):
-    qkv_w, proj_w, fc1_w, fc2_w = weights
-    features, hidden_width = fc1_w.shape
-    tokens = 4 * toks[0].size // features
+def weight_places(features, hidden_width):
+    qkv_at = 2 * hidden_width
+    proj_at = -(-(qkv_at + 3 * features) // LANES) * LANES
+    return (
+        (0, hidden_width),
+        (hidden_width, hidden_width),
+        (qkv_at, 3 * features),
+        (proj_at, features),
+    )
+
+
+def window_call(core, quads, weights, vectors):
+    features, hidden_width = weights[0].shape
+    tokens = 2 * quads[0].size // features
     rows = grad_rows(features, hidden_width)
-    quad = jax.ShapeDtypeStruct(toks[0].shape, BF16)
+    places = weight_places(features, hidden_width)
+    gap = jnp.zeros((features, places[3][0] - places[2][0] - places[2][1]), BF16)
+    joined = jnp.concatenate([*weights[:3], gap, weights[3]], axis=1)
+    rows_of_vectors = jnp.concatenate(vectors).reshape(-1, LANES)
+    quad = jax.ShapeDtypeStruct((quads[0].shape[0] // 2, quads[0].shape[1]), BF16)
     half = jax.ShapeDtypeStruct((rows // 2, LANES), BF16)
-    qkv_wt, proj_wt, fc1_wt, columns = prepared
     return pl.pallas_call(
         window_kernel,
         out_shape=[quad] * 4 + [half] * 2,
-        in_specs=[SMEM] + [VMEM] * 16,
+        in_specs=[SMEM] + [VMEM] * 6,
         out_specs=[VMEM] * 6,
         scratch_shapes=[
             pltpu.VMEM((HEADS, tokens, tokens), F32),
-            pltpu.VMEM((qkv_w.shape[1], tokens), F32),
+            pltpu.VMEM((3 * features, tokens), F32),
             pltpu.VMEM((rows, LANES), BF16),
         ],
         compiler_params=PARAMS,
         name="window",
-    )(core, *toks, *cots, qkv_wt, qkv_w, proj_wt, proj_w, fc1_wt, fc1_w, fc2_w, columns)
-
-
-def prepare_kernel(qkv_w, proj_w, fc1_w, *refs):
-    vectors, (qkv_wt, proj_wt, fc1_wt, columns) = refs[:-4], refs[-4:]
-    qkv_wt[...] = qkv_w[...].astype(F32).T.astype(BF16)
-    proj_wt[...] = proj_w[...].astype(F32).T.astype(BF16)
-    fc1_wt[...] = fc1_w[...].astype(F32).T.astype(BF16)
-    row = jnp.concatenate([ref[...] for ref in vectors], axis=1)
-    columns[...] = jnp.broadcast_to(row, (8, row.shape[1])).T
-
-
-def prepare(qkv_w, proj_w, fc1_w, vectors):
-    vectors = [v[None, :] for v in vectors]
-    count = sum(v.size for v in vectors)
-    return pl.pallas_call(
-        prepare_kernel,
-        out_shape=[jax.ShapeDtypeStruct(w.shape[::-1], BF16) for w in (qkv_w, proj_w, fc1_w)]
-        + [jax.ShapeDtypeStruct((count, 8), F32)],
-        in_specs=[VMEM] * (3 + len(vectors)),
-        out_specs=[VMEM] * 4,
-        compiler_params=PARAMS,
-        name="prepare",
-    )(qkv_w, proj_w, fc1_w, *vectors)
-
-
-def split_kernel(field_ref, *outs):
+    )(core, *quads, joined, rows_of_vectors)
+
+
+def split_kernel(fields_ref, *outs):
     margin = WIN // 2
-    field = field_ref[...].astype(F32)
+    fields = [fields_ref[i].astype(F32) for i in range(2)]
     for out, (low_x, low_y) in zip(outs, ((margin, margin), (0, margin), (margin, 0), (0, 0))):
         out[...] = jnp.concatenate(
-            [field[low_x + i, low_y : low_y + margin] for i in range(margin)], axis=0
+            [f[low_x + i, low_y : low_y + margin] for f in fields for i in range(margin)], axis=0
         ).astype(BF16)
 
 
-def split_quarters(field):
-    quad = jax.ShapeDtypeStruct((WIN * WIN // 4, field.shape[2]), BF16)
+def split_quarters(tokens, cotangent):
+    quad = jax.ShapeDtypeStruct((WIN * WIN // 2, tokens.shape[2]), BF16)
     return pl.pallas_call(
         split_kernel,
         out_shape=[quad] * 4,
@@ -267,7 +257,7 @@
         out_specs=[VMEM] * 4,
         compiler_params=PARAMS,
         name="split",
-    )(field)
+    )(jnp.stack([tokens, cotangent]))
 
 
 def join_kernel(*refs):
@@ -291,8 +281,7 @@
     )(*parts)
 
 
-def exchange(parts, steps):
-    own, part_x, part_y, part_xy = parts
+def exchange(steps):
     nx, ny = lax.axis_size("gx"), lax.axis_size("gy")
     ring_x = [(i, (i + steps) % nx) for i in range(nx)]
     ring_y = [(i, (i + steps) % ny) for i in range(ny)]
@@ -301,12 +290,11 @@
         for i in range(nx)
         for j in range(ny)
     ]
-    return [
-        own,
-        lax.ppermute(part_x, "gx", ring_x),
-        lax.ppermute(part_y, "gy", ring_y),
-        lax.ppermute(part_xy, BOTH, both),
-    ]
+    return (
+        lambda value: lax.ppermute(value, "gx", ring_x),
+        lambda value: lax.ppermute(value, "gy", ring_y),
+        lambda value: lax.ppermute(value, BOTH, both),
+    )
 
 
 def swap(value, bit):
@@ -321,19 +309,23 @@
 ]
 
 
-def sum_everywhere(keep, send):
+def sum_everywhere(keep, send, own, sends):
     mine = keep + swap(send, CORE)
     chunk = mine.shape[0] // 16
     pieces = lax.all_to_all(
         mine.reshape(16, chunk, LANES), BOTH, 0, 0, axis_index_groups=PLANE, tiled=True
     )
+    received = [move(value) for value, move in zip(sends, exchange(1))]
+    received, pieces = lax.optimization_barrier((received, pieces))
+    grad_tokens = join_quarters([own, *received])
     total = jnp.sum(pieces.astype(F32), axis=0).astype(BF16)
-    for bit in (1, 2, 4):
+    for bit in (1, 2, 7):
         total = total + swap(total, bit)
+    grad_tokens, total = lax.optimization_barrier((grad_tokens, total))
     spread = jnp.broadcast_to(total[None], (16, chunk, LANES))
     whole = lax.all_to_all(spread, BOTH, 0, 0, axis_index_groups=PLANE, tiled=True)
     whole = whole.reshape(-1, LANES)
-    return whole, swap(whole, CORE)
+    return whole, swap(whole, CORE), grad_tokens
 
 
 def finish_kernel(core, mine, other, o_qkv, o_proj, o_fc1, o_fc2, o_vec, grads, *, factor):
@@ -359,11 +351,8 @@
 
     for col in range(0, hidden_width, LANES):
         o_fc1[:, col : col + LANES] = take(features)
-    o_fc2[:, :LANES] = take(hidden_width)
-    half = hidden_width // 2
-    rest = take(half)
-    o_fc2[:half, LANES:] = rest[:, : features - LANES]
-    o_fc2[half:, LANES:] = rest[:, features - LANES :]
+    for col in range(0, hidden_width, LANES):
+        o_fc2[:, col : col + LANES] = take(features)
     both = jnp.concatenate([take(features) for _ in range(4 * features // LANES)], axis=1)
     o_qkv[...] = both[:, : 3 * features]
     o_proj[...] = both[:, 3 * features :]
@@ -371,8 +360,8 @@
 
 
 def finish(core, mine, other, shapes, factor):
-    rows = shapes[4] // LANES
-    outs = [jax.ShapeDtypeStruct(shape, F32) for shape in (*shapes[:4], (rows, LANES))]
+    shapes = (*shapes[:3], shapes[3][::-1], (shapes[4] // LANES, LANES))
+    outs = [jax.ShapeDtypeStruct(shape, F32) for shape in shapes]
     return pl.pallas_call(
         partial(finish_kernel, factor=factor),
         out_shape=outs,
@@ -392,15 +381,15 @@
     factor = float(token_count) ** (-0.5)
     core = (lax.axis_index("gx") % 2).astype(jnp.int32).reshape(1)
     vectors = (qkv_b, proj_b, fc1_b, g1, b1, g2, b2)
-    toks = exchange(split_quarters(tokens), -1)
-    cots = exchange(split_quarters(cotangent), -1)
-    prepared = prepare(qkv_w, proj_w, fc1_w, vectors)
-    *quads, keep, send = window_call(core, toks, cots, prepared, (qkv_w, proj_w, fc1_w, fc2_w))
-    grad_tokens = join_quarters(exchange(quads, 1))
-    mine, other = sum_everywhere(keep, send)
+    own, *sends = split_quarters(tokens, cotangent)
+    quads = [own] + [move(value) for value, move in zip(sends, exchange(-1))]
+    own, *sends, keep, send = window_call(
+        core, quads, (fc1_w, fc2_w.T, qkv_w, proj_w), vectors
+    )
+    mine, other, grad_tokens = sum_everywhere(keep, send, own, sends)
     shapes = [w.shape for w in (qkv_w, proj_w, fc1_w, fc2_w)] + [sum(v.size for v in vectors)]
     grads = finish(core, mine, other, shapes, factor)
-    return (grad_tokens, *grads[:4], grads[4].reshape(-1))
+    return (grad_tokens, *grads[:3], grads[3].T, grads[4].reshape(-1))
 
 
 def solution(mesh):

time: 95.3 us -> 83 us (0.87)
  blocking collectives: 24.7 us -> 13 us
  local copies, waits for them, and re-layouts: 8.94 us -> 0.88 us
  starting transfers between devices: 30.1 us -> 34 us
  waiting for transfers between devices: 15.7 us -> 18.5 us
  other arithmetic: 0.23 us -> 2.11 us
    all_to_all x1 -> x0, blocking collectives: 13 us -> none  [sum_everywhere(): lax.all_to_all(mine.reshape(16, chunk, LANES), BOTH, 0, 0, axis_index_gro...]
    unnamed x22, local copies, waits for them, and re-layouts: 7.5 us -> 0.4 us
    all_to_all x0 -> x1, starting transfers between devices: none -> 6.96 us  [sum_everywhere(): lax.all_to_all(mine.reshape(16, chunk, LANES), BOTH, 0, 0, axis_index_gro...]
    ppermute x9 -> x6, waiting for transfers between devices: 4.87 us -> 8.01 us  [the longest x2 2.94 us: exchange(): lax.ppermute(value, 'gx', ring_x)]
    ppermute x9 -> x6, starting transfers between devices: 18.6 us -> 16.5 us  [the longest x2 6.78 us: exchange(): lax.ppermute(value, 'gx', ring_x)]
    broadcast_in_dim x2 -> x1, local copies, waits for them, and re-layouts: 1.38 us -> 0.01 us  [window_call(): jnp.zeros((features, places[3][0] - places[2][0] - places[2][1]), BF16)]
    all_to_all x1, blocking collectives: 11.7 us -> 13 us  [sum_everywhere(): lax.all_to_all(spread, BOTH, 0, 0, axis_index_groups=PLANE, tiled=True)]
    another operation x0 -> x1, other arithmetic: none -> 1.12 us  [split_quarters(): jnp.stack([tokens, cotangent])]
  transfers between devices with their start and end apart: 14 -> 12, of which waited for: 6 -> 10; matrix products, arithmetic and copies ran while one was open for 3% -> 1% of each run, Pallas kernels for 2% -> 1%
where the time goes in v2:
time: 83 us; the launch traced here: 82.7 us
  starting transfers between devices  34 us (41%)
  waiting for transfers between devices  18.5 us (22%)
  Pallas kernels  13.3 us (16%)
  blocking collectives  13 us (16%)
  other arithmetic  2.11 us (3%)
  local copies, waits for them, and re-layouts  0.88 us (1%)
  between operations  0.84 us (1%)
    all_to_all x1, blocking collectives, sum_everywhere(): lax.all_to_all(spread, BOTH, 0, 0, axis_index_groups=PLANE, tiled=True)  13 us
    pallas_call x1, Pallas kernels, window_call(): pl.pallas_call(window_kernel, out_shape=[quad] * 4 + [half] * 2, in_specs...  11.1 us
    ppermute x5, starting transfers between devices, swap(): return lax.ppermute(value, BOTH, [(i, i ^ bit) for i in range(256)])  10.6 us
    ppermute x5, waiting for transfers between devices, swap(): return lax.ppermute(value, BOTH, [(i, i ^ bit) for i in range(256)])  10.2 us
    all_to_all x1, starting transfers between devices, sum_everywhere(): lax.all_to_all(mine.reshape(16, chunk, LANES), BOTH, 0, 0, axis_index_gro...  6.96 us
    ppermute x2, starting transfers between devices, exchange(): lax.ppermute(value, 'gx', ring_x)  6.78 us
    ppermute x2, starting transfers between devices, exchange(): lax.ppermute(value, BOTH, both)  4.91 us
    ppermute x2, starting transfers between devices, exchange(): lax.ppermute(value, 'gy', ring_y)  4.77 us
  transfers between devices with their start and end apart: 12, of which 10 were waited for; matrix products, arithmetic and copies ran while one was open for 1% of the time, Pallas kernels for 1%

profile of v2, /device:TPU:1, one launch (start us, length us, event | category | flops | bytes accessed | tf_op | source)
XLA Modules:
  0.0 82.7 jit_solution(13116126941815113621)
XLA Ops:
  0.7 1.1 %pad_maximum_fusion.fields_ref = bf16[2,8,8,1536]{3,2,1,0:T(8,128)(2,1)S(1)} fusion(bf16[1,8,8,1536]{3,2,1,0:T(8,128)(2,1)} %bitcast.13, bf16[1,8,8,1536]{3,2,1,0:T(8,128)(2,1)} %bitcast.14), kind=kLoop, calls=%fused_computation | loop fusion | flops 196608 | bytes 786432 | tf_op jit(solution)/shard_map/stack | solution.py:260
  1.8 0.0 copy-start
  1.8 0.0 copy-start.3
  1.8 0.1 split.1
  1.9 3.3 %collective-permute-start = (bf16[32,1536]{1,0:T(8,128)(2,1)S(1)}, bf16[32,1536]{1,0:T(8,128)(2,1)S(1)}, u32[]{:S(2)}, u32[]{:S(2)}) collective-permute-start(bf16[32,1536]{1,0:T(8,128)(2,1)S(1)} %get-tuple-element.28), channel_id=1, source_target_pairs={{0,240},{16,0},{32,16},{48,32},{64,48},{80,64},{96,80},{112,96},{1... | collective-permute-start | bytes 294920 | tf_op jit(solution)/shard_map/ppermute | solution.py:294
  5.2 4.8 %collective-permute-start.1 = (bf16[32,1536]{1,0:T(8,128)(2,1)S(1)}, bf16[32,1536]{1,0:T(8,128)(2,1)S(1)}, u32[]{:S(2)}, u32[]{:S(2)}) collective-permute-start(bf16[32,1536]{1,0:T(8,128)(2,1)S(1)} %get-tuple-element.29), channel_id=1, source_target_pairs={{0,15},{1,0},{2,1},{3,2},{4,3},{5,4},{6,5},{7,6},{8,7},{9,8},{10,9... | collective-permute-start | bytes 294920 | tf_op jit(solution)/shard_map/ppermute | solution.py:295
  10.0 4.9 %collective-permute-start.2 = (bf16[32,1536]{1,0:T(8,128)(2,1)S(1)}, bf16[32,1536]{1,0:T(8,128)(2,1)S(1)}, u32[]{:S(2)}, u32[]{:S(2)}) collective-permute-start(bf16[32,1536]{1,0:T(8,128)(2,1)S(1)} %get-tuple-element.30), channel_id=1, source_target_pairs={{0,255},{1,240},{2,241},{3,242},{4,243},{5,244},{6,245},{7,246},{8... | collective-permute-start | bytes 294920 | tf_op jit(solution)/shard_map/ppermute | solution.py:296
  15.0 0.0 copy-start.4
  15.0 0.0 copy-start.5
  15.0 0.0 copy-start.6
  15.0 0.0 copy-start.7
  15.0 0.0 copy-start.8
  15.0 0.0 copy-start.9
  15.0 0.0 copy-start.10
  15.1 0.3 concatenate.6.weights
  15.4 0.3 copy-done.4
  15.7 0.0 copy-done.5
  15.7 0.0 copy-done.6
  15.7 0.0 copy-done.7
  15.7 0.0 copy-done.8
  15.7 0.0 copy-done.9
  15.7 0.0 copy-done.10
  15.8 0.1 concatenate.7
  15.8 1.6 %collective-permute-done.2.quad3 = bf16[32,1536]{1,0:T(8,128)(2,1)S(1)} collective-permute-done((bf16[32,1536]{1,0:T(8,128)(2,1)S(1)}, bf16[32,1536]{1,0:T(8,128)(2,1)S(1)}, u32[]{:S(2)}, u32[]{:S(2)}) %collective-permute-start.2) | collective-permute-done | bytes 98336 | tf_op jit(solution)/shard_map/ppermute | solution.py:296
  17.5 11.1 %window.1 = (bf16[16,1536]{1,0:T(8,128)(2,1)S(1)}, bf16[16,1536]{1,0:T(8,128)(2,1)S(1)}, bf16[16,1536]{1,0:T(8,128)(2,1)S(1)}, bf16[16,1536]{1,0:T(8,128)(2,1)S(...) custom-call(s32[1]{0:T(128)} %bitcast.core, bf16[32,1536]{1,0:T(8,128)(2,1)S(1)} %get-tuple-element.27.quad0, ...), custom_call_target="tpu_custom_call" | custom-call | tf_op jit(solution)/shard_map/window/pallas_call | solution.py:227
  28.5 1.1 %collective-permute-start.6 = (bf16[1792,128]{1,0:T(8,128)(2,1)S(1)}, bf16[1792,128]{1,0:T(8,128)(2,1)S(1)}, u32[]{:S(2)}, u32[]{:S(2)}) collective-permute-start(bf16[1792,128]{1,0:T(8,128)(2,1)S(1)} %get-tuple-element.36), channel_id=1, source_target_pairs={{0,16},{1,17},{2,18},{3,19},{4,20},{5,21},{6,22},{7,23},{8,24},{9,... | collective-permute-start | bytes 1376264 | tf_op jit(solution)/shard_map/ppermute | solution.py:301
  29.7 1.4 %collective-permute-done.6 = bf16[1792,128]{1,0:T(8,128)(2,1)S(1)} collective-permute-done((bf16[1792,128]{1,0:T(8,128)(2,1)S(1)}, bf16[1792,128]{1,0:T(8,128)(2,1)S(1)}, u32[]{:S(2)}, u32[]{:S(2)}) %collective-permute-start.6) | collective-permute-done | bytes 458784 | tf_op jit(solution)/shard_map/ppermute | solution.py:301
  31.1 0.9 %add.17 = bf16[1792,128]{1,0:T(8,128)(2,1)} add(bf16[1792,128]{1,0:T(8,128)(2,1)S(1)} %get-tuple-element.35, bf16[1792,128]{1,0:T(8,128)(2,1)S(1)} %collective-permute-done.6) | non-fusion elementwise | flops 229376 | bytes 1376256 | tf_op jit(solution)/shard_map/add | solution.py:313
  32.0 7.0 %all-to-all-start = ((bf16[16,112,128]{2,1,0:T(8,128)(2,1)}), bf16[16,112,128]{2,1,0:T(8,128)(2,1)S(1)}, u32[]{:S(2)}, u32[]{:S(2)}) async-start(bf16[16,112,128]{2,1,0:T(8,128)(2,1)} %bitcast.5), calls=%async_computation | async-start | bytes 917504 | tf_op jit(solution)/shard_map/all_to_all | solution.py:315
  39.0 3.5 %collective-permute-start.3 = (bf16[16,1536]{1,0:T(8,128)(2,1)S(1)}, bf16[16,1536]{1,0:T(8,128)(2,1)S(1)}, u32[]{:S(2)}, u32[]{:S(2)}) collective-permute-start(bf16[16,1536]{1,0:T(8,128)(2,1)S(1)} %get-tuple-element.32), channel_id=1, source_target_pairs={{0,16},{16,32},{32,48},{48,64},{64,80},{80,96},{96,112},{112,128},... | collective-permute-start | bytes 147464 | tf_op jit(solution)/shard_map/ppermute | solution.py:294
  42.4 0.0 collective-permute-start.4
  42.4 2.9 %collective-permute-done.3.refs_1_ = bf16[16,1536]{1,0:T(8,128)(2,1)S(1)} collective-permute-done((bf16[16,1536]{1,0:T(8,128)(2,1)S(1)}, bf16[16,1536]{1,0:T(8,128)(2,1)S(1)}, u32[]{:S(2)}, u32[]{:S(2)}) %collective-permute-start.3) | collective-permute-done | bytes 49184 | tf_op jit(solution)/shard_map/ppermute | solution.py:294
  45.4 2.4 %collective-permute-done.4.refs_2_ = bf16[16,1536]{1,0:T(8,128)(2,1)S(1)} collective-permute-done((bf16[16,1536]{1,0:T(8,128)(2,1)S(1)}, bf16[16,1536]{1,0:T(8,128)(2,1)S(1)}, u32[]{:S(2)}, u32[]{:S(2)}) %collective-permute-start.4) | collective-permute-done | bytes 49184 | tf_op jit(solution)/shard_map/ppermute | solution.py:295
  47.8 1.1 %collective-permute-done.5.refs_3_ = bf16[16,1536]{1,0:T(8,128)(2,1)S(1)} collective-permute-done((bf16[16,1536]{1,0:T(8,128)(2,1)S(1)}, bf16[16,1536]{1,0:T(8,128)(2,1)S(1)}, u32[]{:S(2)}, u32[]{:S(2)}) %collective-permute-start.5) | collective-permute-done | bytes 49184 | tf_op jit(solution)/shard_map/ppermute | solution.py:296
  48.8 0.4 all-to-all-done
  49.2 0.1 reduce_sum.12
  49.3 0.1 collective-permute-start.7
  49.4 3.0 %collective-permute-done.7 = bf16[112,128]{1,0:T(8,128)(2,1)S(1)} collective-permute-done((bf16[112,128]{1,0:T(8,128)(2,1)S(1)}, bf16[112,128]{1,0:T(8,128)(2,1)S(1)}, u32[]{:S(2)}, u32[]{:S(2)}) %collective-permute-start.7) | collective-permute-done | bytes 28704 | tf_op jit(solution)/shard_map/ppermute | solution.py:301
  52.4 0.1 collective-permute-start.8
  52.5 3.6 %collective-permute-done.8 = bf16[112,128]{1,0:T(8,128)(2,1)S(1)} collective-permute-done((bf16[112,128]{1,0:T(8,128)(2,1)S(1)}, bf16[112,128]{1,0:T(8,128)(2,1)S(1)}, u32[]{:S(2)}, u32[]{:S(2)}) %collective-permute-start.8) | collective-permute-done | bytes 28704 | tf_op jit(solution)/shard_map/ppermute | solution.py:301
  56.1 2.6 %collective-permute-start.9 = (bf16[112,128]{1,0:T(8,128)(2,1)S(1)}, bf16[112,128]{1,0:T(8,128)(2,1)S(1)}, u32[]{:S(2)}, u32[]{:S(2)}) collective-permute-start(bf16[112,128]{1,0:T(8,128)(2,1)S(1)} %add.19), channel_id=1, source_target_pairs={{0,7},{1,6},{2,5},{3,4},{4,3},{5,2},{6,1},{7,0},{8,15},{9,14},{10,... | collective-permute-start | bytes 86024 | tf_op jit(solution)/shard_map/ppermute | solution.py:301
  58.8 0.7 join.1
  59.5 0.6 collective-permute-done.9
  60.2 0.1 broadcast_in_dim.10
  60.2 13.0 %all_to_all.10 = bf16[16,112,128]{2,1,0:T(8,128)(2,1)S(1)} all-to-all(bf16[16,112,128]{2,1,0:T(8,128)(2,1)S(1)} %broadcast_in_dim.10), channel_id=1, replica_groups={{0,8,32,40,64,72,96,104,128,136,160,168,192,200,224,232},{1,9,33,41,65,..., dimensions={0} | all-to-all | bytes 917504 | tf_op jit(solution)/shard_map/all_to_all | solution.py:326
  73.3 6.6 %collective-permute-start.10 = (bf16[1792,128]{1,0:T(8,128)(2,1)S(1)}, bf16[1792,128]{1,0:T(8,128)(2,1)S(1)}, u32[]{:S(2)}, u32[]{:S(2)}) collective-permute-start(bf16[1792,128]{1,0:T(8,128)(2,1)S(1)} %bitcast.9), channel_id=1, source_target_pairs={{0,16},{1,17},{2,18},{3,19},{4,20},{5,21},{6,22},{7,23},{8,24},{9,... | collective-permute-start | bytes 1376264 | tf_op jit(solution)/shard_map/ppermute | solution.py:301
  79.9 1.4 %collective-permute-done.10.other = bf16[1792,128]{1,0:T(8,128)(2,1)S(1)} collective-permute-done((bf16[1792,128]{1,0:T(8,128)(2,1)S(1)}, bf16[1792,128]{1,0:T(8,128)(2,1)S(1)}, u32[]{:S(2)}, u32[]{:S(2)}) %collective-permute-start.10) | collective-permute-done | bytes 458784 | tf_op jit(solution)/shard_map/ppermute | solution.py:301
  81.3 1.4 %finish.1 = (f32[192,576]{1,0:T(8,128)}, f32[192,192]{1,0:T(8,128)}, f32[192,768]{1,0:T(8,128)}, f32[192,768]{1,0:T(8,128)}, f32[18,128]{1,0:T(8,128)}) custom-call(s32[1]{0:T(128)} %bitcast.core, bf16[1792,128]{1,0:T(8,128)(2,1)S(1)} %bitcast.10, bf16[1792,128]{1,0:T(8,128)(2,1)S(1)} %collective-permute-done.10.other), custom_call_target="tpu_custom_call" | custom-call | tf_op jit(solution)/shard_map/finish/pallas_call | solution.py:365
  (13 shorter events, 0.1 us)
Async XLA Ops:
  0.6 14.3 %copy-start.1 = (bf16[768,192]{0,1:T(8,128)(2,1)S(1)}, bf16[768,192]{0,1:T(8,128)(2,1)}, u32[]{:S(2)}) copy-start(bf16[768,192]{0,1:T(8,128)(2,1)} %param.21) | copy-start | bytes 884740
  0.6 14.3 %copy-start.2 = (bf16[192,576]{1,0:T(8,128)(2,1)S(1)}, bf16[192,576]{1,0:T(8,128)(2,1)}, u32[]{:S(2)}) copy-start(bf16[192,576]{1,0:T(8,128)(2,1)} %param.15) | copy-start | bytes 663556
  1.8 13.2 %copy-start = (bf16[192,768]{1,0:T(8,128)(2,1)S(1)}, bf16[192,768]{1,0:T(8,128)(2,1)}, u32[]{:S(2)}) copy-start(bf16[192,768]{1,0:T(8,128)(2,1)} %param.19) | copy-start | bytes 884740
  1.8 13.2 %copy-start.3 = (bf16[192,192]{1,0:T(8,128)(2,1)S(1)}, bf16[192,192]{1,0:T(8,128)(2,1)}, u32[]{:S(2)}) copy-start(bf16[192,192]{1,0:T(8,128)(2,1)} %param.17) | copy-start | bytes 221188
  1.9 13.9 %collective-permute-start = (bf16[32,1536]{1,0:T(8,128)(2,1)S(1)}, bf16[32,1536]{1,0:T(8,128)(2,1)S(1)}, u32[]{:S(2)}, u32[]{:S(2)}) collective-permute-start(bf16[32,1536]{1,0:T(8,128)(2,1)S(1)} %get-tuple-element.28), channel_id=1, source_target_pairs={{0,240},{16,0},{32,16},{48,32},{64,48},{80,64},{96,80},{112,96},{1... | collective-permute-start | bytes 294920 | tf_op jit(solution)/shard_map/ppermute | solution.py:294
  5.2 10.6 %collective-permute-start.1 = (bf16[32,1536]{1,0:T(8,128)(2,1)S(1)}, bf16[32,1536]{1,0:T(8,128)(2,1)S(1)}, u32[]{:S(2)}, u32[]{:S(2)}) collective-permute-start(bf16[32,1536]{1,0:T(8,128)(2,1)S(1)} %get-tuple-element.29), channel_id=1, source_target_pairs={{0,15},{1,0},{2,1},{3,2},{4,3},{5,4},{6,5},{7,6},{8,7},{9,8},{10,9... | collective-permute-start | bytes 294920 | tf_op jit(solution)/shard_map/ppermute | solution.py:295
  10.0 7.4 %collective-permute-start.2 = (bf16[32,1536]{1,0:T(8,128)(2,1)S(1)}, bf16[32,1536]{1,0:T(8,128)(2,1)S(1)}, u32[]{:S(2)}, u32[]{:S(2)}) collective-permute-start(bf16[32,1536]{1,0:T(8,128)(2,1)S(1)} %get-tuple-element.30), channel_id=1, source_target_pairs={{0,255},{1,240},{2,241},{3,242},{4,243},{5,244},{6,245},{7,246},{8... | collective-permute-start | bytes 294920 | tf_op jit(solution)/shard_map/ppermute | solution.py:296
  15.0 0.7 copy-start.4
  15.0 0.7 copy-start.5
  15.0 0.7 copy-start.6
  15.0 0.7 copy-start.7
  15.0 0.7 copy-start.8
  15.0 0.7 copy-start.9
  15.0 0.7 copy-start.10
  28.5 2.6 %collective-permute-start.6 = (bf16[1792,128]{1,0:T(8,128)(2,1)S(1)}, bf16[1792,128]{1,0:T(8,128)(2,1)S(1)}, u32[]{:S(2)}, u32[]{:S(2)}) collective-permute-start(bf16[1792,128]{1,0:T(8,128)(2,1)S(1)} %get-tuple-element.36), channel_id=1, source_target_pairs={{0,16},{1,17},{2,18},{3,19},{4,20},{5,21},{6,22},{7,23},{8,24},{9,... | collective-permute-start | bytes 1376264 | tf_op jit(solution)/shard_map/ppermute | solution.py:301
  32.0 17.2 %all-to-all-start = ((bf16[16,112,128]{2,1,0:T(8,128)(2,1)}), bf16[16,112,128]{2,1,0:T(8,128)(2,1)S(1)}, u32[]{:S(2)}, u32[]{:S(2)}) async-start(bf16[16,112,128]{2,1,0:T(8,128)(2,1)} %bitcast.5), calls=%async_computation | async-start | bytes 917504 | tf_op jit(solution)/shard_map/all_to_all | solution.py:315
  39.0 6.4 %collective-permute-start.3 = (bf16[16,1536]{1,0:T(8,128)(2,1)S(1)}, bf16[16,1536]{1,0:T(8,128)(2,1)S(1)}, u32[]{:S(2)}, u32[]{:S(2)}) collective-permute-start(bf16[16,1536]{1,0:T(8,128)(2,1)S(1)} %get-tuple-element.32), channel_id=1, source_target_pairs={{0,16},{16,32},{32,48},{48,64},{64,80},{80,96},{96,112},{112,128},... | collective-permute-start | bytes 147464 | tf_op jit(solution)/shard_map/ppermute | solution.py:294
  42.4 5.3 %collective-permute-start.4 = (bf16[16,1536]{1,0:T(8,128)(2,1)S(1)}, bf16[16,1536]{1,0:T(8,128)(2,1)S(1)}, u32[]{:S(2)}, u32[]{:S(2)}) collective-permute-start(bf16[16,1536]{1,0:T(8,128)(2,1)S(1)} %get-tuple-element.33), channel_id=1, source_target_pairs={{0,1},{1,2},{2,3},{3,4},{4,5},{5,6},{6,7},{7,8},{8,9},{9,10},{10,1... | collective-permute-start | bytes 147464 | tf_op jit(solution)/shard_map/ppermute | solution.py:295
  42.4 6.4 %collective-permute-start.5 = (bf16[16,1536]{1,0:T(8,128)(2,1)S(1)}, bf16[16,1536]{1,0:T(8,128)(2,1)S(1)}, u32[]{:S(2)}, u32[]{:S(2)}) collective-permute-start(bf16[16,1536]{1,0:T(8,128)(2,1)S(1)} %get-tuple-element.34), channel_id=1, source_target_pairs={{0,17},{1,18},{2,19},{3,20},{4,21},{5,22},{6,23},{7,24},{8,25},{9,... | collective-permute-start | bytes 147464 | tf_op jit(solution)/shard_map/ppermute | solution.py:296
  49.3 3.1 %collective-permute-start.7 = (bf16[112,128]{1,0:T(8,128)(2,1)S(1)}, bf16[112,128]{1,0:T(8,128)(2,1)S(1)}, u32[]{:S(2)}, u32[]{:S(2)}) collective-permute-start(bf16[112,128]{1,0:T(8,128)(2,1)S(1)} %reduce_sum.12), channel_id=1, source_target_pairs={{0,1},{1,0},{2,3},{3,2},{4,5},{5,4},{6,7},{7,6},{8,9},{9,8},{10,11... | collective-permute-start | bytes 86024 | tf_op jit(solution)/shard_map/ppermute | solution.py:301
  52.4 3.7 %collective-permute-start.8 = (bf16[112,128]{1,0:T(8,128)(2,1)S(1)}, bf16[112,128]{1,0:T(8,128)(2,1)S(1)}, u32[]{:S(2)}, u32[]{:S(2)}) collective-permute-start(bf16[112,128]{1,0:T(8,128)(2,1)S(1)} %add.18), channel_id=1, source_target_pairs={{0,2},{1,3},{2,0},{3,1},{4,6},{5,7},{6,4},{7,5},{8,10},{9,11},{10,... | collective-permute-start | bytes 86024 | tf_op jit(solution)/shard_map/ppermute | solution.py:301
  56.1 4.0 %collective-permute-start.9 = (bf16[112,128]{1,0:T(8,128)(2,1)S(1)}, bf16[112,128]{1,0:T(8,128)(2,1)S(1)}, u32[]{:S(2)}, u32[]{:S(2)}) collective-permute-start(bf16[112,128]{1,0:T(8,128)(2,1)S(1)} %add.19), channel_id=1, source_target_pairs={{0,7},{1,6},{2,5},{3,4},{4,3},{5,2},{6,1},{7,0},{8,15},{9,14},{10,... | collective-permute-start | bytes 86024 | tf_op jit(solution)/shard_map/ppermute | solution.py:301
  73.3 8.1 %collective-permute-start.10 = (bf16[1792,128]{1,0:T(8,128)(2,1)S(1)}, bf16[1792,128]{1,0:T(8,128)(2,1)S(1)}, u32[]{:S(2)}, u32[]{:S(2)}) collective-permute-start(bf16[1792,128]{1,0:T(8,128)(2,1)S(1)} %bitcast.9), channel_id=1, source_target_pairs={{0,16},{1,17},{2,18},{3,19},{4,20},{5,21},{6,22},{7,23},{8,24},{9,... | collective-permute-start | bytes 1376264 | tf_op jit(solution)/shard_map/ppermute | solution.py:301

commit v3 on v2

--- a/solution.py
+++ b/solution.py
@@ -57,58 +57,59 @@
 
 
 def window_kernel(
-    core, quad0, quad1, quad2, quad3, weights, vectors,
+    core, quad0, quad1, quad2, quad3, weights, turned, columns,
     out0, out1, out2, out3, keep, send,
-    attn_ref, gp_ref, grads,
+    attn_ref, score_ref, gp_ref, grads,
 ):
     features = weights.shape[0]
-    hidden_width = vectors.shape[0] * LANES - 8 * features
+    hidden_width = columns.shape[0] - 8 * features
     head = features // HEADS
     depth = quad0.shape[1] // features
     quads = (quad0, quad1, quad2, quad3)
     scale = head ** (-0.5)
     at = 0
-    fc1_w, fc2_wt, qkv_w, proj_w = [
-        weights[:, low : low + size] for low, size in weight_places(features, hidden_width)
-    ]
-    row = jnp.concatenate([vectors[i : i + 1, :] for i in range(vectors.shape[0])], axis=1)
-    columns = jnp.broadcast_to(row, (8, row.shape[1])).T
+    places = weight_places(features, hidden_width)
+    fc1_w, _, qkv_w, proj_w = [weights[:, low : low + size] for low, size in places]
+    fc1_wt, fc2_w, qkv_wt, proj_wt = [turned[low : low + size, :] for low, size in places]
+    tokens = depth * WIN * WIN
     params = []
     for size in (3 * features, features, hidden_width) + (features,) * 4:
-        params.append(columns[at : at + size, 0:1])
+        params.append(jnp.concatenate([columns[at : at + size, :]] * (tokens // LANES), axis=1))
         at += size
     qkv_b, proj_b, fc1_b, g1, b1, g2, b2 = params
 
     tok_t = gather_window(quads, 0, depth, features).astype(F32).T
     hat1, inv1 = norm_forward(tok_t)
     attn_in = (hat1 * g1 + b1).astype(BF16)
-    projected = dot_tn(qkv_w, attn_in) + qkv_b
+    projected = dot_nn(qkv_wt, attn_in) + qkv_b
     queries = (projected[:features] * scale).astype(BF16)
     keys = projected[features : 2 * features].astype(BF16)
     values = projected[2 * features :].astype(BF16)
-    blended = []
+    ones = jnp.ones((16, values.shape[1]), BF16)
+    blends, inverses = [], []
     for h in range(HEADS):
         rows = slice(h * head, (h + 1) * head)
         scores = dot_tn(keys[rows], queries[rows])
-        top = jnp.max(scores, axis=0, keepdims=True)
-        raised = jnp.exp(scores - top)
-        attention = raised * (1.0 / jnp.sum(raised, axis=0, keepdims=True))
-        attn_ref[h] = attention
-        blended.append(dot_nn(values[rows], attention.astype(BF16)))
-    blended = jnp.concatenate(blended, axis=0).astype(BF16)
-    branch = (dot_tn(proj_w, blended) + proj_b).astype(BF16)
+        attn_ref[h] = jnp.exp(scores - jnp.max(scores, axis=0, keepdims=True)).astype(BF16)
+    for h in range(HEADS):
+        rows = slice(h * head, (h + 1) * head)
+        mixed = dot_nn(jnp.concatenate([values[rows], ones], axis=0), attn_ref[h])
+        inverses.append(1.0 / mixed[head : head + 1])
+        blends.append(mixed[:head] * inverses[h])
+    blended = jnp.concatenate(blends, axis=0).astype(BF16)
+    branch = (dot_nn(proj_wt, blended) + proj_b).astype(BF16)
     residual = tok_t + branch.astype(F32)
     hat2, inv2 = norm_forward(residual)
     mlp_in = (hat2 * g2 + b2).astype(BF16)
 
     cot_t = gather_window(quads, 1, depth, features).astype(F32).T
     cot_b = cot_t.astype(BF16)
-    hidden = dot_tn(fc1_w, mlp_in) + fc1_b
+    hidden = dot_nn(fc1_wt, mlp_in) + fc1_b
     cdf = 0.5 * (1.0 + lax.erf(hidden * 0.7071067811865476))
     pdf = jnp.exp(-0.5 * hidden * hidden) * 0.3989422804014327
     active = (hidden * cdf).astype(BF16)
     fc2_sum = dot_nt(cot_b, active).astype(BF16)
-    grad_pre = dot_tn(fc2_wt, cot_b) * (cdf + hidden * pdf)
+    grad_pre = dot_nn(fc2_w, cot_b) * (cdf + hidden * pdf)
     grad_pre_b = grad_pre.astype(BF16)
     fc1_sum = dot_nt(mlp_in, grad_pre_b).astype(BF16)
     at = 0
@@ -122,19 +123,24 @@
     proj_sum = dot_nt(blended, grad_branch).astype(BF16)
     grad_blend = dot_nn(proj_w, grad_branch).astype(BF16)
 
+    grad_outs = []
     for h in range(HEADS):
         rows = slice(h * head, (h + 1) * head)
-        grad_out = grad_blend[rows]
-        attention = attn_ref[h]
-        grad_attention = dot_tn(values[rows], grad_out)
-        total = jnp.sum(grad_attention * attention, axis=0, keepdims=True)
-        grad_scores = (attention * (grad_attention - total)).astype(BF16)
+        grad_out = (grad_blend[rows].astype(F32) * inverses[h]).astype(BF16)
+        grad_outs.append(grad_out)
+        low = 2 * features + h * head
+        gp_ref[low : low + head, :] = dot_nt(grad_out, attn_ref[h])
+        total = jnp.sum(grad_out.astype(F32) * blends[h], axis=0, keepdims=True)
+        score_ref[h] = (
+            attn_ref[h].astype(F32) * (dot_tn(values[rows], grad_out) - total)
+        ).astype(BF16)
+    for h in range(HEADS):
+        rows = slice(h * head, (h + 1) * head)
+        grad_scores = score_ref[h]
         low = h * head
         gp_ref[low : low + head, :] = dot_nn(keys[rows], grad_scores) * scale
         low += features
         gp_ref[low : low + head, :] = dot_nt(queries[rows], grad_scores)
-        low += features
-        gp_ref[low : low + head, :] = dot_nt(grad_out, attention.astype(BF16))
     grad_proj_in = gp_ref[...]
     grad_proj_b = grad_proj_in.astype(BF16)
     qkv_sum = dot_nt(attn_in, grad_proj_b).astype(BF16)
@@ -214,29 +220,53 @@
     )
 
 
-def window_call(core, quads, weights, vectors):
+def prepare_kernel(weights, vectors, turned, columns):
+    turned[...] = weights[...].T
+    row = jnp.concatenate([vectors[i : i + 1, :] for i in range(vectors.shape[0])], axis=1)
+    columns[...] = jnp.broadcast_to(row, (LANES, row.shape[1])).T
+
+
+def prepare(weights, vectors):
     features, hidden_width = weights[0].shape
-    tokens = 2 * quads[0].size // features
-    rows = grad_rows(features, hidden_width)
     places = weight_places(features, hidden_width)
     gap = jnp.zeros((features, places[3][0] - places[2][0] - places[2][1]), BF16)
     joined = jnp.concatenate([*weights[:3], gap, weights[3]], axis=1)
     rows_of_vectors = jnp.concatenate(vectors).reshape(-1, LANES)
+    turned, columns = pl.pallas_call(
+        prepare_kernel,
+        out_shape=[
+            jax.ShapeDtypeStruct(joined.shape[::-1], BF16),
+            jax.ShapeDtypeStruct((rows_of_vectors.size, LANES), F32),
+        ],
+        in_specs=[VMEM] * 2,
+        out_specs=[VMEM] * 2,
+        compiler_params=PARAMS,
+        name="prepare",
+    )(joined, rows_of_vectors)
+    return joined, turned, columns
+
+
+def window_call(core, quads, prepared):
+    features = prepared[0].shape[0]
+    hidden_width = prepared[2].shape[0] - 8 * features
+    tokens = 2 * quads[0].size // features
+    rows = grad_rows(features, hidden_width)
     quad = jax.ShapeDtypeStruct((quads[0].shape[0] // 2, quads[0].shape[1]), BF16)
     half = jax.ShapeDtypeStruct((rows // 2, LANES), BF16)
     return pl.pallas_call(
         window_kernel,
         out_shape=[quad] * 4 + [half] * 2,
-        in_specs=[SMEM] + [VMEM] * 6,
+        in_specs=[SMEM] + [VMEM] * 7,
         out_specs=[VMEM] * 6,
         scratch_shapes=[
-            pltpu.VMEM((HEADS, tokens, tokens), F32),
+            pltpu.VMEM((HEADS, tokens, tokens), BF16),
+            pltpu.VMEM((HEADS, tokens, tokens), BF16),
             pltpu.VMEM((3 * features, tokens), F32),
             pltpu.VMEM((rows, LANES), BF16),
         ],
         compiler_params=PARAMS,
         name="window",
-    )(core, *quads, joined, rows_of_vectors)
+    )(core, *quads, *prepared)
 
 
 def split_kernel(fields_ref, *outs):
@@ -383,9 +413,8 @@
     vectors = (qkv_b, proj_b, fc1_b, g1, b1, g2, b2)
     own, *sends = split_quarters(tokens, cotangent)
     quads = [own] + [move(value) for value, move in zip(sends, exchange(-1))]
-    own, *sends, keep, send = window_call(
-        core, quads, (fc1_w, fc2_w.T, qkv_w, proj_w), vectors
-    )
+    prepared = prepare((fc1_w, fc2_w.T, qkv_w, proj_w), vectors)
+    own, *sends, keep, send = window_call(core, quads, prepared)
     mine, other, grad_tokens = sum_everywhere(keep, send, own, sends)
     shapes = [w.shape for w in (qkv_w, proj_w, fc1_w, fc2_w)] + [sum(v.size for v in vectors)]
     grads = finish(core, mine, other, shapes, factor)

time: 83 us -> 80.4 us (0.969)
  Pallas kernels: 13.3 us -> 11.3 us
    pallas_call x1, Pallas kernels: 11.1 us -> 8.39 us  [window_call(): pl.pallas_call(window_kernel, out_shape=[quad] * 4 + [half] * 2, in_specs...]
  transfers between devices with their start and end apart: 12 -> 12, of which waited for: 10 -> 10; matrix products, arithmetic and copies ran while one was open for 1% -> 1% of each run, Pallas kernels for 1% -> 2%
where the time goes in v3:
time: 80.4 us; the launch traced here: 80.2 us
  starting transfers between devices  34 us (42%)
  waiting for transfers between devices  18.2 us (23%)
  blocking collectives  13 us (16%)
  Pallas kernels  11.3 us (14%)
  other arithmetic  2.13 us (3%)
  between operations  0.91 us (1%)
    all_to_all x1, blocking collectives, sum_everywhere(): lax.all_to_all(spread, BOTH, 0, 0, axis_index_groups=PLANE, tiled=True)  13 us
    ppermute x5, starting transfers between devices, swap(): return lax.ppermute(value, BOTH, [(i, i ^ bit) for i in range(256)])  10.6 us
    ppermute x5, waiting for transfers between devices, swap(): return lax.ppermute(value, BOTH, [(i, i ^ bit) for i in range(256)])  10.2 us
    pallas_call x1, Pallas kernels, window_call(): pl.pallas_call(window_kernel, out_shape=[quad] * 4 + [half] * 2, in_specs...  8.39 us
    all_to_all x1, starting transfers between devices, sum_everywhere(): lax.all_to_all(mine.reshape(16, chunk, LANES), BOTH, 0, 0, axis_index_gro...  6.97 us
    ppermute x2, starting transfers between devices, exchange(): lax.ppermute(value, 'gx', ring_x)  6.79 us
    ppermute x2, starting transfers between devices, exchange(): lax.ppermute(value, BOTH, both)  4.91 us
    ppermute x2, starting transfers between devices, exchange(): lax.ppermute(value, 'gy', ring_y)  4.77 us
  transfers between devices with their start and end apart: 12, of which 10 were waited for; matrix products, arithmetic and copies ran while one was open for 1% of the time, Pallas kernels for 2%

profile of v3, /device:TPU:1, one launch (start us, length us, event | category | flops | bytes accessed | tf_op | source)
XLA Modules:
  0.0 80.2 jit_solution(12597701519773521839)
XLA Ops:
  0.6 0.0 copy-start.1
  0.6 0.0 copy-start
  0.7 0.0 copy-start.3
  0.7 0.0 copy-start.2
  0.7 1.1 %pad_maximum_fusion.fields_ref = bf16[2,8,8,1536]{3,2,1,0:T(8,128)(2,1)S(1)} fusion(bf16[1,8,8,1536]{3,2,1,0:T(8,128)(2,1)} %bitcast.13, bf16[1,8,8,1536]{3,2,1,0:T(8,128)(2,1)} %bitcast.14), kind=kLoop, calls=%fused_computation | loop fusion | flops 196608 | bytes 786432 | tf_op jit(solution)/shard_map/stack | solution.py:290
  1.8 0.0 copy-start.4
  1.8 0.0 copy-start.5
  1.8 0.0 copy-start.6
  1.8 0.0 copy-start.7
  1.9 0.0 copy-start.8
  1.9 0.0 copy-start.9
  1.9 0.0 copy-start.10
  1.9 0.1 split.1
  2.0 3.3 %collective-permute-start = (bf16[32,1536]{1,0:T(8,128)(2,1)S(1)}, bf16[32,1536]{1,0:T(8,128)(2,1)S(1)}, u32[]{:S(2)}, u32[]{:S(2)}) collective-permute-start(bf16[32,1536]{1,0:T(8,128)(2,1)S(1)} %get-tuple-element.30), channel_id=1, source_target_pairs={{0,240},{16,0},{32,16},{48,32},{64,48},{80,64},{96,80},{112,96},{1... | collective-permute-start | bytes 294920 | tf_op jit(solution)/shard_map/ppermute | solution.py:324
  5.3 4.8 %collective-permute-start.1 = (bf16[32,1536]{1,0:T(8,128)(2,1)S(1)}, bf16[32,1536]{1,0:T(8,128)(2,1)S(1)}, u32[]{:S(2)}, u32[]{:S(2)}) collective-permute-start(bf16[32,1536]{1,0:T(8,128)(2,1)S(1)} %get-tuple-element.31), channel_id=1, source_target_pairs={{0,15},{1,0},{2,1},{3,2},{4,3},{5,4},{6,5},{7,6},{8,7},{9,8},{10,9... | collective-permute-start | bytes 294920 | tf_op jit(solution)/shard_map/ppermute | solution.py:325
  10.1 4.9 %collective-permute-start.2 = (bf16[32,1536]{1,0:T(8,128)(2,1)S(1)}, bf16[32,1536]{1,0:T(8,128)(2,1)S(1)}, u32[]{:S(2)}, u32[]{:S(2)}) collective-permute-start(bf16[32,1536]{1,0:T(8,128)(2,1)S(1)} %get-tuple-element.32), channel_id=1, source_target_pairs={{0,255},{1,240},{2,241},{3,242},{4,243},{5,244},{6,245},{7,246},{8... | collective-permute-start | bytes 294920 | tf_op jit(solution)/shard_map/ppermute | solution.py:326
  15.0 0.0 copy-done.1
  15.1 0.3 concatenate.6.weights
  15.5 0.1 concatenate.7
  15.6 0.7 prepare.1
  16.3 0.0 collective-permute-done.quad1
  16.3 0.0 collective-permute-done.1.quad2
  16.3 1.3 %collective-permute-done.2.quad3 = bf16[32,1536]{1,0:T(8,128)(2,1)S(1)} collective-permute-done((bf16[32,1536]{1,0:T(8,128)(2,1)S(1)}, bf16[32,1536]{1,0:T(8,128)(2,1)S(1)}, u32[]{:S(2)}, u32[]{:S(2)}) %collective-permute-start.2) | collective-permute-done | bytes 98336 | tf_op jit(solution)/shard_map/ppermute | solution.py:326
  17.6 8.4 %window.1 = (bf16[16,1536]{1,0:T(8,128)(2,1)S(1)}, bf16[16,1536]{1,0:T(8,128)(2,1)S(1)}, bf16[16,1536]{1,0:T(8,128)(2,1)S(1)}, bf16[16,1536]{1,0:T(8,128)(2,1)S(...) custom-call(s32[1]{0:T(128)} %bitcast.core, bf16[32,1536]{1,0:T(8,128)(2,1)S(1)} %get-tuple-element.29.quad0, ...), custom_call_target="tpu_custom_call" | custom-call | tf_op jit(solution)/shard_map/window/pallas_call | solution.py:256
  26.0 1.1 %collective-permute-start.6 = (bf16[1792,128]{1,0:T(8,128)(2,1)S(1)}, bf16[1792,128]{1,0:T(8,128)(2,1)S(1)}, u32[]{:S(2)}, u32[]{:S(2)}) collective-permute-start(bf16[1792,128]{1,0:T(8,128)(2,1)S(1)} %get-tuple-element.40), channel_id=1, source_target_pairs={{0,16},{1,17},{2,18},{3,19},{4,20},{5,21},{6,22},{7,23},{8,24},{9,... | collective-permute-start | bytes 1376264 | tf_op jit(solution)/shard_map/ppermute | solution.py:331
  27.1 1.4 %collective-permute-done.6 = bf16[1792,128]{1,0:T(8,128)(2,1)S(1)} collective-permute-done((bf16[1792,128]{1,0:T(8,128)(2,1)S(1)}, bf16[1792,128]{1,0:T(8,128)(2,1)S(1)}, u32[]{:S(2)}, u32[]{:S(2)}) %collective-permute-start.6) | collective-permute-done | bytes 458784 | tf_op jit(solution)/shard_map/ppermute | solution.py:331
  28.5 0.9 %add.17 = bf16[1792,128]{1,0:T(8,128)(2,1)} add(bf16[1792,128]{1,0:T(8,128)(2,1)S(1)} %get-tuple-element.39, bf16[1792,128]{1,0:T(8,128)(2,1)S(1)} %collective-permute-done.6) | non-fusion elementwise | flops 229376 | bytes 1376256 | tf_op jit(solution)/shard_map/add | solution.py:343
  29.4 7.0 %all-to-all-start = ((bf16[16,112,128]{2,1,0:T(8,128)(2,1)}), bf16[16,112,128]{2,1,0:T(8,128)(2,1)S(1)}, u32[]{:S(2)}, u32[]{:S(2)}) async-start(bf16[16,112,128]{2,1,0:T(8,128)(2,1)} %bitcast.5), calls=%async_computation | async-start | bytes 917504 | tf_op jit(solution)/shard_map/all_to_all | solution.py:345
  36.4 3.5 %collective-permute-start.3 = (bf16[16,1536]{1,0:T(8,128)(2,1)S(1)}, bf16[16,1536]{1,0:T(8,128)(2,1)S(1)}, u32[]{:S(2)}, u32[]{:S(2)}) collective-permute-start(bf16[16,1536]{1,0:T(8,128)(2,1)S(1)} %get-tuple-element.36), channel_id=1, source_target_pairs={{0,16},{16,32},{32,48},{48,64},{64,80},{80,96},{96,112},{112,128},... | collective-permute-start | bytes 147464 | tf_op jit(solution)/shard_map/ppermute | solution.py:324
  39.9 0.0 collective-permute-start.4
  39.9 0.0 collective-permute-start.5
  39.9 2.9 %collective-permute-done.3.refs_1_ = bf16[16,1536]{1,0:T(8,128)(2,1)S(1)} collective-permute-done((bf16[16,1536]{1,0:T(8,128)(2,1)S(1)}, bf16[16,1536]{1,0:T(8,128)(2,1)S(1)}, u32[]{:S(2)}, u32[]{:S(2)}) %collective-permute-start.3) | collective-permute-done | bytes 49184 | tf_op jit(solution)/shard_map/ppermute | solution.py:324
  42.8 2.4 %collective-permute-done.4.refs_2_ = bf16[16,1536]{1,0:T(8,128)(2,1)S(1)} collective-permute-done((bf16[16,1536]{1,0:T(8,128)(2,1)S(1)}, bf16[16,1536]{1,0:T(8,128)(2,1)S(1)}, u32[]{:S(2)}, u32[]{:S(2)}) %collective-permute-start.4) | collective-permute-done | bytes 49184 | tf_op jit(solution)/shard_map/ppermute | solution.py:325
  45.2 1.1 %collective-permute-done.5.refs_3_ = bf16[16,1536]{1,0:T(8,128)(2,1)S(1)} collective-permute-done((bf16[16,1536]{1,0:T(8,128)(2,1)S(1)}, bf16[16,1536]{1,0:T(8,128)(2,1)S(1)}, u32[]{:S(2)}, u32[]{:S(2)}) %collective-permute-start.5) | collective-permute-done | bytes 49184 | tf_op jit(solution)/shard_map/ppermute | solution.py:326
  46.3 0.4 all-to-all-done
  46.6 0.1 reduce_sum.12
  46.7 0.1 collective-permute-start.7
  46.8 3.0 %collective-permute-done.7 = bf16[112,128]{1,0:T(8,128)(2,1)S(1)} collective-permute-done((bf16[112,128]{1,0:T(8,128)(2,1)S(1)}, bf16[112,128]{1,0:T(8,128)(2,1)S(1)}, u32[]{:S(2)}, u32[]{:S(2)}) %collective-permute-start.7) | collective-permute-done | bytes 28704 | tf_op jit(solution)/shard_map/ppermute | solution.py:331
  49.8 0.1 collective-permute-start.8
  49.9 3.6 %collective-permute-done.8 = bf16[112,128]{1,0:T(8,128)(2,1)S(1)} collective-permute-done((bf16[112,128]{1,0:T(8,128)(2,1)S(1)}, bf16[112,128]{1,0:T(8,128)(2,1)S(1)}, u32[]{:S(2)}, u32[]{:S(2)}) %collective-permute-start.8) | collective-permute-done | bytes 28704 | tf_op jit(solution)/shard_map/ppermute | solution.py:331
  53.6 2.6 %collective-permute-start.9 = (bf16[112,128]{1,0:T(8,128)(2,1)S(1)}, bf16[112,128]{1,0:T(8,128)(2,1)S(1)}, u32[]{:S(2)}, u32[]{:S(2)}) collective-permute-start(bf16[112,128]{1,0:T(8,128)(2,1)S(1)} %add.19), channel_id=1, source_target_pairs={{0,7},{1,6},{2,5},{3,4},{4,3},{5,2},{6,1},{7,0},{8,15},{9,14},{10,... | collective-permute-start | bytes 86024 | tf_op jit(solution)/shard_map/ppermute | solution.py:331
  56.2 0.7 join.1
  56.9 0.6 collective-permute-done.9
  57.6 0.1 broadcast_in_dim.10
  57.7 13.0 %all_to_all.10 = bf16[16,112,128]{2,1,0:T(8,128)(2,1)S(1)} all-to-all(bf16[16,112,128]{2,1,0:T(8,128)(2,1)S(1)} %broadcast_in_dim.10), channel_id=1, replica_groups={{0,8,32,40,64,72,96,104,128,136,160,168,192,200,224,232},{1,9,33,41,65,..., dimensions={0} | all-to-all | bytes 917504 | tf_op jit(solution)/shard_map/all_to_all | solution.py:356
  70.7 6.6 %collective-permute-start.10 = (bf16[1792,128]{1,0:T(8,128)(2,1)S(1)}, bf16[1792,128]{1,0:T(8,128)(2,1)S(1)}, u32[]{:S(2)}, u32[]{:S(2)}) collective-permute-start(bf16[1792,128]{1,0:T(8,128)(2,1)S(1)} %bitcast.9), channel_id=1, source_target_pairs={{0,16},{1,17},{2,18},{3,19},{4,20},{5,21},{6,22},{7,23},{8,24},{9,... | collective-permute-start | bytes 1376264 | tf_op jit(solution)/shard_map/ppermute | solution.py:331
  77.3 1.4 %collective-permute-done.10.other = bf16[1792,128]{1,0:T(8,128)(2,1)S(1)} collective-permute-done((bf16[1792,128]{1,0:T(8,128)(2,1)S(1)}, bf16[1792,128]{1,0:T(8,128)(2,1)S(1)}, u32[]{:S(2)}, u32[]{:S(2)}) %collective-permute-start.10) | collective-permute-done | bytes 458784 | tf_op jit(solution)/shard_map/ppermute | solution.py:331
  78.8 1.4 %finish.1 = (f32[192,576]{1,0:T(8,128)}, f32[192,192]{1,0:T(8,128)}, f32[192,768]{1,0:T(8,128)}, f32[192,768]{1,0:T(8,128)}, f32[18,128]{1,0:T(8,128)}) custom-call(s32[1]{0:T(128)} %bitcast.core, bf16[1792,128]{1,0:T(8,128)(2,1)S(1)} %bitcast.10, bf16[1792,128]{1,0:T(8,128)(2,1)S(1)} %collective-permute-done.10.other), custom_call_target="tpu_custom_call" | custom-call | tf_op jit(solution)/shard_map/finish/pallas_call | solution.py:395
  (14 shorter events, 0.1 us)
Async XLA Ops:
  0.6 14.4 %copy-start.1 = (bf16[768,192]{0,1:T(8,128)(2,1)S(1)}, bf16[768,192]{0,1:T(8,128)(2,1)}, u32[]{:S(2)}) copy-start(bf16[768,192]{0,1:T(8,128)(2,1)} %param.21) | copy-start | bytes 884740
  0.6 14.4 %copy-start = (bf16[192,768]{1,0:T(8,128)(2,1)S(1)}, bf16[192,768]{1,0:T(8,128)(2,1)}, u32[]{:S(2)}) copy-start(bf16[192,768]{1,0:T(8,128)(2,1)} %param.19) | copy-start | bytes 884740
  0.7 14.4 %copy-start.3 = (bf16[192,192]{1,0:T(8,128)(2,1)S(1)}, bf16[192,192]{1,0:T(8,128)(2,1)}, u32[]{:S(2)}) copy-start(bf16[192,192]{1,0:T(8,128)(2,1)} %param.17) | copy-start | bytes 221188
  0.7 14.4 %copy-start.2 = (bf16[192,576]{1,0:T(8,128)(2,1)S(1)}, bf16[192,576]{1,0:T(8,128)(2,1)}, u32[]{:S(2)}) copy-start(bf16[192,576]{1,0:T(8,128)(2,1)} %param.15) | copy-start | bytes 663556
  1.8 13.6 %copy-start.4 = (f32[576]{0:T(1024)S(1)}, f32[576]{0:T(1024)}, u32[]{:S(2)}) copy-start(f32[576]{0:T(1024)} %param.16) | copy-start | bytes 6916
  1.8 13.6 %copy-start.5 = (f32[768]{0:T(1024)S(1)}, f32[768]{0:T(1024)}, u32[]{:S(2)}) copy-start(f32[768]{0:T(1024)} %param.20) | copy-start | bytes 9220
  1.8 13.6 %copy-start.6 = (f32[192]{0:T(256)S(1)}, f32[192]{0:T(256)}, u32[]{:S(2)}) copy-start(f32[192]{0:T(256)} %param.18) | copy-start | bytes 2308
  1.8 13.6 %copy-start.7 = (f32[192]{0:T(256)S(1)}, f32[192]{0:T(256)}, u32[]{:S(2)}) copy-start(f32[192]{0:T(256)} %param.22) | copy-start | bytes 2308
  1.9 13.6 %copy-start.8 = (f32[192]{0:T(256)S(1)}, f32[192]{0:T(256)}, u32[]{:S(2)}) copy-start(f32[192]{0:T(256)} %param.23) | copy-start | bytes 2308
  1.9 13.6 %copy-start.9 = (f32[192]{0:T(256)S(1)}, f32[192]{0:T(256)}, u32[]{:S(2)}) copy-start(f32[192]{0:T(256)} %param.24) | copy-start | bytes 2308
  1.9 13.6 %copy-start.10 = (f32[192]{0:T(256)S(1)}, f32[192]{0:T(256)}, u32[]{:S(2)}) copy-start(f32[192]{0:T(256)} %param.25) | copy-start | bytes 2308
  2.0 14.2 %collective-permute-start = (bf16[32,1536]{1,0:T(8,128)(2,1)S(1)}, bf16[32,1536]{1,0:T(8,128)(2,1)S(1)}, u32[]{:S(2)}, u32[]{:S(2)}) collective-permute-start(bf16[32,1536]{1,0:T(8,128)(2,1)S(1)} %get-tuple-element.30), channel_id=1, source_target_pairs={{0,240},{16,0},{32,16},{48,32},{64,48},{80,64},{96,80},{112,96},{1... | collective-permute-start | bytes 294920 | tf_op jit(solution)/shard_map/ppermute | solution.py:324
  5.3 10.9 %collective-permute-start.1 = (bf16[32,1536]{1,0:T(8,128)(2,1)S(1)}, bf16[32,1536]{1,0:T(8,128)(2,1)S(1)}, u32[]{:S(2)}, u32[]{:S(2)}) collective-permute-start(bf16[32,1536]{1,0:T(8,128)(2,1)S(1)} %get-tuple-element.31), channel_id=1, source_target_pairs={{0,15},{1,0},{2,1},{3,2},{4,3},{5,4},{6,5},{7,6},{8,7},{9,8},{10,9... | collective-permute-start | bytes 294920 | tf_op jit(solution)/shard_map/ppermute | solution.py:325
  10.1 7.4 %collective-permute-start.2 = (bf16[32,1536]{1,0:T(8,128)(2,1)S(1)}, bf16[32,1536]{1,0:T(8,128)(2,1)S(1)}, u32[]{:S(2)}, u32[]{:S(2)}) collective-permute-start(bf16[32,1536]{1,0:T(8,128)(2,1)S(1)} %get-tuple-element.32), channel_id=1, source_target_pairs={{0,255},{1,240},{2,241},{3,242},{4,243},{5,244},{6,245},{7,246},{8... | collective-permute-start | bytes 294920 | tf_op jit(solution)/shard_map/ppermute | solution.py:326
  26.0 2.6 %collective-permute-start.6 = (bf16[1792,128]{1,0:T(8,128)(2,1)S(1)}, bf16[1792,128]{1,0:T(8,128)(2,1)S(1)}, u32[]{:S(2)}, u32[]{:S(2)}) collective-permute-start(bf16[1792,128]{1,0:T(8,128)(2,1)S(1)} %get-tuple-element.40), channel_id=1, source_target_pairs={{0,16},{1,17},{2,18},{3,19},{4,20},{5,21},{6,22},{7,23},{8,24},{9,... | collective-permute-start | bytes 1376264 | tf_op jit(solution)/shard_map/ppermute | solution.py:331
  29.4 17.2 %all-to-all-start = ((bf16[16,112,128]{2,1,0:T(8,128)(2,1)}), bf16[16,112,128]{2,1,0:T(8,128)(2,1)S(1)}, u32[]{:S(2)}, u32[]{:S(2)}) async-start(bf16[16,112,128]{2,1,0:T(8,128)(2,1)} %bitcast.5), calls=%async_computation | async-start | bytes 917504 | tf_op jit(solution)/shard_map/all_to_all | solution.py:345
  36.4 6.4 %collective-permute-start.3 = (bf16[16,1536]{1,0:T(8,128)(2,1)S(1)}, bf16[16,1536]{1,0:T(8,128)(2,1)S(1)}, u32[]{:S(2)}, u32[]{:S(2)}) collective-permute-start(bf16[16,1536]{1,0:T(8,128)(2,1)S(1)} %get-tuple-element.36), channel_id=1, source_target_pairs={{0,16},{16,32},{32,48},{48,64},{64,80},{80,96},{96,112},{112,128},... | collective-permute-start | bytes 147464 | tf_op jit(solution)/shard_map/ppermute | solution.py:324
  39.9 5.3 %collective-permute-start.4 = (bf16[16,1536]{1,0:T(8,128)(2,1)S(1)}, bf16[16,1536]{1,0:T(8,128)(2,1)S(1)}, u32[]{:S(2)}, u32[]{:S(2)}) collective-permute-start(bf16[16,1536]{1,0:T(8,128)(2,1)S(1)} %get-tuple-element.37), channel_id=1, source_target_pairs={{0,1},{1,2},{2,3},{3,4},{4,5},{5,6},{6,7},{7,8},{8,9},{9,10},{10,1... | collective-permute-start | bytes 147464 | tf_op jit(solution)/shard_map/ppermute | solution.py:325
  39.9 6.4 %collective-permute-start.5 = (bf16[16,1536]{1,0:T(8,128)(2,1)S(1)}, bf16[16,1536]{1,0:T(8,128)(2,1)S(1)}, u32[]{:S(2)}, u32[]{:S(2)}) collective-permute-start(bf16[16,1536]{1,0:T(8,128)(2,1)S(1)} %get-tuple-element.38), channel_id=1, source_target_pairs={{0,17},{1,18},{2,19},{3,20},{4,21},{5,22},{6,23},{7,24},{8,25},{9,... | collective-permute-start | bytes 147464 | tf_op jit(solution)/shard_map/ppermute | solution.py:326
  46.7 3.1 %collective-permute-start.7 = (bf16[112,128]{1,0:T(8,128)(2,1)S(1)}, bf16[112,128]{1,0:T(8,128)(2,1)S(1)}, u32[]{:S(2)}, u32[]{:S(2)}) collective-permute-start(bf16[112,128]{1,0:T(8,128)(2,1)S(1)} %reduce_sum.12), channel_id=1, source_target_pairs={{0,1},{1,0},{2,3},{3,2},{4,5},{5,4},{6,7},{7,6},{8,9},{9,8},{10,11... | collective-permute-start | bytes 86024 | tf_op jit(solution)/shard_map/ppermute | solution.py:331
  49.8 3.7 %collective-permute-start.8 = (bf16[112,128]{1,0:T(8,128)(2,1)S(1)}, bf16[112,128]{1,0:T(8,128)(2,1)S(1)}, u32[]{:S(2)}, u32[]{:S(2)}) collective-permute-start(bf16[112,128]{1,0:T(8,128)(2,1)S(1)} %add.18), channel_id=1, source_target_pairs={{0,2},{1,3},{2,0},{3,1},{4,6},{5,7},{6,4},{7,5},{8,10},{9,11},{10,... | collective-permute-start | bytes 86024 | tf_op jit(solution)/shard_map/ppermute | solution.py:331
  53.6 4.0 %collective-permute-start.9 = (bf16[112,128]{1,0:T(8,128)(2,1)S(1)}, bf16[112,128]{1,0:T(8,128)(2,1)S(1)}, u32[]{:S(2)}, u32[]{:S(2)}) collective-permute-start(bf16[112,128]{1,0:T(8,128)(2,1)S(1)} %add.19), channel_id=1, source_target_pairs={{0,7},{1,6},{2,5},{3,4},{4,3},{5,2},{6,1},{7,0},{8,15},{9,14},{10,... | collective-permute-start | bytes 86024 | tf_op jit(solution)/shard_map/ppermute | solution.py:331
  70.7 8.1 %collective-permute-start.10 = (bf16[1792,128]{1,0:T(8,128)(2,1)S(1)}, bf16[1792,128]{1,0:T(8,128)(2,1)S(1)}, u32[]{:S(2)}, u32[]{:S(2)}) collective-permute-start(bf16[1792,128]{1,0:T(8,128)(2,1)S(1)} %bitcast.9), channel_id=1, source_target_pairs={{0,16},{1,17},{2,18},{3,19},{4,20},{5,21},{6,22},{7,23},{8,24},{9,... | collective-permute-start | bytes 1376264 | tf_op jit(solution)/shard_map/ppermute | solution.py:331

commit v4 on v3

--- a/solution.py
+++ b/solution.py
@@ -58,7 +58,7 @@
 
 def window_kernel(
     core, quad0, quad1, quad2, quad3, weights, turned, columns,
-    out0, out1, out2, out3, keep, send,
+    out0, out_x, out_y, keep, send,
     attn_ref, score_ref, gp_ref, grads,
 ):
     features = weights.shape[0]
@@ -78,18 +78,20 @@
         at += size
     qkv_b, proj_b, fc1_b, g1, b1, g2, b2 = params
 
-    tok_t = gather_window(quads, 0, depth, features).astype(F32).T
+    tok_t = gather_window(quads, 0, depth, features).T.astype(F32)
     hat1, inv1 = norm_forward(tok_t)
     attn_in = (hat1 * g1 + b1).astype(BF16)
     projected = dot_nn(qkv_wt, attn_in) + qkv_b
     queries = (projected[:features] * scale).astype(BF16)
     keys = projected[features : 2 * features].astype(BF16)
     values = projected[2 * features :].astype(BF16)
+    keys_t = keys.T
+    values_t = values.T
     ones = jnp.ones((16, values.shape[1]), BF16)
     blends, inverses = [], []
     for h in range(HEADS):
         rows = slice(h * head, (h + 1) * head)
-        scores = dot_tn(keys[rows], queries[rows])
+        scores = dot_nn(keys_t[:, rows], queries[rows])
         attn_ref[h] = jnp.exp(scores - jnp.max(scores, axis=0, keepdims=True)).astype(BF16)
     for h in range(HEADS):
         rows = slice(h * head, (h + 1) * head)
@@ -102,8 +104,8 @@
     hat2, inv2 = norm_forward(residual)
     mlp_in = (hat2 * g2 + b2).astype(BF16)
 
-    cot_t = gather_window(quads, 1, depth, features).astype(F32).T
-    cot_b = cot_t.astype(BF16)
+    cot_b = gather_window(quads, 1, depth, features).T
+    cot_t = cot_b.astype(F32)
     hidden = dot_nn(fc1_wt, mlp_in) + fc1_b
     cdf = 0.5 * (1.0 + lax.erf(hidden * 0.7071067811865476))
     pdf = jnp.exp(-0.5 * hidden * hidden) * 0.3989422804014327
@@ -124,6 +126,14 @@
     grad_blend = dot_nn(proj_w, grad_branch).astype(BF16)
 
     grad_outs = []
+    def finish_head(h):
+        rows = slice(h * head, (h + 1) * head)
+        grad_scores = score_ref[h]
+        low = h * head
+        gp_ref[low : low + head, :] = dot_nn(keys[rows], grad_scores) * scale
+        low += features
+        gp_ref[low : low + head, :] = dot_nt(queries[rows], grad_scores)
+
     for h in range(HEADS):
         rows = slice(h * head, (h + 1) * head)
         grad_out = (grad_blend[rows].astype(F32) * inverses[h]).astype(BF16)
@@ -132,15 +142,11 @@
         gp_ref[low : low + head, :] = dot_nt(grad_out, attn_ref[h])
         total = jnp.sum(grad_out.astype(F32) * blends[h], axis=0, keepdims=True)
         score_ref[h] = (
-            attn_ref[h].astype(F32) * (dot_tn(values[rows], grad_out) - total)
+            attn_ref[h].astype(F32) * (dot_nn(values_t[:, rows], grad_out) - total)
         ).astype(BF16)
-    for h in range(HEADS):
-        rows = slice(h * head, (h + 1) * head)
-        grad_scores = score_ref[h]
-        low = h * head
-        gp_ref[low : low + head, :] = dot_nn(keys[rows], grad_scores) * scale
-        low += features
-        gp_ref[low : low + head, :] = dot_nt(queries[rows], grad_scores)
+        if h:
+            finish_head(h - 1)
+    finish_head(HEADS - 1)
     grad_proj_in = gp_ref[...]
     grad_proj_b = grad_proj_in.astype(BF16)
     qkv_sum = dot_nt(attn_in, grad_proj_b).astype(BF16)
@@ -185,17 +191,22 @@
         keep[...] = grads[size:, :]
         send[...] = grads[:size, :]
 
-    rows_t = grad_tok.T.astype(BF16)
+    rows_t = grad_tok.astype(BF16).T
     places = rows_t.shape[0] // depth
     quarter = places // 4
-    for k, out in enumerate((out0, out1, out2, out3)):
-        out[...] = jnp.concatenate(
+    parts = [
+        jnp.concatenate(
             [
                 rows_t[t * places + k * quarter : t * places + (k + 1) * quarter]
                 for t in range(depth)
             ],
             axis=1,
         )
+        for k in range(4)
+    ]
+    out0[...] = parts[0]
+    out_x[...] = jnp.concatenate([parts[1], parts[3]], axis=0)
+    out_y[...] = parts[2]
 
 
 VMEM = pl.BlockSpec(memory_space=pltpu.VMEM)
@@ -255,9 +266,9 @@
     half = jax.ShapeDtypeStruct((rows // 2, LANES), BF16)
     return pl.pallas_call(
         window_kernel,
-        out_shape=[quad] * 4 + [half] * 2,
+        out_shape=[quad, jax.ShapeDtypeStruct(quads[0].shape, BF16), quad] + [half] * 2,
         in_specs=[SMEM] + [VMEM] * 7,
-        out_specs=[VMEM] * 6,
+        out_specs=[VMEM] * 5,
         scratch_shapes=[
             pltpu.VMEM((HEADS, tokens, tokens), BF16),
             pltpu.VMEM((HEADS, tokens, tokens), BF16),
@@ -292,8 +303,10 @@
 
 def join_kernel(*refs):
     margin = WIN // 2
-    own, part_x, part_y, part_xy = [ref[...].astype(F32) for ref in refs[:4]]
-    out = refs[4]
+    own, from_x, from_y = [ref[...].astype(F32) for ref in refs[:3]]
+    out = refs[3]
+    part_x = from_x[: margin * margin]
+    part_y, part_xy = from_y[: margin * margin], from_y[margin * margin :]
     for i in range(margin):
         rows = slice(i * margin, (i + 1) * margin)
         out[i] = jnp.concatenate([part_xy[rows], part_x[rows]], axis=0).astype(BF16)
@@ -304,7 +317,7 @@
     return pl.pallas_call(
         join_kernel,
         out_shape=jax.ShapeDtypeStruct((WIN, WIN, parts[0].shape[1]), BF16),
-        in_specs=[VMEM] * 4,
+        in_specs=[VMEM] * 3,
         out_specs=VMEM,
         compiler_params=PARAMS,
         name="join",
@@ -333,26 +346,33 @@
 
 CORE = 16
 PLANE = [
-    [16 * (4 * y + 2 * xh + core) + 8 * xl + z for y in range(4) for xh in (0, 1) for xl in (0, 1)]
+    [
+        16 * (4 * y + 2 * xh + core) + 8 * xl + 2 * z + zl
+        for y in range(4)
+        for xh in (0, 1)
+        for xl in (0, 1)
+        for zl in (0, 1)
+    ]
     for core in (0, 1)
-    for z in range(8)
+    for z in range(4)
 ]
 
 
 def sum_everywhere(keep, send, own, sends):
     mine = keep + swap(send, CORE)
-    chunk = mine.shape[0] // 16
+    chunk = mine.shape[0] // 32
     pieces = lax.all_to_all(
-        mine.reshape(16, chunk, LANES), BOTH, 0, 0, axis_index_groups=PLANE, tiled=True
-    )
-    received = [move(value) for value, move in zip(sends, exchange(1))]
-    received, pieces = lax.optimization_barrier((received, pieces))
-    grad_tokens = join_quarters([own, *received])
+        mine.reshape(32, chunk, LANES), BOTH, 0, 0, axis_index_groups=PLANE, tiled=True
+    )
+    hop_x, hop_y, _ = exchange(1)
+    from_x = hop_x(sends[0])
+    from_y = hop_y(jnp.concatenate([sends[1], from_x[own.shape[0] :]], axis=0))
+    grad_tokens = join_quarters([own, from_x, from_y])
     total = jnp.sum(pieces.astype(F32), axis=0).astype(BF16)
-    for bit in (1, 2, 7):
+    for bit in (2, 6):
         total = total + swap(total, bit)
     grad_tokens, total = lax.optimization_barrier((grad_tokens, total))
-    spread = jnp.broadcast_to(total[None], (16, chunk, LANES))
+    spread = jnp.broadcast_to(total[None], (32, chunk, LANES))
     whole = lax.all_to_all(spread, BOTH, 0, 0, axis_index_groups=PLANE, tiled=True)
     whole = whole.reshape(-1, LANES)
     return whole, swap(whole, CORE), grad_tokens

time: 80.4 us -> 78.1 us (0.971)
  waiting for transfers between devices: 18.2 us -> 13.8 us
  starting transfers between devices: 34 us -> 36 us
    ppermute x5 -> x4, waiting for transfers between devices: 10.2 us -> 6.55 us  [swap(): return lax.ppermute(value, BOTH, [(i, i ^ bit) for i in range(256)])]
    all_to_all x1, waiting for transfers between devices: 0.36 us -> 3.19 us  [sum_everywhere(): lax.all_to_all(mine.reshape(32, chunk, LANES), BOTH, 0, 0, axis_index_gro...]
    ppermute x2, waiting for transfers between devices: 2.4 us -> 0.01 us  [exchange(): lax.ppermute(value, 'gy', ring_y)]
    ppermute x2, starting transfers between devices: 4.77 us -> 6.1 us  [exchange(): lax.ppermute(value, 'gy', ring_y)]
    ppermute x2 -> x1, waiting for transfers between devices: 2.33 us -> 1.28 us  [exchange(): lax.ppermute(value, BOTH, both)]
    ppermute x5 -> x4, starting transfers between devices: 10.6 us -> 10.9 us  [swap(): return lax.ppermute(value, BOTH, [(i, i ^ bit) for i in range(256)])]
    ppermute x2 -> x1, starting transfers between devices: 4.91 us -> 4.91 us  [exchange(): lax.ppermute(value, BOTH, both)]
  transfers between devices with their start and end apart: 12 -> 10, of which waited for: 10 -> 7; matrix products, arithmetic and copies ran while one was open for 1% -> 1% of each run, Pallas kernels for 2% -> 2%
where the time goes in v4:
time: 78.1 us; the launch traced here: 77.9 us
  starting transfers between devices  36 us (46%)
  waiting for transfers between devices  13.8 us (18%)
  blocking collectives  13.3 us (17%)
  Pallas kernels  11.2 us (14%)
  other arithmetic  2.12 us (3%)
  between operations  0.89 us (1%)
    all_to_all x1, blocking collectives, sum_everywhere(): lax.all_to_all(spread, BOTH, 0, 0, axis_index_groups=PLANE, tiled=True)  13.3 us
    ppermute x4, starting transfers between devices, swap(): return lax.ppermute(value, BOTH, [(i, i ^ bit) for i in range(256)])  10.9 us
    pallas_call x1, Pallas kernels, window_call(): pl.pallas_call(window_kernel, out_shape=[quad, jax.ShapeDtypeStruct(quads...  8.27 us
    all_to_all x1, starting transfers between devices, sum_everywhere(): lax.all_to_all(mine.reshape(32, chunk, LANES), BOTH, 0, 0, axis_index_gro...  7.25 us
    ppermute x2, starting transfers between devices, exchange(): lax.ppermute(value, 'gx', ring_x)  6.91 us
    ppermute x4, waiting for transfers between devices, swap(): return lax.ppermute(value, BOTH, [(i, i ^ bit) for i in range(256)])  6.55 us
    ppermute x2, starting transfers between devices, exchange(): lax.ppermute(value, 'gy', ring_y)  6.1 us
    ppermute x1, starting transfers between devices, exchange(): lax.ppermute(value, BOTH, both)  4.91 us
  transfers between devices with their start and end apart: 10, of which 7 were waited for; matrix products, arithmetic and copies ran while one was open for 1% of the time, Pallas kernels for 2%

profile of v4, /device:TPU:1, one launch (start us, length us, event | category | flops | bytes accessed | tf_op | source)
XLA Modules:
  0.0 77.9 jit_solution(11941118575911732993)
XLA Ops:
  0.6 0.0 copy-start.1
  0.6 0.0 copy-start
  0.7 0.0 copy-start.3
  0.7 0.0 copy-start.2
  0.7 1.1 %pad_maximum_fusion.fields_ref = bf16[2,8,8,1536]{3,2,1,0:T(8,128)(2,1)S(1)} fusion(bf16[1,8,8,1536]{3,2,1,0:T(8,128)(2,1)} %bitcast.13, bf16[1,8,8,1536]{3,2,1,0:T(8,128)(2,1)} %bitcast.14), kind=kLoop, calls=%fused_computation | loop fusion | flops 196608 | bytes 786432 | tf_op jit(solution)/shard_map/stack | solution.py:301
  1.8 0.0 copy-start.4
  1.8 0.0 copy-start.5
  1.8 0.0 copy-start.6
  1.8 0.0 copy-start.7
  1.9 0.0 copy-start.8
  1.9 0.0 copy-start.9
  1.9 0.0 copy-start.10
  1.9 0.1 split.1
  2.0 3.3 %collective-permute-start = (bf16[32,1536]{1,0:T(8,128)(2,1)S(1)}, bf16[32,1536]{1,0:T(8,128)(2,1)S(1)}, u32[]{:S(2)}, u32[]{:S(2)}) collective-permute-start(bf16[32,1536]{1,0:T(8,128)(2,1)S(1)} %get-tuple-element.25), channel_id=1, source_target_pairs={{0,240},{16,0},{32,16},{48,32},{64,48},{80,64},{96,80},{112,96},{1... | collective-permute-start | bytes 294920 | tf_op jit(solution)/shard_map/ppermute | solution.py:337
  5.3 4.8 %collective-permute-start.1 = (bf16[32,1536]{1,0:T(8,128)(2,1)S(1)}, bf16[32,1536]{1,0:T(8,128)(2,1)S(1)}, u32[]{:S(2)}, u32[]{:S(2)}) collective-permute-start(bf16[32,1536]{1,0:T(8,128)(2,1)S(1)} %get-tuple-element.26), channel_id=1, source_target_pairs={{0,15},{1,0},{2,1},{3,2},{4,3},{5,4},{6,5},{7,6},{8,7},{9,8},{10,9... | collective-permute-start | bytes 294920 | tf_op jit(solution)/shard_map/ppermute | solution.py:338
  10.1 4.9 %collective-permute-start.2 = (bf16[32,1536]{1,0:T(8,128)(2,1)S(1)}, bf16[32,1536]{1,0:T(8,128)(2,1)S(1)}, u32[]{:S(2)}, u32[]{:S(2)}) collective-permute-start(bf16[32,1536]{1,0:T(8,128)(2,1)S(1)} %get-tuple-element.27), channel_id=1, source_target_pairs={{0,255},{1,240},{2,241},{3,242},{4,243},{5,244},{6,245},{7,246},{8... | collective-permute-start | bytes 294920 | tf_op jit(solution)/shard_map/ppermute | solution.py:339
  15.0 0.0 copy-done.1
  15.0 0.0 copy-done
  15.1 0.0 copy-done.3
  15.1 0.0 copy-done.2
  15.1 0.3 concatenate.9.weights
  15.4 0.0 copy-done.4
  15.5 0.1 concatenate.10
  15.6 0.7 prepare.1
  16.3 0.0 collective-permute-done.quad1
  16.3 0.0 collective-permute-done.1.quad2
  16.3 1.3 %collective-permute-done.2.quad3 = bf16[32,1536]{1,0:T(8,128)(2,1)S(1)} collective-permute-done((bf16[32,1536]{1,0:T(8,128)(2,1)S(1)}, bf16[32,1536]{1,0:T(8,128)(2,1)S(1)}, u32[]{:S(2)}, u32[]{:S(2)}) %collective-permute-start.2) | collective-permute-done | bytes 98336 | tf_op jit(solution)/shard_map/ppermute | solution.py:339
  17.6 8.3 %window.1 = (bf16[16,1536]{1,0:T(8,128)(2,1)S(1)}, bf16[32,1536]{1,0:T(8,128)(2,1)S(1)}, bf16[16,1536]{1,0:T(8,128)(2,1)S(1)}, bf16[1792,128]{1,0:T(8,128)(2,1)S(1)}, bf16[1792,128]{1,0:T(8,128)(2,1)S(1)}) custom-call(s32[1]{0:T(128)} %bitcast.core, bf16[32,1536]{1,0:T(8,128)(2,1)S(1)} %get-tuple-element.24.quad0, ...), custom_call_target="tpu_custom_call" | custom-call | tf_op jit(solution)/shard_map/window/pallas_call | solution.py:267
  25.8 1.1 %collective-permute-start.5 = (bf16[1792,128]{1,0:T(8,128)(2,1)S(1)}, bf16[1792,128]{1,0:T(8,128)(2,1)S(1)}, u32[]{:S(2)}, u32[]{:S(2)}) collective-permute-start(bf16[1792,128]{1,0:T(8,128)(2,1)S(1)} %get-tuple-element.34), channel_id=1, source_target_pairs={{0,16},{1,17},{2,18},{3,19},{4,20},{5,21},{6,22},{7,23},{8,24},{9,... | collective-permute-start | bytes 1376264 | tf_op jit(solution)/shard_map/ppermute | solution.py:344
  27.0 1.4 %collective-permute-done.5 = bf16[1792,128]{1,0:T(8,128)(2,1)S(1)} collective-permute-done((bf16[1792,128]{1,0:T(8,128)(2,1)S(1)}, bf16[1792,128]{1,0:T(8,128)(2,1)S(1)}, u32[]{:S(2)}, u32[]{:S(2)}) %collective-permute-start.5) | collective-permute-done | bytes 458784 | tf_op jit(solution)/shard_map/ppermute | solution.py:344
  28.4 0.9 %add.14 = bf16[1792,128]{1,0:T(8,128)(2,1)} add(bf16[1792,128]{1,0:T(8,128)(2,1)S(1)} %get-tuple-element.33, bf16[1792,128]{1,0:T(8,128)(2,1)S(1)} %collective-permute-done.5) | non-fusion elementwise | flops 229376 | bytes 1376256 | tf_op jit(solution)/shard_map/add | solution.py:362
  29.3 7.3 %all-to-all-start = ((bf16[32,56,128]{2,1,0:T(8,128)(2,1)}), bf16[32,56,128]{2,1,0:T(8,128)(2,1)S(1)}, u32[]{:S(2)}, u32[]{:S(2)}) async-start(bf16[32,56,128]{2,1,0:T(8,128)(2,1)} %bitcast.5), calls=%async_computation | async-start | bytes 917504 | tf_op jit(solution)/shard_map/all_to_all | solution.py:364
  36.6 3.6 %collective-permute-start.3 = (bf16[32,1536]{1,0:T(8,128)(2,1)S(1)}, bf16[32,1536]{1,0:T(8,128)(2,1)S(1)}, u32[]{:S(2)}, u32[]{:S(2)}) collective-permute-start(bf16[32,1536]{1,0:T(8,128)(2,1)S(1)} %get-tuple-element.31), channel_id=1, source_target_pairs={{0,16},{16,32},{32,48},{48,64},{64,80},{80,96},{96,112},{112,128},... | collective-permute-start | bytes 294920 | tf_op jit(solution)/shard_map/ppermute | solution.py:337
  40.2 2.8 %collective-permute-done.3.refs_1_ = bf16[32,1536]{1,0:T(8,128)(2,1)S(1)} collective-permute-done((bf16[32,1536]{1,0:T(8,128)(2,1)S(1)}, bf16[32,1536]{1,0:T(8,128)(2,1)S(1)}, u32[]{:S(2)}, u32[]{:S(2)}) %collective-permute-start.3) | collective-permute-done | bytes 98336 | tf_op jit(solution)/shard_map/ppermute | solution.py:337
  42.9 1.3 %collective-permute-start.4 = (bf16[32,1536]{1,0:T(8,128)(2,1)S(1)}, bf16[32,1536]{1,0:T(8,128)(2,1)S(1)}, u32[]{:S(2)}, u32[]{:S(2)}) collective-permute-start(bf16[32,1536]{1,0:T(8,128)(2,1)S(1)} %pad_maximum_fusion.1), channel_id=1, source_target_pairs={{0,1},{1,2},{2,3},{3,4},{4,5},{5,6},{6,7},{7,8},{8,9},{9,10},{10,1... | collective-permute-start | bytes 294920 | tf_op jit(solution)/shard_map/ppermute | solution.py:338
  44.3 3.2 %all-to-all-done = bf16[32,56,128]{2,1,0:T(8,128)(2,1)S(1)} async-done(((bf16[32,56,128]{2,1,0:T(8,128)(2,1)}), bf16[32,56,128]{2,1,0:T(8,128)(2,1)S(1)}, u32[]{:S(2)}, u32[]{:S(2)}) %all-to-all-start) | async-done | bytes 458784 | tf_op jit(solution)/shard_map/all_to_all | solution.py:364
  47.5 0.1 reduce_sum.12
  47.6 0.7 collective-permute-start.6
  48.3 2.8 %collective-permute-done.6 = bf16[56,128]{1,0:T(8,128)(2,1)S(1)} collective-permute-done((bf16[56,128]{1,0:T(8,128)(2,1)S(1)}, bf16[56,128]{1,0:T(8,128)(2,1)S(1)}, u32[]{:S(2)}, u32[]{:S(2)}) %collective-permute-start.6) | collective-permute-done | bytes 14368 | tf_op jit(solution)/shard_map/ppermute | solution.py:344
  51.1 3.3 %collective-permute-start.7 = (bf16[56,128]{1,0:T(8,128)(2,1)S(1)}, bf16[56,128]{1,0:T(8,128)(2,1)S(1)}, u32[]{:S(2)}, u32[]{:S(2)}) collective-permute-start(bf16[56,128]{1,0:T(8,128)(2,1)S(1)} %add.15), channel_id=1, source_target_pairs={{0,6},{1,7},{2,4},{3,5},{4,2},{5,3},{6,0},{7,1},{8,14},{9,15},{10,... | collective-permute-start | bytes 43016 | tf_op jit(solution)/shard_map/ppermute | solution.py:344
  54.4 0.0 collective-permute-done.4.refs_2_
  54.4 0.7 join.1
  55.2 0.8 %collective-permute-done.7 = bf16[56,128]{1,0:T(8,128)(2,1)S(1)} collective-permute-done((bf16[56,128]{1,0:T(8,128)(2,1)S(1)}, bf16[56,128]{1,0:T(8,128)(2,1)S(1)}, u32[]{:S(2)}, u32[]{:S(2)}) %collective-permute-start.7) | collective-permute-done | bytes 14368 | tf_op jit(solution)/shard_map/ppermute | solution.py:344
  56.0 0.1 broadcast_in_dim.10
  56.1 13.3 %all_to_all.10 = bf16[32,56,128]{2,1,0:T(8,128)(2,1)S(1)} all-to-all(bf16[32,56,128]{2,1,0:T(8,128)(2,1)S(1)} %broadcast_in_dim.10), channel_id=1, replica_groups={{0,1,8,9,32,33,40,41,64,65,72,73,96,97,104,105,128,129,136,137,160,161,..., dimensions={0} | all-to-all | bytes 917504 | tf_op jit(solution)/shard_map/all_to_all | solution.py:376
  69.3 5.7 %collective-permute-start.8 = (bf16[1792,128]{1,0:T(8,128)(2,1)S(1)}, bf16[1792,128]{1,0:T(8,128)(2,1)S(1)}, u32[]{:S(2)}, u32[]{:S(2)}) collective-permute-start(bf16[1792,128]{1,0:T(8,128)(2,1)S(1)} %bitcast.9), channel_id=1, source_target_pairs={{0,16},{1,17},{2,18},{3,19},{4,20},{5,21},{6,22},{7,23},{8,24},{9,... | collective-permute-start | bytes 1376264 | tf_op jit(solution)/shard_map/ppermute | solution.py:344
  75.0 1.4 %collective-permute-done.8.other = bf16[1792,128]{1,0:T(8,128)(2,1)S(1)} collective-permute-done((bf16[1792,128]{1,0:T(8,128)(2,1)S(1)}, bf16[1792,128]{1,0:T(8,128)(2,1)S(1)}, u32[]{:S(2)}, u32[]{:S(2)}) %collective-permute-start.8) | collective-permute-done | bytes 458784 | tf_op jit(solution)/shard_map/ppermute | solution.py:344
  76.5 1.4 %finish.1 = (f32[192,576]{1,0:T(8,128)}, f32[192,192]{1,0:T(8,128)}, f32[192,768]{1,0:T(8,128)}, f32[192,768]{1,0:T(8,128)}, f32[18,128]{1,0:T(8,128)}) custom-call(s32[1]{0:T(128)} %bitcast.core, bf16[1792,128]{1,0:T(8,128)(2,1)S(1)} %bitcast.10, bf16[1792,128]{1,0:T(8,128)(2,1)S(1)} %collective-permute-done.8.other), custom_call_target="tpu_custom_call" | custom-call | tf_op jit(solution)/shard_map/finish/pallas_call | solution.py:415
  (11 shorter events, 0.0 us)
Async XLA Ops:
  0.6 14.4 %copy-start.1 = (bf16[768,192]{0,1:T(8,128)(2,1)S(1)}, bf16[768,192]{0,1:T(8,128)(2,1)}, u32[]{:S(2)}) copy-start(bf16[768,192]{0,1:T(8,128)(2,1)} %param.21) | copy-start | bytes 884740
  0.6 14.4 %copy-start = (bf16[192,768]{1,0:T(8,128)(2,1)S(1)}, bf16[192,768]{1,0:T(8,128)(2,1)}, u32[]{:S(2)}) copy-start(bf16[192,768]{1,0:T(8,128)(2,1)} %param.19) | copy-start | bytes 884740
  0.7 14.4 %copy-start.3 = (bf16[192,192]{1,0:T(8,128)(2,1)S(1)}, bf16[192,192]{1,0:T(8,128)(2,1)}, u32[]{:S(2)}) copy-start(bf16[192,192]{1,0:T(8,128)(2,1)} %param.17) | copy-start | bytes 221188
  0.7 14.4 %copy-start.2 = (bf16[192,576]{1,0:T(8,128)(2,1)S(1)}, bf16[192,576]{1,0:T(8,128)(2,1)}, u32[]{:S(2)}) copy-start(bf16[192,576]{1,0:T(8,128)(2,1)} %param.15) | copy-start | bytes 663556
  1.8 13.6 %copy-start.4 = (f32[576]{0:T(1024)S(1)}, f32[576]{0:T(1024)}, u32[]{:S(2)}) copy-start(f32[576]{0:T(1024)} %param.16) | copy-start | bytes 6916
  1.8 13.6 %copy-start.5 = (f32[768]{0:T(1024)S(1)}, f32[768]{0:T(1024)}, u32[]{:S(2)}) copy-start(f32[768]{0:T(1024)} %param.20) | copy-start | bytes 9220
  1.8 13.6 %copy-start.6 = (f32[192]{0:T(256)S(1)}, f32[192]{0:T(256)}, u32[]{:S(2)}) copy-start(f32[192]{0:T(256)} %param.18) | copy-start | bytes 2308
  1.8 13.6 %copy-start.7 = (f32[192]{0:T(256)S(1)}, f32[192]{0:T(256)}, u32[]{:S(2)}) copy-start(f32[192]{0:T(256)} %param.22) | copy-start | bytes 2308
  1.9 13.6 %copy-start.8 = (f32[192]{0:T(256)S(1)}, f32[192]{0:T(256)}, u32[]{:S(2)}) copy-start(f32[192]{0:T(256)} %param.23) | copy-start | bytes 2308
  1.9 13.6 %copy-start.9 = (f32[192]{0:T(256)S(1)}, f32[192]{0:T(256)}, u32[]{:S(2)}) copy-start(f32[192]{0:T(256)} %param.24) | copy-start | bytes 2308
  1.9 13.6 %copy-start.10 = (f32[192]{0:T(256)S(1)}, f32[192]{0:T(256)}, u32[]{:S(2)}) copy-start(f32[192]{0:T(256)} %param.25) | copy-start | bytes 2308
  2.0 14.2 %collective-permute-start = (bf16[32,1536]{1,0:T(8,128)(2,1)S(1)}, bf16[32,1536]{1,0:T(8,128)(2,1)S(1)}, u32[]{:S(2)}, u32[]{:S(2)}) collective-permute-start(bf16[32,1536]{1,0:T(8,128)(2,1)S(1)} %get-tuple-element.25), channel_id=1, source_target_pairs={{0,240},{16,0},{32,16},{48,32},{64,48},{80,64},{96,80},{112,96},{1... | collective-permute-start | bytes 294920 | tf_op jit(solution)/shard_map/ppermute | solution.py:337
  5.3 10.9 %collective-permute-start.1 = (bf16[32,1536]{1,0:T(8,128)(2,1)S(1)}, bf16[32,1536]{1,0:T(8,128)(2,1)S(1)}, u32[]{:S(2)}, u32[]{:S(2)}) collective-permute-start(bf16[32,1536]{1,0:T(8,128)(2,1)S(1)} %get-tuple-element.26), channel_id=1, source_target_pairs={{0,15},{1,0},{2,1},{3,2},{4,3},{5,4},{6,5},{7,6},{8,7},{9,8},{10,9... | collective-permute-start | bytes 294920 | tf_op jit(solution)/shard_map/ppermute | solution.py:338
  10.1 7.4 %collective-permute-start.2 = (bf16[32,1536]{1,0:T(8,128)(2,1)S(1)}, bf16[32,1536]{1,0:T(8,128)(2,1)S(1)}, u32[]{:S(2)}, u32[]{:S(2)}) collective-permute-start(bf16[32,1536]{1,0:T(8,128)(2,1)S(1)} %get-tuple-element.27), channel_id=1, source_target_pairs={{0,255},{1,240},{2,241},{3,242},{4,243},{5,244},{6,245},{7,246},{8... | collective-permute-start | bytes 294920 | tf_op jit(solution)/shard_map/ppermute | solution.py:339
  25.8 2.6 %collective-permute-start.5 = (bf16[1792,128]{1,0:T(8,128)(2,1)S(1)}, bf16[1792,128]{1,0:T(8,128)(2,1)S(1)}, u32[]{:S(2)}, u32[]{:S(2)}) collective-permute-start(bf16[1792,128]{1,0:T(8,128)(2,1)S(1)} %get-tuple-element.34), channel_id=1, source_target_pairs={{0,16},{1,17},{2,18},{3,19},{4,20},{5,21},{6,22},{7,23},{8,24},{9,... | collective-permute-start | bytes 1376264 | tf_op jit(solution)/shard_map/ppermute | solution.py:344
  29.3 18.2 %all-to-all-start = ((bf16[32,56,128]{2,1,0:T(8,128)(2,1)}), bf16[32,56,128]{2,1,0:T(8,128)(2,1)S(1)}, u32[]{:S(2)}, u32[]{:S(2)}) async-start(bf16[32,56,128]{2,1,0:T(8,128)(2,1)} %bitcast.5), calls=%async_computation | async-start | bytes 917504 | tf_op jit(solution)/shard_map/all_to_all | solution.py:364
  36.6 6.4 %collective-permute-start.3 = (bf16[32,1536]{1,0:T(8,128)(2,1)S(1)}, bf16[32,1536]{1,0:T(8,128)(2,1)S(1)}, u32[]{:S(2)}, u32[]{:S(2)}) collective-permute-start(bf16[32,1536]{1,0:T(8,128)(2,1)S(1)} %get-tuple-element.31), channel_id=1, source_target_pairs={{0,16},{16,32},{32,48},{48,64},{64,80},{80,96},{96,112},{112,128},... | collective-permute-start | bytes 294920 | tf_op jit(solution)/shard_map/ppermute | solution.py:337
  42.9 11.5 %collective-permute-start.4 = (bf16[32,1536]{1,0:T(8,128)(2,1)S(1)}, bf16[32,1536]{1,0:T(8,128)(2,1)S(1)}, u32[]{:S(2)}, u32[]{:S(2)}) collective-permute-start(bf16[32,1536]{1,0:T(8,128)(2,1)S(1)} %pad_maximum_fusion.1), channel_id=1, source_target_pairs={{0,1},{1,2},{2,3},{3,4},{4,5},{5,6},{6,7},{7,8},{8,9},{9,10},{10,1... | collective-permute-start | bytes 294920 | tf_op jit(solution)/shard_map/ppermute | solution.py:338
  47.6 3.6 %collective-permute-start.6 = (bf16[56,128]{1,0:T(8,128)(2,1)S(1)}, bf16[56,128]{1,0:T(8,128)(2,1)S(1)}, u32[]{:S(2)}, u32[]{:S(2)}) collective-permute-start(bf16[56,128]{1,0:T(8,128)(2,1)S(1)} %reduce_sum.12), channel_id=1, source_target_pairs={{0,2},{1,3},{2,0},{3,1},{4,6},{5,7},{6,4},{7,5},{8,10},{9,11},{10,... | collective-permute-start | bytes 43016 | tf_op jit(solution)/shard_map/ppermute | solution.py:344
  51.1 4.9 %collective-permute-start.7 = (bf16[56,128]{1,0:T(8,128)(2,1)S(1)}, bf16[56,128]{1,0:T(8,128)(2,1)S(1)}, u32[]{:S(2)}, u32[]{:S(2)}) collective-permute-start(bf16[56,128]{1,0:T(8,128)(2,1)S(1)} %add.15), channel_id=1, source_target_pairs={{0,6},{1,7},{2,4},{3,5},{4,2},{5,3},{6,0},{7,1},{8,14},{9,15},{10,... | collective-permute-start | bytes 43016 | tf_op jit(solution)/shard_map/ppermute | solution.py:344
  69.3 7.2 %collective-permute-start.8 = (bf16[1792,128]{1,0:T(8,128)(2,1)S(1)}, bf16[1792,128]{1,0:T(8,128)(2,1)S(1)}, u32[]{:S(2)}, u32[]{:S(2)}) collective-permute-start(bf16[1792,128]{1,0:T(8,128)(2,1)S(1)} %bitcast.9), channel_id=1, source_target_pairs={{0,16},{1,17},{2,18},{3,19},{4,20},{5,21},{6,22},{7,23},{8,24},{9,... | collective-permute-start | bytes 1376264 | tf_op jit(solution)/shard_map/ppermute | solution.py:344

commit v5 on v4

--- a/solution.py
+++ b/solution.py
@@ -58,7 +58,7 @@
 
 def window_kernel(
     core, quad0, quad1, quad2, quad3, weights, turned, columns,
-    out0, out_x, out_y, keep, send,
+    out0, out1, out2, out3, keep, send,
     attn_ref, score_ref, gp_ref, grads,
 ):
     features = weights.shape[0]
@@ -136,16 +136,17 @@
 
     for h in range(HEADS):
         rows = slice(h * head, (h + 1) * head)
-        grad_out = (grad_blend[rows].astype(F32) * inverses[h]).astype(BF16)
-        grad_outs.append(grad_out)
+        grad_outs.append((grad_blend[rows].astype(F32) * inverses[h]).astype(BF16))
+    for h in range(HEADS):
+        rows = slice(h * head, (h + 1) * head)
+        grad_out = grad_outs[h]
+        grad_attention = dot_nn(values_t[:, rows], grad_out)
+        if h:
+            finish_head(h - 1)
         low = 2 * features + h * head
         gp_ref[low : low + head, :] = dot_nt(grad_out, attn_ref[h])
         total = jnp.sum(grad_out.astype(F32) * blends[h], axis=0, keepdims=True)
-        score_ref[h] = (
-            attn_ref[h].astype(F32) * (dot_nn(values_t[:, rows], grad_out) - total)
-        ).astype(BF16)
-        if h:
-            finish_head(h - 1)
+        score_ref[h] = (attn_ref[h].astype(F32) * (grad_attention - total)).astype(BF16)
     finish_head(HEADS - 1)
     grad_proj_in = gp_ref[...]
     grad_proj_b = grad_proj_in.astype(BF16)
@@ -194,19 +195,14 @@
     rows_t = grad_tok.astype(BF16).T
     places = rows_t.shape[0] // depth
     quarter = places // 4
-    parts = [
-        jnp.concatenate(
+    for k, out in enumerate((out0, out1, out2, out3)):
+        out[...] = jnp.concatenate(
             [
                 rows_t[t * places + k * quarter : t * places + (k + 1) * quarter]
                 for t in range(depth)
             ],
             axis=1,
         )
-        for k in range(4)
-    ]
-    out0[...] = parts[0]
-    out_x[...] = jnp.concatenate([parts[1], parts[3]], axis=0)
-    out_y[...] = parts[2]
 
 
 VMEM = pl.BlockSpec(memory_space=pltpu.VMEM)
@@ -266,9 +262,9 @@
     half = jax.ShapeDtypeStruct((rows // 2, LANES), BF16)
     return pl.pallas_call(
         window_kernel,
-        out_shape=[quad, jax.ShapeDtypeStruct(quads[0].shape, BF16), quad] + [half] * 2,
+        out_shape=[quad] * 4 + [half] * 2,
         in_specs=[SMEM] + [VMEM] * 7,
-        out_specs=[VMEM] * 5,
+        out_specs=[VMEM] * 6,
         scratch_shapes=[
             pltpu.VMEM((HEADS, tokens, tokens), BF16),
             pltpu.VMEM((HEADS, tokens, tokens), BF16),
@@ -303,10 +299,8 @@
 
 def join_kernel(*refs):
     margin = WIN // 2
-    own, from_x, from_y = [ref[...].astype(F32) for ref in refs[:3]]
-    out = refs[3]
-    part_x = from_x[: margin * margin]
-    part_y, part_xy = from_y[: margin * margin], from_y[margin * margin :]
+    own, part_x, part_y, part_xy = [ref[...].astype(F32) for ref in refs[:4]]
+    out = refs[4]
     for i in range(margin):
         rows = slice(i * margin, (i + 1) * margin)
         out[i] = jnp.concatenate([part_xy[rows], part_x[rows]], axis=0).astype(BF16)
@@ -317,7 +311,7 @@
     return pl.pallas_call(
         join_kernel,
         out_shape=jax.ShapeDtypeStruct((WIN, WIN, parts[0].shape[1]), BF16),
-        in_specs=[VMEM] * 3,
+        in_specs=[VMEM] * 4,
         out_specs=VMEM,
         compiler_params=PARAMS,
         name="join",
@@ -364,10 +358,8 @@
     pieces = lax.all_to_all(
         mine.reshape(32, chunk, LANES), BOTH, 0, 0, axis_index_groups=PLANE, tiled=True
     )
-    hop_x, hop_y, _ = exchange(1)
-    from_x = hop_x(sends[0])
-    from_y = hop_y(jnp.concatenate([sends[1], from_x[own.shape[0] :]], axis=0))
-    grad_tokens = join_quarters([own, from_x, from_y])
+    received = [move(value) for value, move in zip(sends, exchange(1))]
+    grad_tokens = join_quarters([own, *received])
     total = jnp.sum(pieces.astype(F32), axis=0).astype(BF16)
     for bit in (2, 6):
         total = total + swap(total, bit)
@@ -378,35 +370,39 @@
     return whole, swap(whole, CORE), grad_tokens
 
 
-def finish_kernel(core, mine, other, o_qkv, o_proj, o_fc1, o_fc2, o_vec, grads, *, factor):
+def finish_kernel(core, mine, other, o_qkv, o_proj, o_fc1, o_fc2, o_vec, *, factor):
+    features, hidden_width = o_fc1.shape
     size = mine.shape[0]
+
+    def unpack(first, second):
+        at = 0
+
+        def take(rows):
+            nonlocal at
+            low, at = at, at + rows
+            if at <= size:
+                value = first[low:at, :]
+            elif low >= size:
+                value = second[low - size : at - size, :]
+            else:
+                value = jnp.concatenate([first[low:, :], second[: at - size, :]], axis=0)
+            return value.astype(F32) * factor
+
+        for out in (o_fc1, o_fc2):
+            for col in range(0, hidden_width, LANES):
+                out[:, col : col + LANES] = take(features)
+        both = jnp.concatenate([take(features) for _ in range(4 * features // LANES)], axis=1)
+        o_qkv[...] = both[:, : 3 * features]
+        o_proj[...] = both[:, 3 * features :]
+        o_vec[...] = take(LANES)[: o_vec.shape[0]]
 
     @pl.when(core[0] == 0)
     def _():
-        grads[:size, :] = mine[...]
-        grads[size:, :] = other[...]
+        unpack(mine, other)
 
     @pl.when(core[0] != 0)
     def _():
-        grads[:size, :] = other[...]
-        grads[size:, :] = mine[...]
-
-    features, hidden_width = o_fc1.shape
-    at = 0
-
-    def take(rows):
-        nonlocal at
-        at += rows
-        return grads[at - rows : at, :].astype(F32) * factor
-
-    for col in range(0, hidden_width, LANES):
-        o_fc1[:, col : col + LANES] = take(features)
-    for col in range(0, hidden_width, LANES):
-        o_fc2[:, col : col + LANES] = take(features)
-    both = jnp.concatenate([take(features) for _ in range(4 * features // LANES)], axis=1)
-    o_qkv[...] = both[:, : 3 * features]
-    o_proj[...] = both[:, 3 * features :]
-    o_vec[...] = take(LANES)[: o_vec.shape[0]]
+        unpack(other, mine)
 
 
 def finish(core, mine, other, shapes, factor):
@@ -417,7 +413,6 @@
         out_shape=outs,
         in_specs=[SMEM, VMEM, VMEM],
         out_specs=[VMEM] * 5,
-        scratch_shapes=[pltpu.VMEM((2 * mine.shape[0], LANES), BF16)],
         compiler_params=PARAMS,
         name="finish",
     )(core, mine, other)

time: 78.1 us -> 77.8 us (level)
    all_to_all x1, waiting for transfers between devices: 3.19 us -> 6.29 us  [sum_everywhere(): lax.all_to_all(mine.reshape(32, chunk, LANES), BOTH, 0, 0, axis_index_gro...]
    ppermute x2, waiting for transfers between devices: 2.78 us -> 0.01 us  [exchange(): lax.ppermute(value, 'gx', ring_x)]
    ppermute x1 -> x2, starting transfers between devices: 4.91 us -> 4.91 us  [exchange(): lax.ppermute(value, BOTH, both)]
  transfers between devices with their start and end apart: 10 -> 11, of which waited for: 7 -> 6; matrix products, arithmetic and copies ran while one was open for 1% -> 1% of each run, Pallas kernels for 2% -> 2%
where the time goes in v5:
time: 77.8 us; the launch traced here: 77.6 us
  starting transfers between devices  35.6 us (46%)
  waiting for transfers between devices  14.3 us (18%)
  blocking collectives  13 us (17%)
  Pallas kernels  11.1 us (14%)
  other arithmetic  2.12 us (3%)
  between operations  0.89 us (1%)
    all_to_all x1, blocking collectives, sum_everywhere(): lax.all_to_all(spread, BOTH, 0, 0, axis_index_groups=PLANE, tiled=True)  13 us
    ppermute x4, starting transfers between devices, swap(): return lax.ppermute(value, BOTH, [(i, i ^ bit) for i in range(256)])  10.6 us
    pallas_call x1, Pallas kernels, window_call(): pl.pallas_call(window_kernel, out_shape=[quad] * 4 + [half] * 2, in_specs...  8.18 us
    all_to_all x1, starting transfers between devices, sum_everywhere(): lax.all_to_all(mine.reshape(32, chunk, LANES), BOTH, 0, 0, axis_index_gro...  7.25 us
    ppermute x2, starting transfers between devices, exchange(): lax.ppermute(value, 'gx', ring_x)  6.91 us
    ppermute x4, waiting for transfers between devices, swap(): return lax.ppermute(value, BOTH, [(i, i ^ bit) for i in range(256)])  6.75 us
    all_to_all x1, waiting for transfers between devices, sum_everywhere(): lax.all_to_all(mine.reshape(32, chunk, LANES), BOTH, 0, 0, axis_index_gro...  6.29 us
    ppermute x2, starting transfers between devices, exchange(): lax.ppermute(value, 'gy', ring_y)  5.95 us
  transfers between devices with their start and end apart: 11, of which 6 were waited for; matrix products, arithmetic and copies ran while one was open for 1% of the time, Pallas kernels for 2%

profile of v5, /device:TPU:1, one launch (start us, length us, event | category | flops | bytes accessed | tf_op | source)
XLA Modules:
  0.0 77.6 jit_solution(1888857955872026717)
XLA Ops:
  0.7 1.1 %pad_maximum_fusion.fields_ref = bf16[2,8,8,1536]{3,2,1,0:T(8,128)(2,1)S(1)} fusion(bf16[1,8,8,1536]{3,2,1,0:T(8,128)(2,1)} %bitcast.13, bf16[1,8,8,1536]{3,2,1,0:T(8,128)(2,1)} %bitcast.14), kind=kLoop, calls=%fused_computation | loop fusion | flops 196608 | bytes 786432 | tf_op jit(solution)/shard_map/stack | solution.py:297
  1.8 0.0 copy-start.4
  1.8 0.0 copy-start.5
  1.8 0.0 copy-start.6
  1.8 0.0 copy-start.7
  1.9 0.0 copy-start.8
  1.9 0.0 copy-start.9
  1.9 0.0 copy-start.10
  1.9 0.1 split.1
  2.0 3.3 %collective-permute-start = (bf16[32,1536]{1,0:T(8,128)(2,1)S(1)}, bf16[32,1536]{1,0:T(8,128)(2,1)S(1)}, u32[]{:S(2)}, u32[]{:S(2)}) collective-permute-start(bf16[32,1536]{1,0:T(8,128)(2,1)S(1)} %get-tuple-element.26), channel_id=1, source_target_pairs={{0,240},{16,0},{32,16},{48,32},{64,48},{80,64},{96,80},{112,96},{1... | collective-permute-start | bytes 294920 | tf_op jit(solution)/shard_map/ppermute | solution.py:331
  5.3 4.8 %collective-permute-start.1 = (bf16[32,1536]{1,0:T(8,128)(2,1)S(1)}, bf16[32,1536]{1,0:T(8,128)(2,1)S(1)}, u32[]{:S(2)}, u32[]{:S(2)}) collective-permute-start(bf16[32,1536]{1,0:T(8,128)(2,1)S(1)} %get-tuple-element.27), channel_id=1, source_target_pairs={{0,15},{1,0},{2,1},{3,2},{4,3},{5,4},{6,5},{7,6},{8,7},{9,8},{10,9... | collective-permute-start | bytes 294920 | tf_op jit(solution)/shard_map/ppermute | solution.py:332
  10.1 4.9 %collective-permute-start.2 = (bf16[32,1536]{1,0:T(8,128)(2,1)S(1)}, bf16[32,1536]{1,0:T(8,128)(2,1)S(1)}, u32[]{:S(2)}, u32[]{:S(2)}) collective-permute-start(bf16[32,1536]{1,0:T(8,128)(2,1)S(1)} %get-tuple-element.28), channel_id=1, source_target_pairs={{0,255},{1,240},{2,241},{3,242},{4,243},{5,244},{6,245},{7,246},{8... | collective-permute-start | bytes 294920 | tf_op jit(solution)/shard_map/ppermute | solution.py:333
  15.1 0.3 concatenate.6.weights
  15.4 0.0 copy-done.4
  15.4 0.0 copy-done.5
  15.4 0.0 copy-done.6
  15.4 0.0 copy-done.7
  15.4 0.0 copy-done.8
  15.5 0.0 copy-done.9
  15.5 0.0 copy-done.10
  15.5 0.1 concatenate.7
  15.6 0.7 prepare.1
  16.3 0.0 collective-permute-done.quad1
  16.3 0.0 collective-permute-done.1.quad2
  16.3 1.3 %collective-permute-done.2.quad3 = bf16[32,1536]{1,0:T(8,128)(2,1)S(1)} collective-permute-done((bf16[32,1536]{1,0:T(8,128)(2,1)S(1)}, bf16[32,1536]{1,0:T(8,128)(2,1)S(1)}, u32[]{:S(2)}, u32[]{:S(2)}) %collective-permute-start.2) | collective-permute-done | bytes 98336 | tf_op jit(solution)/shard_map/ppermute | solution.py:333
  17.6 8.2 %window.1 = (bf16[16,1536]{1,0:T(8,128)(2,1)S(1)}, bf16[16,1536]{1,0:T(8,128)(2,1)S(1)}, bf16[16,1536]{1,0:T(8,128)(2,1)S(1)}, bf16[16,1536]{1,0:T(8,128)(2,1)S(...) custom-call(s32[1]{0:T(128)} %bitcast.core, bf16[32,1536]{1,0:T(8,128)(2,1)S(1)} %get-tuple-element.25.quad0, ...), custom_call_target="tpu_custom_call" | custom-call | tf_op jit(solution)/shard_map/window/pallas_call | solution.py:263
  25.7 1.1 %collective-permute-start.6 = (bf16[1792,128]{1,0:T(8,128)(2,1)S(1)}, bf16[1792,128]{1,0:T(8,128)(2,1)S(1)}, u32[]{:S(2)}, u32[]{:S(2)}) collective-permute-start(bf16[1792,128]{1,0:T(8,128)(2,1)S(1)} %get-tuple-element.36), channel_id=1, source_target_pairs={{0,16},{1,17},{2,18},{3,19},{4,20},{5,21},{6,22},{7,23},{8,24},{9,... | collective-permute-start | bytes 1376264 | tf_op jit(solution)/shard_map/ppermute | solution.py:338
  26.9 1.4 %collective-permute-done.6 = bf16[1792,128]{1,0:T(8,128)(2,1)S(1)} collective-permute-done((bf16[1792,128]{1,0:T(8,128)(2,1)S(1)}, bf16[1792,128]{1,0:T(8,128)(2,1)S(1)}, u32[]{:S(2)}, u32[]{:S(2)}) %collective-permute-start.6) | collective-permute-done | bytes 458784 | tf_op jit(solution)/shard_map/ppermute | solution.py:338
  28.3 0.9 %add.14 = bf16[1792,128]{1,0:T(8,128)(2,1)} add(bf16[1792,128]{1,0:T(8,128)(2,1)S(1)} %get-tuple-element.35, bf16[1792,128]{1,0:T(8,128)(2,1)S(1)} %collective-permute-done.6) | non-fusion elementwise | flops 229376 | bytes 1376256 | tf_op jit(solution)/shard_map/add | solution.py:356
  29.2 7.3 %all-to-all-start = ((bf16[32,56,128]{2,1,0:T(8,128)(2,1)}), bf16[32,56,128]{2,1,0:T(8,128)(2,1)S(1)}, u32[]{:S(2)}, u32[]{:S(2)}) async-start(bf16[32,56,128]{2,1,0:T(8,128)(2,1)} %bitcast.5), calls=%async_computation | async-start | bytes 917504 | tf_op jit(solution)/shard_map/all_to_all | solution.py:358
  36.5 3.6 %collective-permute-start.3 = (bf16[16,1536]{1,0:T(8,128)(2,1)S(1)}, bf16[16,1536]{1,0:T(8,128)(2,1)S(1)}, u32[]{:S(2)}, u32[]{:S(2)}) collective-permute-start(bf16[16,1536]{1,0:T(8,128)(2,1)S(1)} %get-tuple-element.32), channel_id=1, source_target_pairs={{0,16},{16,32},{32,48},{48,64},{64,80},{80,96},{96,112},{112,128},... | collective-permute-start | bytes 147464 | tf_op jit(solution)/shard_map/ppermute | solution.py:331
  40.1 1.2 %collective-permute-start.4 = (bf16[16,1536]{1,0:T(8,128)(2,1)S(1)}, bf16[16,1536]{1,0:T(8,128)(2,1)S(1)}, u32[]{:S(2)}, u32[]{:S(2)}) collective-permute-start(bf16[16,1536]{1,0:T(8,128)(2,1)S(1)} %get-tuple-element.33), channel_id=1, source_target_pairs={{0,1},{1,2},{2,3},{3,4},{4,5},{5,6},{6,7},{7,8},{8,9},{9,10},{10,1... | collective-permute-start | bytes 147464 | tf_op jit(solution)/shard_map/ppermute | solution.py:332
  41.2 0.0 collective-permute-start.5
  41.2 6.3 %all-to-all-done = bf16[32,56,128]{2,1,0:T(8,128)(2,1)S(1)} async-done(((bf16[32,56,128]{2,1,0:T(8,128)(2,1)}), bf16[32,56,128]{2,1,0:T(8,128)(2,1)S(1)}, u32[]{:S(2)}, u32[]{:S(2)}) %all-to-all-start) | async-done | bytes 458784 | tf_op jit(solution)/shard_map/all_to_all | solution.py:358
  47.5 0.1 reduce_sum.12
  47.6 0.6 collective-permute-start.7
  48.2 3.0 %collective-permute-done.7 = bf16[56,128]{1,0:T(8,128)(2,1)S(1)} collective-permute-done((bf16[56,128]{1,0:T(8,128)(2,1)S(1)}, bf16[56,128]{1,0:T(8,128)(2,1)S(1)}, u32[]{:S(2)}, u32[]{:S(2)}) %collective-permute-start.7) | collective-permute-done | bytes 14368 | tf_op jit(solution)/shard_map/ppermute | solution.py:338
  51.2 3.2 %collective-permute-start.8 = (bf16[56,128]{1,0:T(8,128)(2,1)S(1)}, bf16[56,128]{1,0:T(8,128)(2,1)S(1)}, u32[]{:S(2)}, u32[]{:S(2)}) collective-permute-start(bf16[56,128]{1,0:T(8,128)(2,1)S(1)} %add.15), channel_id=1, source_target_pairs={{0,6},{1,7},{2,4},{3,5},{4,2},{5,3},{6,0},{7,1},{8,14},{9,15},{10,... | collective-permute-start | bytes 43016 | tf_op jit(solution)/shard_map/ppermute | solution.py:338
  54.3 0.0 collective-permute-done.3.refs_1_
  54.3 0.0 collective-permute-done.4.refs_2_
  54.3 0.0 collective-permute-done.5.refs_3_
  54.3 0.7 join.1
  55.1 0.9 %collective-permute-done.8 = bf16[56,128]{1,0:T(8,128)(2,1)S(1)} collective-permute-done((bf16[56,128]{1,0:T(8,128)(2,1)S(1)}, bf16[56,128]{1,0:T(8,128)(2,1)S(1)}, u32[]{:S(2)}, u32[]{:S(2)}) %collective-permute-start.8) | collective-permute-done | bytes 14368 | tf_op jit(solution)/shard_map/ppermute | solution.py:338
  56.0 0.1 broadcast_in_dim.10
  56.0 13.0 %all_to_all.10 = bf16[32,56,128]{2,1,0:T(8,128)(2,1)S(1)} all-to-all(bf16[32,56,128]{2,1,0:T(8,128)(2,1)S(1)} %broadcast_in_dim.10), channel_id=1, replica_groups={{0,1,8,9,32,33,40,41,64,65,72,73,96,97,104,105,128,129,136,137,160,161,..., dimensions={0} | all-to-all | bytes 917504 | tf_op jit(solution)/shard_map/all_to_all | solution.py:368
  69.0 5.7 %collective-permute-start.9 = (bf16[1792,128]{1,0:T(8,128)(2,1)S(1)}, bf16[1792,128]{1,0:T(8,128)(2,1)S(1)}, u32[]{:S(2)}, u32[]{:S(2)}) collective-permute-start(bf16[1792,128]{1,0:T(8,128)(2,1)S(1)} %bitcast.9), channel_id=1, source_target_pairs={{0,16},{1,17},{2,18},{3,19},{4,20},{5,21},{6,22},{7,23},{8,24},{9,... | collective-permute-start | bytes 1376264 | tf_op jit(solution)/shard_map/ppermute | solution.py:338
  74.7 1.4 %collective-permute-done.9.other = bf16[1792,128]{1,0:T(8,128)(2,1)S(1)} collective-permute-done((bf16[1792,128]{1,0:T(8,128)(2,1)S(1)}, bf16[1792,128]{1,0:T(8,128)(2,1)S(1)}, u32[]{:S(2)}, u32[]{:S(2)}) %collective-permute-start.9) | collective-permute-done | bytes 458784 | tf_op jit(solution)/shard_map/ppermute | solution.py:338
  76.2 1.4 %finish.1 = (f32[192,576]{1,0:T(8,128)}, f32[192,192]{1,0:T(8,128)}, f32[192,768]{1,0:T(8,128)}, f32[192,768]{1,0:T(8,128)}, f32[18,128]{1,0:T(8,128)}) custom-call(s32[1]{0:T(128)} %bitcast.core, bf16[1792,128]{1,0:T(8,128)(2,1)S(1)} %bitcast.10, bf16[1792,128]{1,0:T(8,128)(2,1)S(1)} %collective-permute-done.9.other), custom_call_target="tpu_custom_call" | custom-call | tf_op jit(solution)/shard_map/finish/pallas_call | solution.py:411
  (11 shorter events, 0.0 us)
Async XLA Ops:
  0.6 14.4 %copy-start.1 = (bf16[768,192]{0,1:T(8,128)(2,1)S(1)}, bf16[768,192]{0,1:T(8,128)(2,1)}, u32[]{:S(2)}) copy-start(bf16[768,192]{0,1:T(8,128)(2,1)} %param.21) | copy-start | bytes 884740
  0.6 14.4 %copy-start = (bf16[192,768]{1,0:T(8,128)(2,1)S(1)}, bf16[192,768]{1,0:T(8,128)(2,1)}, u32[]{:S(2)}) copy-start(bf16[192,768]{1,0:T(8,128)(2,1)} %param.19) | copy-start | bytes 884740
  0.7 14.4 %copy-start.3 = (bf16[192,192]{1,0:T(8,128)(2,1)S(1)}, bf16[192,192]{1,0:T(8,128)(2,1)}, u32[]{:S(2)}) copy-start(bf16[192,192]{1,0:T(8,128)(2,1)} %param.17) | copy-start | bytes 221188
  0.7 14.4 %copy-start.2 = (bf16[192,576]{1,0:T(8,128)(2,1)S(1)}, bf16[192,576]{1,0:T(8,128)(2,1)}, u32[]{:S(2)}) copy-start(bf16[192,576]{1,0:T(8,128)(2,1)} %param.15) | copy-start | bytes 663556
  1.8 13.6 %copy-start.4 = (f32[576]{0:T(1024)S(1)}, f32[576]{0:T(1024)}, u32[]{:S(2)}) copy-start(f32[576]{0:T(1024)} %param.16) | copy-start | bytes 6916
  1.8 13.6 %copy-start.5 = (f32[768]{0:T(1024)S(1)}, f32[768]{0:T(1024)}, u32[]{:S(2)}) copy-start(f32[768]{0:T(1024)} %param.20) | copy-start | bytes 9220
  1.8 13.6 %copy-start.6 = (f32[192]{0:T(256)S(1)}, f32[192]{0:T(256)}, u32[]{:S(2)}) copy-start(f32[192]{0:T(256)} %param.18) | copy-start | bytes 2308
  1.8 13.6 %copy-start.7 = (f32[192]{0:T(256)S(1)}, f32[192]{0:T(256)}, u32[]{:S(2)}) copy-start(f32[192]{0:T(256)} %param.22) | copy-start | bytes 2308
  1.9 13.6 %copy-start.8 = (f32[192]{0:T(256)S(1)}, f32[192]{0:T(256)}, u32[]{:S(2)}) copy-start(f32[192]{0:T(256)} %param.23) | copy-start | bytes 2308
  1.9 13.6 %copy-start.9 = (f32[192]{0:T(256)S(1)}, f32[192]{0:T(256)}, u32[]{:S(2)}) copy-start(f32[192]{0:T(256)} %param.24) | copy-start | bytes 2308
  1.9 13.6 %copy-start.10 = (f32[192]{0:T(256)S(1)}, f32[192]{0:T(256)}, u32[]{:S(2)}) copy-start(f32[192]{0:T(256)} %param.25) | copy-start | bytes 2308
  2.0 14.2 %collective-permute-start = (bf16[32,1536]{1,0:T(8,128)(2,1)S(1)}, bf16[32,1536]{1,0:T(8,128)(2,1)S(1)}, u32[]{:S(2)}, u32[]{:S(2)}) collective-permute-start(bf16[32,1536]{1,0:T(8,128)(2,1)S(1)} %get-tuple-element.26), channel_id=1, source_target_pairs={{0,240},{16,0},{32,16},{48,32},{64,48},{80,64},{96,80},{112,96},{1... | collective-permute-start | bytes 294920 | tf_op jit(solution)/shard_map/ppermute | solution.py:331
  5.3 10.9 %collective-permute-start.1 = (bf16[32,1536]{1,0:T(8,128)(2,1)S(1)}, bf16[32,1536]{1,0:T(8,128)(2,1)S(1)}, u32[]{:S(2)}, u32[]{:S(2)}) collective-permute-start(bf16[32,1536]{1,0:T(8,128)(2,1)S(1)} %get-tuple-element.27), channel_id=1, source_target_pairs={{0,15},{1,0},{2,1},{3,2},{4,3},{5,4},{6,5},{7,6},{8,7},{9,8},{10,9... | collective-permute-start | bytes 294920 | tf_op jit(solution)/shard_map/ppermute | solution.py:332
  10.1 7.4 %collective-permute-start.2 = (bf16[32,1536]{1,0:T(8,128)(2,1)S(1)}, bf16[32,1536]{1,0:T(8,128)(2,1)S(1)}, u32[]{:S(2)}, u32[]{:S(2)}) collective-permute-start(bf16[32,1536]{1,0:T(8,128)(2,1)S(1)} %get-tuple-element.28), channel_id=1, source_target_pairs={{0,255},{1,240},{2,241},{3,242},{4,243},{5,244},{6,245},{7,246},{8... | collective-permute-start | bytes 294920 | tf_op jit(solution)/shard_map/ppermute | solution.py:333
  25.7 2.6 %collective-permute-start.6 = (bf16[1792,128]{1,0:T(8,128)(2,1)S(1)}, bf16[1792,128]{1,0:T(8,128)(2,1)S(1)}, u32[]{:S(2)}, u32[]{:S(2)}) collective-permute-start(bf16[1792,128]{1,0:T(8,128)(2,1)S(1)} %get-tuple-element.36), channel_id=1, source_target_pairs={{0,16},{1,17},{2,18},{3,19},{4,20},{5,21},{6,22},{7,23},{8,24},{9,... | collective-permute-start | bytes 1376264 | tf_op jit(solution)/shard_map/ppermute | solution.py:338
  29.2 18.3 %all-to-all-start = ((bf16[32,56,128]{2,1,0:T(8,128)(2,1)}), bf16[32,56,128]{2,1,0:T(8,128)(2,1)S(1)}, u32[]{:S(2)}, u32[]{:S(2)}) async-start(bf16[32,56,128]{2,1,0:T(8,128)(2,1)} %bitcast.5), calls=%async_computation | async-start | bytes 917504 | tf_op jit(solution)/shard_map/all_to_all | solution.py:358
  36.5 17.9 %collective-permute-start.3 = (bf16[16,1536]{1,0:T(8,128)(2,1)S(1)}, bf16[16,1536]{1,0:T(8,128)(2,1)S(1)}, u32[]{:S(2)}, u32[]{:S(2)}) collective-permute-start(bf16[16,1536]{1,0:T(8,128)(2,1)S(1)} %get-tuple-element.32), channel_id=1, source_target_pairs={{0,16},{16,32},{32,48},{48,64},{64,80},{80,96},{96,112},{112,128},... | collective-permute-start | bytes 147464 | tf_op jit(solution)/shard_map/ppermute | solution.py:331
  40.1 14.3 %collective-permute-start.4 = (bf16[16,1536]{1,0:T(8,128)(2,1)S(1)}, bf16[16,1536]{1,0:T(8,128)(2,1)S(1)}, u32[]{:S(2)}, u32[]{:S(2)}) collective-permute-start(bf16[16,1536]{1,0:T(8,128)(2,1)S(1)} %get-tuple-element.33), channel_id=1, source_target_pairs={{0,1},{1,2},{2,3},{3,4},{4,5},{5,6},{6,7},{7,8},{8,9},{9,10},{10,1... | collective-permute-start | bytes 147464 | tf_op jit(solution)/shard_map/ppermute | solution.py:332
  41.2 13.1 %collective-permute-start.5 = (bf16[16,1536]{1,0:T(8,128)(2,1)S(1)}, bf16[16,1536]{1,0:T(8,128)(2,1)S(1)}, u32[]{:S(2)}, u32[]{:S(2)}) collective-permute-start(bf16[16,1536]{1,0:T(8,128)(2,1)S(1)} %get-tuple-element.34), channel_id=1, source_target_pairs={{0,17},{1,18},{2,19},{3,20},{4,21},{5,22},{6,23},{7,24},{8,25},{9,... | collective-permute-start | bytes 147464 | tf_op jit(solution)/shard_map/ppermute | solution.py:333
  47.6 3.6 %collective-permute-start.7 = (bf16[56,128]{1,0:T(8,128)(2,1)S(1)}, bf16[56,128]{1,0:T(8,128)(2,1)S(1)}, u32[]{:S(2)}, u32[]{:S(2)}) collective-permute-start(bf16[56,128]{1,0:T(8,128)(2,1)S(1)} %reduce_sum.12), channel_id=1, source_target_pairs={{0,2},{1,3},{2,0},{3,1},{4,6},{5,7},{6,4},{7,5},{8,10},{9,11},{10,... | collective-permute-start | bytes 43016 | tf_op jit(solution)/shard_map/ppermute | solution.py:338
  51.2 4.8 %collective-permute-start.8 = (bf16[56,128]{1,0:T(8,128)(2,1)S(1)}, bf16[56,128]{1,0:T(8,128)(2,1)S(1)}, u32[]{:S(2)}, u32[]{:S(2)}) collective-permute-start(bf16[56,128]{1,0:T(8,128)(2,1)S(1)} %add.15), channel_id=1, source_target_pairs={{0,6},{1,7},{2,4},{3,5},{4,2},{5,3},{6,0},{7,1},{8,14},{9,15},{10,... | collective-permute-start | bytes 43016 | tf_op jit(solution)/shard_map/ppermute | solution.py:338
  69.0 7.1 %collective-permute-start.9 = (bf16[1792,128]{1,0:T(8,128)(2,1)S(1)}, bf16[1792,128]{1,0:T(8,128)(2,1)S(1)}, u32[]{:S(2)}, u32[]{:S(2)}) collective-permute-start(bf16[1792,128]{1,0:T(8,128)(2,1)S(1)} %bitcast.9), channel_id=1, source_target_pairs={{0,16},{1,17},{2,18},{3,19},{4,20},{5,21},{6,22},{7,23},{8,24},{9,... | collective-permute-start | bytes 1376264 | tf_op jit(solution)/shard_map/ppermute | solution.py:338

commit v6 on v5

--- a/solution.py
+++ b/solution.py
@@ -342,10 +342,10 @@
 PLANE = [
     [
         16 * (4 * y + 2 * xh + core) + 8 * xl + 2 * z + zl
-        for y in range(4)
+        for zl in (0, 1)
         for xh in (0, 1)
         for xl in (0, 1)
-        for zl in (0, 1)
+        for y in range(4)
     ]
     for core in (0, 1)
     for z in range(4)

time: 77.8 us -> 76.7 us (0.986)
  waiting for transfers between devices: 14.3 us -> 12 us
  starting transfers between devices: 35.6 us -> 37 us
    all_to_all x1, waiting for transfers between devices: 6.29 us -> 4.92 us  [sum_everywhere(): lax.all_to_all(mine.reshape(32, chunk, LANES), BOTH, 0, 0, axis_index_gro...]
    ppermute x4, starting transfers between devices: 10.6 us -> 11.9 us  [swap(): return lax.ppermute(value, BOTH, [(i, i ^ bit) for i in range(256)])]
    ppermute x4, waiting for transfers between devices: 6.75 us -> 5.77 us  [swap(): return lax.ppermute(value, BOTH, [(i, i ^ bit) for i in range(256)])]
where the time goes in v6:
time: 76.7 us; the launch traced here: 76.4 us
  starting transfers between devices  37 us (48%)
  blocking collectives  12.8 us (17%)
  waiting for transfers between devices  12 us (16%)
  Pallas kernels  11.1 us (14%)
  other arithmetic  2.12 us (3%)
  between operations  0.89 us (1%)
    all_to_all x1, blocking collectives, sum_everywhere(): lax.all_to_all(spread, BOTH, 0, 0, axis_index_groups=PLANE, tiled=True)  12.8 us
    ppermute x4, starting transfers between devices, swap(): return lax.ppermute(value, BOTH, [(i, i ^ bit) for i in range(256)])  11.9 us
    pallas_call x1, Pallas kernels, window_call(): pl.pallas_call(window_kernel, out_shape=[quad] * 4 + [half] * 2, in_specs...  8.18 us
    all_to_all x1, starting transfers between devices, sum_everywhere(): lax.all_to_all(mine.reshape(32, chunk, LANES), BOTH, 0, 0, axis_index_gro...  7.25 us
    ppermute x2, starting transfers between devices, exchange(): lax.ppermute(value, 'gx', ring_x)  6.91 us
    ppermute x2, starting transfers between devices, exchange(): lax.ppermute(value, 'gy', ring_y)  5.99 us
    ppermute x4, waiting for transfers between devices, swap(): return lax.ppermute(value, BOTH, [(i, i ^ bit) for i in range(256)])  5.77 us
    all_to_all x1, waiting for transfers between devices, sum_everywhere(): lax.all_to_all(mine.reshape(32, chunk, LANES), BOTH, 0, 0, axis_index_gro...  4.92 us
  transfers between devices with their start and end apart: 11, of which 6 were waited for; matrix products, arithmetic and copies ran while one was open for 1% of the time, Pallas kernels for 2%

profile of v6, /device:TPU:1, one launch (start us, length us, event | category | flops | bytes accessed | tf_op | source)
XLA Modules:
  0.0 76.4 jit_solution(8264601404491291958)
XLA Ops:
  0.6 0.0 copy-start.1
  0.6 0.0 copy-start
  0.7 0.0 copy-start.3
  0.7 0.0 copy-start.2
  0.7 1.1 %pad_maximum_fusion.fields_ref = bf16[2,8,8,1536]{3,2,1,0:T(8,128)(2,1)S(1)} fusion(bf16[1,8,8,1536]{3,2,1,0:T(8,128)(2,1)} %bitcast.13, bf16[1,8,8,1536]{3,2,1,0:T(8,128)(2,1)} %bitcast.14), kind=kLoop, calls=%fused_computation | loop fusion | flops 196608 | bytes 786432 | tf_op jit(solution)/shard_map/stack | solution.py:297
  1.8 0.0 copy-start.4
  1.8 0.0 copy-start.5
  1.8 0.0 copy-start.6
  1.8 0.0 copy-start.7
  1.9 0.0 copy-start.8
  1.9 0.0 copy-start.9
  1.9 0.0 copy-start.10
  1.9 0.1 split.1
  2.0 3.3 %collective-permute-start = (bf16[32,1536]{1,0:T(8,128)(2,1)S(1)}, bf16[32,1536]{1,0:T(8,128)(2,1)S(1)}, u32[]{:S(2)}, u32[]{:S(2)}) collective-permute-start(bf16[32,1536]{1,0:T(8,128)(2,1)S(1)} %get-tuple-element.26), channel_id=1, source_target_pairs={{0,240},{16,0},{32,16},{48,32},{64,48},{80,64},{96,80},{112,96},{1... | collective-permute-start | bytes 294920 | tf_op jit(solution)/shard_map/ppermute | solution.py:331
  5.3 4.8 %collective-permute-start.1 = (bf16[32,1536]{1,0:T(8,128)(2,1)S(1)}, bf16[32,1536]{1,0:T(8,128)(2,1)S(1)}, u32[]{:S(2)}, u32[]{:S(2)}) collective-permute-start(bf16[32,1536]{1,0:T(8,128)(2,1)S(1)} %get-tuple-element.27), channel_id=1, source_target_pairs={{0,15},{1,0},{2,1},{3,2},{4,3},{5,4},{6,5},{7,6},{8,7},{9,8},{10,9... | collective-permute-start | bytes 294920 | tf_op jit(solution)/shard_map/ppermute | solution.py:332
  10.1 4.9 %collective-permute-start.2 = (bf16[32,1536]{1,0:T(8,128)(2,1)S(1)}, bf16[32,1536]{1,0:T(8,128)(2,1)S(1)}, u32[]{:S(2)}, u32[]{:S(2)}) collective-permute-start(bf16[32,1536]{1,0:T(8,128)(2,1)S(1)} %get-tuple-element.28), channel_id=1, source_target_pairs={{0,255},{1,240},{2,241},{3,242},{4,243},{5,244},{6,245},{7,246},{8... | collective-permute-start | bytes 294920 | tf_op jit(solution)/shard_map/ppermute | solution.py:333
  15.0 0.0 copy-done.1
  15.0 0.0 copy-done
  15.1 0.0 copy-done.3
  15.1 0.3 concatenate.6.weights
  15.5 0.1 concatenate.7
  15.6 0.7 prepare.1
  16.3 0.0 collective-permute-done.quad1
  16.3 0.0 collective-permute-done.1.quad2
  16.3 1.3 %collective-permute-done.2.quad3 = bf16[32,1536]{1,0:T(8,128)(2,1)S(1)} collective-permute-done((bf16[32,1536]{1,0:T(8,128)(2,1)S(1)}, bf16[32,1536]{1,0:T(8,128)(2,1)S(1)}, u32[]{:S(2)}, u32[]{:S(2)}) %collective-permute-start.2) | collective-permute-done | bytes 98336 | tf_op jit(solution)/shard_map/ppermute | solution.py:333
  17.6 8.2 %window.1 = (bf16[16,1536]{1,0:T(8,128)(2,1)S(1)}, bf16[16,1536]{1,0:T(8,128)(2,1)S(1)}, bf16[16,1536]{1,0:T(8,128)(2,1)S(1)}, bf16[16,1536]{1,0:T(8,128)(2,1)S(...) custom-call(s32[1]{0:T(128)} %bitcast.core, bf16[32,1536]{1,0:T(8,128)(2,1)S(1)} %get-tuple-element.25.quad0, ...), custom_call_target="tpu_custom_call" | custom-call | tf_op jit(solution)/shard_map/window/pallas_call | solution.py:263
  25.7 1.1 %collective-permute-start.6 = (bf16[1792,128]{1,0:T(8,128)(2,1)S(1)}, bf16[1792,128]{1,0:T(8,128)(2,1)S(1)}, u32[]{:S(2)}, u32[]{:S(2)}) collective-permute-start(bf16[1792,128]{1,0:T(8,128)(2,1)S(1)} %get-tuple-element.36), channel_id=1, source_target_pairs={{0,16},{1,17},{2,18},{3,19},{4,20},{5,21},{6,22},{7,23},{8,24},{9,... | collective-permute-start | bytes 1376264 | tf_op jit(solution)/shard_map/ppermute | solution.py:338
  26.9 1.4 %collective-permute-done.6 = bf16[1792,128]{1,0:T(8,128)(2,1)S(1)} collective-permute-done((bf16[1792,128]{1,0:T(8,128)(2,1)S(1)}, bf16[1792,128]{1,0:T(8,128)(2,1)S(1)}, u32[]{:S(2)}, u32[]{:S(2)}) %collective-permute-start.6) | collective-permute-done | bytes 458784 | tf_op jit(solution)/shard_map/ppermute | solution.py:338
  28.3 0.9 %add.14 = bf16[1792,128]{1,0:T(8,128)(2,1)} add(bf16[1792,128]{1,0:T(8,128)(2,1)S(1)} %get-tuple-element.35, bf16[1792,128]{1,0:T(8,128)(2,1)S(1)} %collective-permute-done.6) | non-fusion elementwise | flops 229376 | bytes 1376256 | tf_op jit(solution)/shard_map/add | solution.py:356
  29.2 7.3 %all-to-all-start = ((bf16[32,56,128]{2,1,0:T(8,128)(2,1)}), bf16[32,56,128]{2,1,0:T(8,128)(2,1)S(1)}, u32[]{:S(2)}, u32[]{:S(2)}) async-start(bf16[32,56,128]{2,1,0:T(8,128)(2,1)} %bitcast.5), calls=%async_computation | async-start | bytes 917504 | tf_op jit(solution)/shard_map/all_to_all | solution.py:358
  36.5 3.6 %collective-permute-start.3 = (bf16[16,1536]{1,0:T(8,128)(2,1)S(1)}, bf16[16,1536]{1,0:T(8,128)(2,1)S(1)}, u32[]{:S(2)}, u32[]{:S(2)}) collective-permute-start(bf16[16,1536]{1,0:T(8,128)(2,1)S(1)} %get-tuple-element.32), channel_id=1, source_target_pairs={{0,16},{16,32},{32,48},{48,64},{64,80},{80,96},{96,112},{112,128},... | collective-permute-start | bytes 147464 | tf_op jit(solution)/shard_map/ppermute | solution.py:331
  40.1 1.2 %collective-permute-start.4 = (bf16[16,1536]{1,0:T(8,128)(2,1)S(1)}, bf16[16,1536]{1,0:T(8,128)(2,1)S(1)}, u32[]{:S(2)}, u32[]{:S(2)}) collective-permute-start(bf16[16,1536]{1,0:T(8,128)(2,1)S(1)} %get-tuple-element.33), channel_id=1, source_target_pairs={{0,1},{1,2},{2,3},{3,4},{4,5},{5,6},{6,7},{7,8},{8,9},{9,10},{10,1... | collective-permute-start | bytes 147464 | tf_op jit(solution)/shard_map/ppermute | solution.py:332
  41.3 0.0 collective-permute-start.5
  41.3 4.9 %all-to-all-done = bf16[32,56,128]{2,1,0:T(8,128)(2,1)S(1)} async-done(((bf16[32,56,128]{2,1,0:T(8,128)(2,1)}), bf16[32,56,128]{2,1,0:T(8,128)(2,1)S(1)}, u32[]{:S(2)}, u32[]{:S(2)}) %all-to-all-start) | async-done | bytes 458784 | tf_op jit(solution)/shard_map/all_to_all | solution.py:358
  46.2 0.1 reduce_sum.12
  46.3 1.0 %collective-permute-start.7 = (bf16[56,128]{1,0:T(8,128)(2,1)S(1)}, bf16[56,128]{1,0:T(8,128)(2,1)S(1)}, u32[]{:S(2)}, u32[]{:S(2)}) collective-permute-start(bf16[56,128]{1,0:T(8,128)(2,1)S(1)} %reduce_sum.12), channel_id=1, source_target_pairs={{0,2},{1,3},{2,0},{3,1},{4,6},{5,7},{6,4},{7,5},{8,10},{9,11},{10,... | collective-permute-start | bytes 43016 | tf_op jit(solution)/shard_map/ppermute | solution.py:338
  47.3 2.5 %collective-permute-done.7 = bf16[56,128]{1,0:T(8,128)(2,1)S(1)} collective-permute-done((bf16[56,128]{1,0:T(8,128)(2,1)S(1)}, bf16[56,128]{1,0:T(8,128)(2,1)S(1)}, u32[]{:S(2)}, u32[]{:S(2)}) %collective-permute-start.7) | collective-permute-done | bytes 14368 | tf_op jit(solution)/shard_map/ppermute | solution.py:338
  49.9 3.7 %collective-permute-start.8 = (bf16[56,128]{1,0:T(8,128)(2,1)S(1)}, bf16[56,128]{1,0:T(8,128)(2,1)S(1)}, u32[]{:S(2)}, u32[]{:S(2)}) collective-permute-start(bf16[56,128]{1,0:T(8,128)(2,1)S(1)} %add.15), channel_id=1, source_target_pairs={{0,6},{1,7},{2,4},{3,5},{4,2},{5,3},{6,0},{7,1},{8,14},{9,15},{10,... | collective-permute-start | bytes 43016 | tf_op jit(solution)/shard_map/ppermute | solution.py:338
  53.6 0.0 collective-permute-done.3.refs_1_
  53.6 0.0 collective-permute-done.4.refs_2_
  53.6 0.0 collective-permute-done.5.refs_3_
  53.6 0.7 join.1
  54.3 0.4 collective-permute-done.8
  54.7 0.1 broadcast_in_dim.10
  54.7 12.8 %all_to_all.10 = bf16[32,56,128]{2,1,0:T(8,128)(2,1)S(1)} all-to-all(bf16[32,56,128]{2,1,0:T(8,128)(2,1)S(1)} %broadcast_in_dim.10), channel_id=1, replica_groups={{0,64,128,192,8,72,136,200,32,96,160,224,40,104,168,232,1,65,129,193,9,..., dimensions={0} | all-to-all | bytes 917504 | tf_op jit(solution)/shard_map/all_to_all | solution.py:368
  67.5 6.0 %collective-permute-start.9 = (bf16[1792,128]{1,0:T(8,128)(2,1)S(1)}, bf16[1792,128]{1,0:T(8,128)(2,1)S(1)}, u32[]{:S(2)}, u32[]{:S(2)}) collective-permute-start(bf16[1792,128]{1,0:T(8,128)(2,1)S(1)} %bitcast.9), channel_id=1, source_target_pairs={{0,16},{1,17},{2,18},{3,19},{4,20},{5,21},{6,22},{7,23},{8,24},{9,... | collective-permute-start | bytes 1376264 | tf_op jit(solution)/shard_map/ppermute | solution.py:338
  73.6 1.4 %collective-permute-done.9.other = bf16[1792,128]{1,0:T(8,128)(2,1)S(1)} collective-permute-done((bf16[1792,128]{1,0:T(8,128)(2,1)S(1)}, bf16[1792,128]{1,0:T(8,128)(2,1)S(1)}, u32[]{:S(2)}, u32[]{:S(2)}) %collective-permute-start.9) | collective-permute-done | bytes 458784 | tf_op jit(solution)/shard_map/ppermute | solution.py:338
  75.0 1.4 %finish.1 = (f32[192,576]{1,0:T(8,128)}, f32[192,192]{1,0:T(8,128)}, f32[192,768]{1,0:T(8,128)}, f32[192,768]{1,0:T(8,128)}, f32[18,128]{1,0:T(8,128)}) custom-call(s32[1]{0:T(128)} %bitcast.core, bf16[1792,128]{1,0:T(8,128)(2,1)S(1)} %bitcast.10, bf16[1792,128]{1,0:T(8,128)(2,1)S(1)} %collective-permute-done.9.other), custom_call_target="tpu_custom_call" | custom-call | tf_op jit(solution)/shard_map/finish/pallas_call | solution.py:411
  (11 shorter events, 0.0 us)
Async XLA Ops:
  0.6 14.4 %copy-start.1 = (bf16[768,192]{0,1:T(8,128)(2,1)S(1)}, bf16[768,192]{0,1:T(8,128)(2,1)}, u32[]{:S(2)}) copy-start(bf16[768,192]{0,1:T(8,128)(2,1)} %param.21) | copy-start | bytes 884740
  0.6 14.4 %copy-start = (bf16[192,768]{1,0:T(8,128)(2,1)S(1)}, bf16[192,768]{1,0:T(8,128)(2,1)}, u32[]{:S(2)}) copy-start(bf16[192,768]{1,0:T(8,128)(2,1)} %param.19) | copy-start | bytes 884740
  0.7 14.4 %copy-start.3 = (bf16[192,192]{1,0:T(8,128)(2,1)S(1)}, bf16[192,192]{1,0:T(8,128)(2,1)}, u32[]{:S(2)}) copy-start(bf16[192,192]{1,0:T(8,128)(2,1)} %param.17) | copy-start | bytes 221188
  0.7 14.4 %copy-start.2 = (bf16[192,576]{1,0:T(8,128)(2,1)S(1)}, bf16[192,576]{1,0:T(8,128)(2,1)}, u32[]{:S(2)}) copy-start(bf16[192,576]{1,0:T(8,128)(2,1)} %param.15) | copy-start | bytes 663556
  1.8 13.6 %copy-start.4 = (f32[576]{0:T(1024)S(1)}, f32[576]{0:T(1024)}, u32[]{:S(2)}) copy-start(f32[576]{0:T(1024)} %param.16) | copy-start | bytes 6916
  1.8 13.6 %copy-start.5 = (f32[768]{0:T(1024)S(1)}, f32[768]{0:T(1024)}, u32[]{:S(2)}) copy-start(f32[768]{0:T(1024)} %param.20) | copy-start | bytes 9220
  1.8 13.6 %copy-start.6 = (f32[192]{0:T(256)S(1)}, f32[192]{0:T(256)}, u32[]{:S(2)}) copy-start(f32[192]{0:T(256)} %param.18) | copy-start | bytes 2308
  1.8 13.6 %copy-start.7 = (f32[192]{0:T(256)S(1)}, f32[192]{0:T(256)}, u32[]{:S(2)}) copy-start(f32[192]{0:T(256)} %param.22) | copy-start | bytes 2308
  1.9 13.6 %copy-start.8 = (f32[192]{0:T(256)S(1)}, f32[192]{0:T(256)}, u32[]{:S(2)}) copy-start(f32[192]{0:T(256)} %param.23) | copy-start | bytes 2308
  1.9 13.6 %copy-start.9 = (f32[192]{0:T(256)S(1)}, f32[192]{0:T(256)}, u32[]{:S(2)}) copy-start(f32[192]{0:T(256)} %param.24) | copy-start | bytes 2308
  1.9 13.6 %copy-start.10 = (f32[192]{0:T(256)S(1)}, f32[192]{0:T(256)}, u32[]{:S(2)}) copy-start(f32[192]{0:T(256)} %param.25) | copy-start | bytes 2308
  2.0 14.2 %collective-permute-start = (bf16[32,1536]{1,0:T(8,128)(2,1)S(1)}, bf16[32,1536]{1,0:T(8,128)(2,1)S(1)}, u32[]{:S(2)}, u32[]{:S(2)}) collective-permute-start(bf16[32,1536]{1,0:T(8,128)(2,1)S(1)} %get-tuple-element.26), channel_id=1, source_target_pairs={{0,240},{16,0},{32,16},{48,32},{64,48},{80,64},{96,80},{112,96},{1... | collective-permute-start | bytes 294920 | tf_op jit(solution)/shard_map/ppermute | solution.py:331
  5.3 10.9 %collective-permute-start.1 = (bf16[32,1536]{1,0:T(8,128)(2,1)S(1)}, bf16[32,1536]{1,0:T(8,128)(2,1)S(1)}, u32[]{:S(2)}, u32[]{:S(2)}) collective-permute-start(bf16[32,1536]{1,0:T(8,128)(2,1)S(1)} %get-tuple-element.27), channel_id=1, source_target_pairs={{0,15},{1,0},{2,1},{3,2},{4,3},{5,4},{6,5},{7,6},{8,7},{9,8},{10,9... | collective-permute-start | bytes 294920 | tf_op jit(solution)/shard_map/ppermute | solution.py:332
  10.1 7.4 %collective-permute-start.2 = (bf16[32,1536]{1,0:T(8,128)(2,1)S(1)}, bf16[32,1536]{1,0:T(8,128)(2,1)S(1)}, u32[]{:S(2)}, u32[]{:S(2)}) collective-permute-start(bf16[32,1536]{1,0:T(8,128)(2,1)S(1)} %get-tuple-element.28), channel_id=1, source_target_pairs={{0,255},{1,240},{2,241},{3,242},{4,243},{5,244},{6,245},{7,246},{8... | collective-permute-start | bytes 294920 | tf_op jit(solution)/shard_map/ppermute | solution.py:333
  25.7 2.6 %collective-permute-start.6 = (bf16[1792,128]{1,0:T(8,128)(2,1)S(1)}, bf16[1792,128]{1,0:T(8,128)(2,1)S(1)}, u32[]{:S(2)}, u32[]{:S(2)}) collective-permute-start(bf16[1792,128]{1,0:T(8,128)(2,1)S(1)} %get-tuple-element.36), channel_id=1, source_target_pairs={{0,16},{1,17},{2,18},{3,19},{4,20},{5,21},{6,22},{7,23},{8,24},{9,... | collective-permute-start | bytes 1376264 | tf_op jit(solution)/shard_map/ppermute | solution.py:338
  29.2 17.0 %all-to-all-start = ((bf16[32,56,128]{2,1,0:T(8,128)(2,1)}), bf16[32,56,128]{2,1,0:T(8,128)(2,1)S(1)}, u32[]{:S(2)}, u32[]{:S(2)}) async-start(bf16[32,56,128]{2,1,0:T(8,128)(2,1)} %bitcast.5), calls=%async_computation | async-start | bytes 917504 | tf_op jit(solution)/shard_map/all_to_all | solution.py:358
  36.5 17.1 %collective-permute-start.3 = (bf16[16,1536]{1,0:T(8,128)(2,1)S(1)}, bf16[16,1536]{1,0:T(8,128)(2,1)S(1)}, u32[]{:S(2)}, u32[]{:S(2)}) collective-permute-start(bf16[16,1536]{1,0:T(8,128)(2,1)S(1)} %get-tuple-element.32), channel_id=1, source_target_pairs={{0,16},{16,32},{32,48},{48,64},{64,80},{80,96},{96,112},{112,128},... | collective-permute-start | bytes 147464 | tf_op jit(solution)/shard_map/ppermute | solution.py:331
  40.1 13.5 %collective-permute-start.4 = (bf16[16,1536]{1,0:T(8,128)(2,1)S(1)}, bf16[16,1536]{1,0:T(8,128)(2,1)S(1)}, u32[]{:S(2)}, u32[]{:S(2)}) collective-permute-start(bf16[16,1536]{1,0:T(8,128)(2,1)S(1)} %get-tuple-element.33), channel_id=1, source_target_pairs={{0,1},{1,2},{2,3},{3,4},{4,5},{5,6},{6,7},{7,8},{8,9},{9,10},{10,1... | collective-permute-start | bytes 147464 | tf_op jit(solution)/shard_map/ppermute | solution.py:332
  41.3 12.3 %collective-permute-start.5 = (bf16[16,1536]{1,0:T(8,128)(2,1)S(1)}, bf16[16,1536]{1,0:T(8,128)(2,1)S(1)}, u32[]{:S(2)}, u32[]{:S(2)}) collective-permute-start(bf16[16,1536]{1,0:T(8,128)(2,1)S(1)} %get-tuple-element.34), channel_id=1, source_target_pairs={{0,17},{1,18},{2,19},{3,20},{4,21},{5,22},{6,23},{7,24},{8,25},{9,... | collective-permute-start | bytes 147464 | tf_op jit(solution)/shard_map/ppermute | solution.py:333
  46.3 3.6 %collective-permute-start.7 = (bf16[56,128]{1,0:T(8,128)(2,1)S(1)}, bf16[56,128]{1,0:T(8,128)(2,1)S(1)}, u32[]{:S(2)}, u32[]{:S(2)}) collective-permute-start(bf16[56,128]{1,0:T(8,128)(2,1)S(1)} %reduce_sum.12), channel_id=1, source_target_pairs={{0,2},{1,3},{2,0},{3,1},{4,6},{5,7},{6,4},{7,5},{8,10},{9,11},{10,... | collective-permute-start | bytes 43016 | tf_op jit(solution)/shard_map/ppermute | solution.py:338
  49.9 4.8 %collective-permute-start.8 = (bf16[56,128]{1,0:T(8,128)(2,1)S(1)}, bf16[56,128]{1,0:T(8,128)(2,1)S(1)}, u32[]{:S(2)}, u32[]{:S(2)}) collective-permute-start(bf16[56,128]{1,0:T(8,128)(2,1)S(1)} %add.15), channel_id=1, source_target_pairs={{0,6},{1,7},{2,4},{3,5},{4,2},{5,3},{6,0},{7,1},{8,14},{9,15},{10,... | collective-permute-start | bytes 43016 | tf_op jit(solution)/shard_map/ppermute | solution.py:338
  67.5 7.5 %collective-permute-start.9 = (bf16[1792,128]{1,0:T(8,128)(2,1)S(1)}, bf16[1792,128]{1,0:T(8,128)(2,1)S(1)}, u32[]{:S(2)}, u32[]{:S(2)}) collective-permute-start(bf16[1792,128]{1,0:T(8,128)(2,1)S(1)} %bitcast.9), channel_id=1, source_target_pairs={{0,16},{1,17},{2,18},{3,19},{4,20},{5,21},{6,22},{7,23},{8,24},{9,... | collective-permute-start | bytes 1376264 | tf_op jit(solution)/shard_map/ppermute | solution.py:338
